TPU v7x, 768 devices: a whole 4x8x12 slice. The times are simulated.
768 devices in a mesh: gx: 24 (over z, core), gy: 8 (over y), gz: 4 (over x).
Axes of the slice: x: 4, y: 8, z: 12, core: 2. Of those that a mesh axis runs over, the one named last changes fastest.
Arguments:
- right_side: float32 [384, 256, 512], P('gx', 'gy', 'gz'), may hold values from -8 to 8
- diagonal: float32 [384, 256, 512], P('gx', 'gy', 'gz'), may hold values from 0.05 to 2
Outputs:
- solution_field: float32 [384, 256, 512], P('gx', 'gy', 'gz')
- residual: float32 [384, 256, 512], P('gx', 'gy', 'gz')
All inputs are finite; a program needn't handle non-finite values.
Results may differ from a plain program's by a relative error of at most 0.00018.
Values sent between devices are 32-bit elements; how exact they have to be, the bound alone decides.
No kernel may reach another device: no remote copies, remote signals or barrier semaphores. Data moves between devices by JAX's collectives and lax.ppermute only.
A program may use at most 64 MiB of HBM per device.

v0:
```python
import jax
import jax.numpy as jnp
from jax import lax
from jax.sharding import PartitionSpec as P

ITERS = 2
FSWEEPS = 3
CSWEEPS = 4
COARSEN = 4


damping = 2.0 / 3.0


def padded_2(x, sides, width):
    for axis, dim in sides:
        count, length = (lax.axis_size(axis), x.shape[dim])
        up = [(i, (i + 1) % count) for i in range(count - 1)]
        down = [(j, i) for i, j in up]
        last = lax.slice_in_dim(x, length - width, length, axis=dim)
        leading = lax.slice_in_dim(x, 0, width, axis=dim)
        before = lax.ppermute(last, axis, up)
        after = lax.ppermute(leading, axis, down)
        x = jnp.concatenate([before, x, after], axis=dim)
    return x


def neighbour_sum(padded):
    beside = padded[2:, 1:-1, 1:-1] + padded[:-2, 1:-1, 1:-1]
    beside = beside + padded[1:-1, 2:, 1:-1] + padded[1:-1, :-2, 1:-1]
    beside = beside + padded[1:-1, 1:-1, 2:] + padded[1:-1, 1:-1, :-2]
    return beside


def apply_fine(field, diag_plus):
    padded = padded_2(field, (("gx", 0), ("gy", 1), ("gz", 2)), 1)
    return diag_plus * field - neighbour_sum(padded)


def apply_coarse(field, diag_plus):
    padded = padded_2(field, (("gx", 0), ("gy", 1), ("gz", 2)), 1)
    return diag_plus * field - neighbour_sum(padded)


def block_mean(field):
    first, second, third = field.shape
    shaped = field.reshape(
        first // COARSEN, COARSEN, second // COARSEN, COARSEN, third // COARSEN, COARSEN
    )
    return jnp.mean(shaped, axis=(1, 3, 5))


def expand_blocks(field):
    first, second, third = field.shape
    wide = jnp.broadcast_to(
        field[:, None, :, None, :, None], (first, COARSEN, second, COARSEN, third, COARSEN)
    )
    return wide.reshape(first * COARSEN, second * COARSEN, third * COARSEN)


def coarse_jacobi(coarse_rhs, coarse_diag, operator):
    coarse = damping * coarse_rhs / coarse_diag
    for sweep_index in range(CSWEEPS - 1):
        coarse = coarse + damping * (coarse_rhs - operator(coarse, coarse_diag)) / coarse_diag
    return coarse


def smooth_per_sweep(vector, fine_diag):
    smooth = damping * vector / fine_diag
    for sweep_index in range(FSWEEPS - 1):
        smooth = smooth + damping * (vector - apply_fine(smooth, fine_diag)) / fine_diag
    return smooth


def precondition(vector, fine_diag, coarse_diag):
    smooth = smooth_per_sweep(vector, fine_diag)
    coarse_rhs = COARSEN * COARSEN * block_mean(vector)
    coarse = coarse_jacobi(coarse_rhs, coarse_diag, apply_coarse)
    return smooth + expand_blocks(coarse)


def precond_sum(residual, precond):
    return lax.psum(jnp.sum(residual * precond), ("gx", "gy", "gz"))


def on_device(right_side, diagonal):
    fine_diag = 6.0 + diagonal
    coarse_diag = 6.0 + COARSEN * COARSEN * block_mean(diagonal)
    solution = jnp.zeros_like(right_side)
    residual = right_side
    precond = precondition(residual, fine_diag, coarse_diag)
    direction = precond
    rho_value = precond_sum(residual, precond)
    for iter_index in range(ITERS):
        image = apply_fine(direction, fine_diag)
        step_length = rho_value / lax.psum(jnp.sum(direction * image), ("gx", "gy", "gz"))
        solution = solution + step_length * direction
        residual = residual - step_length * image
        if iter_index + 1 < ITERS:
            precond = precondition(residual, fine_diag, coarse_diag)
            rho_next = precond_sum(residual, precond)
            direction = precond + rho_next / rho_value * direction
            rho_value = rho_next
    return (solution, residual)


def solution(mesh):
    in_specs = (P("gx", "gy", "gz"), P("gx", "gy", "gz"))
    out_specs = (P("gx", "gy", "gz"), P("gx", "gy", "gz"))
    return jax.shard_map(
        on_device, mesh=mesh, in_specs=in_specs, out_specs=out_specs, check_vma=False
    )
```

profile of v0, /device:TPU:1, one launch (start us, length us, event | category | flops | bytes accessed | tf_op | source)
XLA Modules:
  0.0 684.2 jit_solution(5284912847392876068)
XLA Ops:
  0.6 10.9 %reshape.21 = f32[4,4,8,4,32,4]{5,4,3,2,1,0:T(8,128)} reshape(f32[16,32,128]{2,1,0:T(8,128)} %param.2) | data formatting | bytes 524288 | tf_op jit(solution)/shard_map/reshape | solution.py:47
  11.6 10.0 %reshape.22 = f32[4,4,8,4,32,4]{5,4,3,2,1,0:T(8,128)} reshape(f32[16,32,128]{2,1,0:T(8,128)S(1)} %copy-done) | data formatting | bytes 524288 | tf_op jit(solution)/shard_map/reshape | solution.py:47
  21.6 4.1 reduce_sum.63
  25.7 4.1 reduce_sum.64
  29.8 12.4 %collective-permute-start.12 = (f32[1,8,32]{2,1,0:T(8,128)S(1)}, f32[1,8,32]{2,1,0:T(8,128)S(1)}, u32[]{:S(2)}, u32[]{:S(2)}) collective-permute-start(f32[1,8,32]{2,1,0:T(8,128)S(1)} %get-tuple-element.84), channel_id=1, source_target_pairs={{32,0},{64,32},{96,64},{128,96},{160,128},{192,160},{224,192},{256... | collective-permute-start | bytes 3080 | tf_op jit(solution)/shard_map/ppermute | solution.py:23
  46.6 4.0 collective-permute-start.15
  57.6 4.4 collective-permute-start.18
  62.0 3.6 collective-permute-start.19
  67.7 4.5 collective-permute-start.21
  77.6 5.3 collective-permute-start.1
  85.1 4.5 collective-permute-start.3
  91.6 4.5 collective-permute-start.25
  96.3 4.3 collective-permute-start.5
  103.2 4.3 collective-permute-start.27
  107.5 4.0 collective-permute-done.4
  113.8 3.9 collective-permute-start.7
  119.9 4.3 collective-permute-start.9
  127.7 4.0 collective-permute-start.11
  133.2 4.5 broadcast_in_dim.4
  137.7 8.2 %reshape.23 = f32[16,32,128]{2,1,0:T(8,128)S(1)} reshape(f32[4,4,8,4,32,4]{5,4,3,2,1,0:T(8,128)} %broadcast_in_dim.4) | data formatting | bytes 524288 | tf_op jit(solution)/shard_map/reshape | solution.py:58
  148.2 5.3 collective-permute-start.31
  155.7 4.9 collective-permute-start.33
  161.6 4.3 collective-permute-start.35
  167.2 5.2 collective-permute-done.35
  172.3 4.1 collective-permute-done.34
  177.4 122.0 %all-reduce = (f32[]{:T(128)}, f32[]{:T(128)}) all-reduce(f32[]{:T(128)} %get-tuple-element.3, f32[]{:T(128)} %get-tuple-element.2), channel_id=1, replica_groups=mesh['gx'=24,'gy'=8,'gz'=4] {'gx','gy','gz'}, use_global_device_ids=true, to_apply=%region_3.0 | all-reduce | flops 2 | bytes 16 | tf_op jit(solution)/shard_map/psum | solution.py:83
  300.8 10.1 %reshape.24 = f32[4,4,8,4,32,4]{5,4,3,2,1,0:T(8,128)} reshape(f32[16,32,128]{2,1,0:T(8,128)S(1)} %get-tuple-element.11) | data formatting | bytes 524288 | tf_op jit(solution)/shard_map/reshape | solution.py:47
  310.9 4.1 reduce_sum.67
  322.6 4.0 collective-permute-start.51
  327.4 3.6 collective-permute-start.53
  336.0 4.0 collective-permute-start.54
  340.0 4.7 collective-permute-start.55
  346.7 4.5 collective-permute-start.57
  357.0 5.3 collective-permute-start.37
  364.5 4.5 collective-permute-start.39
  371.0 4.5 collective-permute-start.61
  375.7 4.3 collective-permute-start.41
  382.6 5.2 collective-permute-start.63
  393.2 4.7 collective-permute-start.43
  400.1 5.5 collective-permute-start.45
  410.2 4.0 collective-permute-start.47
  415.7 4.5 broadcast_in_dim.5
  420.2 8.2 %reshape.25 = f32[16,32,128]{2,1,0:T(8,128)S(1)} reshape(f32[4,4,8,4,32,4]{5,4,3,2,1,0:T(8,128)} %broadcast_in_dim.5) | data formatting | bytes 524288 | tf_op jit(solution)/shard_map/reshape | solution.py:58
  429.3 115.4 %psum.30 = f32[]{:T(128)} all-reduce(f32[]{:T(128)} %get-tuple-element.8), channel_id=1, replica_groups=mesh['gx'=24,'gy'=8,'gz'=4] {'gx','gy','gz'}, use_global_device_ids=true, to_apply=%region_8.0 | all-reduce | flops 1 | bytes 8 | tf_op jit(solution)/shard_map/psum | solution.py:83
  553.9 4.0 collective-permute-start.69
  562.7 6.1 collective-permute-done.71
  568.8 3.8 collective-permute-done.70
  573.5 108.4 %psum.31 = f32[]{:T(128)} all-reduce(f32[]{:T(128)} %get-tuple-element.6), channel_id=1, replica_groups=mesh['gx'=24,'gy'=8,'gz'=4] {'gx','gy','gz'}, use_global_device_ids=true, to_apply=%region_10.0 | all-reduce | flops 1 | bytes 8 | tf_op jit(solution)/shard_map/psum | solution.py:96
  (179 shorter events, 99.4 us)
Async XLA Ops:
  29.8 14.4 %collective-permute-start.12 = (f32[1,8,32]{2,1,0:T(8,128)S(1)}, f32[1,8,32]{2,1,0:T(8,128)S(1)}, u32[]{:S(2)}, u32[]{:S(2)}) collective-permute-start(f32[1,8,32]{2,1,0:T(8,128)S(1)} %get-tuple-element.84), channel_id=1, source_target_pairs={{32,0},{64,32},{96,64},{128,96},{160,128},{192,160},{224,192},{256... | collective-permute-start | bytes 3080 | tf_op jit(solution)/shard_map/ppermute | solution.py:23
  57.6 8.1 %collective-permute-start.18 = (f32[1,8,32]{2,1,0:T(8,128)S(1)}, f32[1,8,32]{2,1,0:T(8,128)S(1)}, u32[]{:S(2)}, u32[]{:S(2)}) collective-permute-start(f32[1,8,32]{2,1,0:T(8,128)S(1)} %get-tuple-element.82), channel_id=1, source_target_pairs={{32,0},{64,32},{96,64},{128,96},{160,128},{192,160},{224,192},{256... | collective-permute-start | bytes 3080 | tf_op jit(solution)/shard_map/ppermute | solution.py:23
  73.0 9.9 %collective-permute-start.23 = (f32[6,10,1]{2,1,0:T(8,128)S(1)}, f32[6,10,1]{2,1,0:T(8,128)S(1)}, u32[]{:S(2)}, u32[]{:S(2)}) collective-permute-start(f32[6,10,1]{2,1,0:T(8,128)S(1)} %get-tuple-element.58), channel_id=1, source_target_pairs={{0,1},{1,2},{2,3},{4,5},{5,6},{6,7},{8,9},{9,10},{10,11},{12,13},{... | collective-permute-start | bytes 728 | tf_op jit(solution)/shard_map/ppermute | solution.py:22
  74.4 8.6 %collective-permute-start.22 = (f32[6,10,1]{2,1,0:T(8,128)S(1)}, f32[6,10,1]{2,1,0:T(8,128)S(1)}, u32[]{:S(2)}, u32[]{:S(2)}) collective-permute-start(f32[6,10,1]{2,1,0:T(8,128)S(1)} %get-tuple-element.57), channel_id=1, source_target_pairs={{1,0},{2,1},{3,2},{5,4},{6,5},{7,6},{9,8},{10,9},{11,10},{13,12},{... | collective-permute-start | bytes 728 | tf_op jit(solution)/shard_map/ppermute | solution.py:23
  75.7 7.4 %collective-permute-start = (f32[1,32,128]{2,1,0:T(8,128)S(1)}, f32[1,32,128]{2,1,0:T(8,128)S(1)}, u32[]{:S(2)}, u32[]{:S(2)}) collective-permute-start(f32[1,32,128]{2,1,0:T(8,128)S(1)} %get-tuple-element.48), channel_id=1, source_target_pairs={{32,0},{64,32},{96,64},{128,96},{160,128},{192,160},{224,192},{256... | collective-permute-start | bytes 49160 | tf_op jit(solution)/shard_map/ppermute | solution.py:23
  77.6 6.2 collective-permute-start.1
  83.8 12.3 %collective-permute-start.2 = (f32[18,1,128]{2,1,0:T(1,128)S(1)}, f32[18,1,128]{2,1,0:T(1,128)S(1)}, u32[]{:S(2)}, u32[]{:S(2)}) collective-permute-start(f32[18,1,128]{2,1,0:T(1,128)S(1)} %get-tuple-element.36), channel_id=1, source_target_pairs={{4,0},{8,4},{12,8},{16,12},{20,16},{24,20},{28,24},{5,1},{9,5},{13... | collective-permute-start | bytes 27656 | tf_op jit(solution)/shard_map/ppermute | solution.py:23
  85.1 11.0 %collective-permute-start.3 = (f32[18,1,128]{2,1,0:T(1,128)S(1)}, f32[18,1,128]{2,1,0:T(1,128)S(1)}, u32[]{:S(2)}, u32[]{:S(2)}) collective-permute-start(f32[18,1,128]{2,1,0:T(1,128)S(1)} %get-tuple-element.35), channel_id=1, source_target_pairs={{0,4},{4,8},{8,12},{12,16},{16,20},{20,24},{24,28},{1,5},{5,9},{9,... | collective-permute-start | bytes 27656 | tf_op jit(solution)/shard_map/ppermute | solution.py:22
  89.6 12.3 %collective-permute-start.24 = (f32[1,8,32]{2,1,0:T(8,128)S(1)}, f32[1,8,32]{2,1,0:T(8,128)S(1)}, u32[]{:S(2)}, u32[]{:S(2)}) collective-permute-start(f32[1,8,32]{2,1,0:T(8,128)S(1)} %get-tuple-element.80), channel_id=1, source_target_pairs={{32,0},{64,32},{96,64},{128,96},{160,128},{192,160},{224,192},{256... | collective-permute-start | bytes 3080 | tf_op jit(solution)/shard_map/ppermute | solution.py:23
  91.6 10.3 %collective-permute-start.25 = (f32[1,8,32]{2,1,0:T(8,128)S(1)}, f32[1,8,32]{2,1,0:T(8,128)S(1)}, u32[]{:S(2)}, u32[]{:S(2)}) collective-permute-start(f32[1,8,32]{2,1,0:T(8,128)S(1)} %get-tuple-element.79), channel_id=1, source_target_pairs={{0,32},{32,64},{64,96},{96,128},{128,160},{160,192},{192,224},{224... | collective-permute-start | bytes 3080 | tf_op jit(solution)/shard_map/ppermute | solution.py:22
  96.3 11.2 %collective-permute-start.5 = (f32[18,34,1]{2,1,0:T(8,128)S(1)}, f32[18,34,1]{2,1,0:T(8,128)S(1)}, u32[]{:S(2)}, u32[]{:S(2)}) collective-permute-start(f32[18,34,1]{2,1,0:T(8,128)S(1)} %get-tuple-element.24), channel_id=1, source_target_pairs={{0,1},{1,2},{2,3},{4,5},{5,6},{6,7},{8,9},{9,10},{10,11},{12,13},{... | collective-permute-start | bytes 7352 | tf_op jit(solution)/shard_map/ppermute | solution.py:22
  100.6 10.9 %collective-permute-start.4 = (f32[18,34,1]{2,1,0:T(8,128)S(1)}, f32[18,34,1]{2,1,0:T(8,128)S(1)}, u32[]{:S(2)}, u32[]{:S(2)}) collective-permute-start(f32[18,34,1]{2,1,0:T(8,128)S(1)} %get-tuple-element.23), channel_id=1, source_target_pairs={{1,0},{2,1},{3,2},{5,4},{6,5},{7,6},{9,8},{10,9},{11,10},{13,12},{... | collective-permute-start | bytes 7352 | tf_op jit(solution)/shard_map/ppermute | solution.py:23
  101.9 15.8 %collective-permute-start.26 = (f32[6,1,32]{2,1,0:T(1,128)S(1)}, f32[6,1,32]{2,1,0:T(1,128)S(1)}, u32[]{:S(2)}, u32[]{:S(2)}) collective-permute-start(f32[6,1,32]{2,1,0:T(1,128)S(1)} %get-tuple-element.68), channel_id=1, source_target_pairs={{4,0},{8,4},{12,8},{16,12},{20,16},{24,20},{28,24},{5,1},{9,5},{13... | collective-permute-start | bytes 2312 | tf_op jit(solution)/shard_map/ppermute | solution.py:23
  103.2 14.5 %collective-permute-start.27 = (f32[6,1,32]{2,1,0:T(1,128)S(1)}, f32[6,1,32]{2,1,0:T(1,128)S(1)}, u32[]{:S(2)}, u32[]{:S(2)}) collective-permute-start(f32[6,1,32]{2,1,0:T(1,128)S(1)} %get-tuple-element.67), channel_id=1, source_target_pairs={{0,4},{4,8},{8,12},{12,16},{16,20},{20,24},{24,28},{1,5},{5,9},{9,... | collective-permute-start | bytes 2312 | tf_op jit(solution)/shard_map/ppermute | solution.py:22
  111.9 5.9 collective-permute-start.6
  118.6 8.9 %collective-permute-start.8 = (f32[18,1,128]{2,1,0:T(1,128)S(1)}, f32[18,1,128]{2,1,0:T(1,128)S(1)}, u32[]{:S(2)}, u32[]{:S(2)}) collective-permute-start(f32[18,1,128]{2,1,0:T(1,128)S(1)} %get-tuple-element.34), channel_id=1, source_target_pairs={{4,0},{8,4},{12,8},{16,12},{20,16},{24,20},{28,24},{5,1},{9,5},{13... | collective-permute-start | bytes 27656 | tf_op jit(solution)/shard_map/ppermute | solution.py:23
  119.9 7.6 %collective-permute-start.9 = (f32[18,1,128]{2,1,0:T(1,128)S(1)}, f32[18,1,128]{2,1,0:T(1,128)S(1)}, u32[]{:S(2)}, u32[]{:S(2)}) collective-permute-start(f32[18,1,128]{2,1,0:T(1,128)S(1)} %get-tuple-element.33), channel_id=1, source_target_pairs={{0,4},{4,8},{8,12},{12,16},{16,20},{20,24},{24,28},{1,5},{5,9},{9,... | collective-permute-start | bytes 27656 | tf_op jit(solution)/shard_map/ppermute | solution.py:22
  124.3 8.8 %collective-permute-start.29 = (f32[6,10,1]{2,1,0:T(8,128)S(1)}, f32[6,10,1]{2,1,0:T(8,128)S(1)}, u32[]{:S(2)}, u32[]{:S(2)}) collective-permute-start(f32[6,10,1]{2,1,0:T(8,128)S(1)} %get-tuple-element.56), channel_id=1, source_target_pairs={{0,1},{1,2},{2,3},{4,5},{5,6},{6,7},{8,9},{9,10},{10,11},{12,13},{... | collective-permute-start | bytes 728 | tf_op jit(solution)/shard_map/ppermute | solution.py:22
  126.2 6.9 %collective-permute-start.28 = (f32[6,10,1]{2,1,0:T(8,128)S(1)}, f32[6,10,1]{2,1,0:T(8,128)S(1)}, u32[]{:S(2)}, u32[]{:S(2)}) collective-permute-start(f32[6,10,1]{2,1,0:T(8,128)S(1)} %get-tuple-element.55), channel_id=1, source_target_pairs={{1,0},{2,1},{3,2},{5,4},{6,5},{7,6},{9,8},{10,9},{11,10},{13,12},{... | collective-permute-start | bytes 728 | tf_op jit(solution)/shard_map/ppermute | solution.py:23
  127.7 18.1 %collective-permute-start.11 = (f32[18,34,1]{2,1,0:T(8,128)S(1)}, f32[18,34,1]{2,1,0:T(8,128)S(1)}, u32[]{:S(2)}, u32[]{:S(2)}) collective-permute-start(f32[18,34,1]{2,1,0:T(8,128)S(1)} %get-tuple-element.22), channel_id=1, source_target_pairs={{0,1},{1,2},{2,3},{4,5},{5,6},{6,7},{8,9},{9,10},{10,11},{12,13},{... | collective-permute-start | bytes 7352 | tf_op jit(solution)/shard_map/ppermute | solution.py:22
  131.7 14.1 %collective-permute-start.10 = (f32[18,34,1]{2,1,0:T(8,128)S(1)}, f32[18,34,1]{2,1,0:T(8,128)S(1)}, u32[]{:S(2)}, u32[]{:S(2)}) collective-permute-start(f32[18,34,1]{2,1,0:T(8,128)S(1)} %get-tuple-element.21), channel_id=1, source_target_pairs={{1,0},{2,1},{3,2},{5,4},{6,5},{7,6},{9,8},{10,9},{11,10},{13,12},{... | collective-permute-start | bytes 7352 | tf_op jit(solution)/shard_map/ppermute | solution.py:23
  146.2 7.3 %collective-permute-start.30 = (f32[1,32,128]{2,1,0:T(8,128)S(1)}, f32[1,32,128]{2,1,0:T(8,128)S(1)}, u32[]{:S(2)}, u32[]{:S(2)}) collective-permute-start(f32[1,32,128]{2,1,0:T(8,128)S(1)} %get-tuple-element.44), channel_id=1, source_target_pairs={{32,0},{64,32},{96,64},{128,96},{160,128},{192,160},{224,192},{256... | collective-permute-start | bytes 49160 | tf_op jit(solution)/shard_map/ppermute | solution.py:23
  148.2 6.2 collective-permute-start.31
  154.4 6.2 collective-permute-start.32
  161.6 10.8 %collective-permute-start.35 = (f32[18,34,1]{2,1,0:T(8,128)S(1)}, f32[18,34,1]{2,1,0:T(8,128)S(1)}, u32[]{:S(2)}, u32[]{:S(2)}) collective-permute-start(f32[18,34,1]{2,1,0:T(8,128)S(1)} %get-tuple-element.20), channel_id=1, source_target_pairs={{0,1},{1,2},{2,3},{4,5},{5,6},{6,7},{8,9},{9,10},{10,11},{12,13},{... | collective-permute-start | bytes 7352 | tf_op jit(solution)/shard_map/ppermute | solution.py:22
  165.9 10.6 %collective-permute-start.34 = (f32[18,34,1]{2,1,0:T(8,128)S(1)}, f32[18,34,1]{2,1,0:T(8,128)S(1)}, u32[]{:S(2)}, u32[]{:S(2)}) collective-permute-start(f32[18,34,1]{2,1,0:T(8,128)S(1)} %get-tuple-element.19), channel_id=1, source_target_pairs={{1,0},{2,1},{3,2},{5,4},{6,5},{7,6},{9,8},{10,9},{11,10},{13,12},{... | collective-permute-start | bytes 7352 | tf_op jit(solution)/shard_map/ppermute | solution.py:23
  336.0 8.7 %collective-permute-start.54 = (f32[1,8,32]{2,1,0:T(8,128)S(1)}, f32[1,8,32]{2,1,0:T(8,128)S(1)}, u32[]{:S(2)}, u32[]{:S(2)}) collective-permute-start(f32[1,8,32]{2,1,0:T(8,128)S(1)} %get-tuple-element.76), channel_id=1, source_target_pairs={{32,0},{64,32},{96,64},{128,96},{160,128},{192,160},{224,192},{256... | collective-permute-start | bytes 3080 | tf_op jit(solution)/shard_map/ppermute | solution.py:23
  352.1 10.2 %collective-permute-start.59 = (f32[6,10,1]{2,1,0:T(8,128)S(1)}, f32[6,10,1]{2,1,0:T(8,128)S(1)}, u32[]{:S(2)}, u32[]{:S(2)}) collective-permute-start(f32[6,10,1]{2,1,0:T(8,128)S(1)} %get-tuple-element.52), channel_id=1, source_target_pairs={{0,1},{1,2},{2,3},{4,5},{5,6},{6,7},{8,9},{9,10},{10,11},{12,13},{... | collective-permute-start | bytes 728 | tf_op jit(solution)/shard_map/ppermute | solution.py:22
  353.7 8.6 %collective-permute-start.58 = (f32[6,10,1]{2,1,0:T(8,128)S(1)}, f32[6,10,1]{2,1,0:T(8,128)S(1)}, u32[]{:S(2)}, u32[]{:S(2)}) collective-permute-start(f32[6,10,1]{2,1,0:T(8,128)S(1)} %get-tuple-element.51), channel_id=1, source_target_pairs={{1,0},{2,1},{3,2},{5,4},{6,5},{7,6},{9,8},{10,9},{11,10},{13,12},{... | collective-permute-start | bytes 728 | tf_op jit(solution)/shard_map/ppermute | solution.py:23
  355.0 7.4 %collective-permute-start.36 = (f32[1,32,128]{2,1,0:T(8,128)S(1)}, f32[1,32,128]{2,1,0:T(8,128)S(1)}, u32[]{:S(2)}, u32[]{:S(2)}) collective-permute-start(f32[1,32,128]{2,1,0:T(8,128)S(1)} %get-tuple-element.42), channel_id=1, source_target_pairs={{32,0},{64,32},{96,64},{128,96},{160,128},{192,160},{224,192},{256... | collective-permute-start | bytes 49160 | tf_op jit(solution)/shard_map/ppermute | solution.py:23
  357.0 6.2 collective-permute-start.37
  363.2 12.3 %collective-permute-start.38 = (f32[18,1,128]{2,1,0:T(1,128)S(1)}, f32[18,1,128]{2,1,0:T(1,128)S(1)}, u32[]{:S(2)}, u32[]{:S(2)}) collective-permute-start(f32[18,1,128]{2,1,0:T(1,128)S(1)} %get-tuple-element.30), channel_id=1, source_target_pairs={{4,0},{8,4},{12,8},{16,12},{20,16},{24,20},{28,24},{5,1},{9,5},{13... | collective-permute-start | bytes 27656 | tf_op jit(solution)/shard_map/ppermute | solution.py:23
  364.5 11.0 %collective-permute-start.39 = (f32[18,1,128]{2,1,0:T(1,128)S(1)}, f32[18,1,128]{2,1,0:T(1,128)S(1)}, u32[]{:S(2)}, u32[]{:S(2)}) collective-permute-start(f32[18,1,128]{2,1,0:T(1,128)S(1)} %get-tuple-element.29), channel_id=1, source_target_pairs={{0,4},{4,8},{8,12},{12,16},{16,20},{20,24},{24,28},{1,5},{5,9},{9,... | collective-permute-start | bytes 27656 | tf_op jit(solution)/shard_map/ppermute | solution.py:22
  369.0 12.3 %collective-permute-start.60 = (f32[1,8,32]{2,1,0:T(8,128)S(1)}, f32[1,8,32]{2,1,0:T(8,128)S(1)}, u32[]{:S(2)}, u32[]{:S(2)}) collective-permute-start(f32[1,8,32]{2,1,0:T(8,128)S(1)} %get-tuple-element.74), channel_id=1, source_target_pairs={{32,0},{64,32},{96,64},{128,96},{160,128},{192,160},{224,192},{256... | collective-permute-start | bytes 3080 | tf_op jit(solution)/shard_map/ppermute | solution.py:23
  371.0 10.3 %collective-permute-start.61 = (f32[1,8,32]{2,1,0:T(8,128)S(1)}, f32[1,8,32]{2,1,0:T(8,128)S(1)}, u32[]{:S(2)}, u32[]{:S(2)}) collective-permute-start(f32[1,8,32]{2,1,0:T(8,128)S(1)} %get-tuple-element.73), channel_id=1, source_target_pairs={{0,32},{32,64},{64,96},{96,128},{128,160},{160,192},{192,224},{224... | collective-permute-start | bytes 3080 | tf_op jit(solution)/shard_map/ppermute | solution.py:22
  375.7 12.2 %collective-permute-start.41 = (f32[18,34,1]{2,1,0:T(8,128)S(1)}, f32[18,34,1]{2,1,0:T(8,128)S(1)}, u32[]{:S(2)}, u32[]{:S(2)}) collective-permute-start(f32[18,34,1]{2,1,0:T(8,128)S(1)} %get-tuple-element.18), channel_id=1, source_target_pairs={{0,1},{1,2},{2,3},{4,5},{5,6},{6,7},{8,9},{9,10},{10,11},{12,13},{... | collective-permute-start | bytes 7352 | tf_op jit(solution)/shard_map/ppermute | solution.py:22
  380.0 10.9 %collective-permute-start.40 = (f32[18,34,1]{2,1,0:T(8,128)S(1)}, f32[18,34,1]{2,1,0:T(8,128)S(1)}, u32[]{:S(2)}, u32[]{:S(2)}) collective-permute-start(f32[18,34,1]{2,1,0:T(8,128)S(1)} %get-tuple-element.17), channel_id=1, source_target_pairs={{1,0},{2,1},{3,2},{5,4},{6,5},{7,6},{9,8},{10,9},{11,10},{13,12},{... | collective-permute-start | bytes 7352 | tf_op jit(solution)/shard_map/ppermute | solution.py:23
  381.3 16.6 %collective-permute-start.62 = (f32[6,1,32]{2,1,0:T(1,128)S(1)}, f32[6,1,32]{2,1,0:T(1,128)S(1)}, u32[]{:S(2)}, u32[]{:S(2)}) collective-permute-start(f32[6,1,32]{2,1,0:T(1,128)S(1)} %get-tuple-element.62), channel_id=1, source_target_pairs={{4,0},{8,4},{12,8},{16,12},{20,16},{24,20},{28,24},{5,1},{9,5},{13... | collective-permute-start | bytes 2312 | tf_op jit(solution)/shard_map/ppermute | solution.py:23
  382.6 15.3 %collective-permute-start.63 = (f32[6,1,32]{2,1,0:T(1,128)S(1)}, f32[6,1,32]{2,1,0:T(1,128)S(1)}, u32[]{:S(2)}, u32[]{:S(2)}) collective-permute-start(f32[6,1,32]{2,1,0:T(1,128)S(1)} %get-tuple-element.61), channel_id=1, source_target_pairs={{0,4},{4,8},{8,12},{12,16},{16,20},{20,24},{24,28},{1,5},{5,9},{9,... | collective-permute-start | bytes 2312 | tf_op jit(solution)/shard_map/ppermute | solution.py:22
  391.3 6.7 collective-permute-start.42
  398.8 11.2 %collective-permute-start.44 = (f32[18,1,128]{2,1,0:T(1,128)S(1)}, f32[18,1,128]{2,1,0:T(1,128)S(1)}, u32[]{:S(2)}, u32[]{:S(2)}) collective-permute-start(f32[18,1,128]{2,1,0:T(1,128)S(1)} %get-tuple-element.28), channel_id=1, source_target_pairs={{4,0},{8,4},{12,8},{16,12},{20,16},{24,20},{28,24},{5,1},{9,5},{13... | collective-permute-start | bytes 27656 | tf_op jit(solution)/shard_map/ppermute | solution.py:23
  400.1 9.9 %collective-permute-start.45 = (f32[18,1,128]{2,1,0:T(1,128)S(1)}, f32[18,1,128]{2,1,0:T(1,128)S(1)}, u32[]{:S(2)}, u32[]{:S(2)}) collective-permute-start(f32[18,1,128]{2,1,0:T(1,128)S(1)} %get-tuple-element.27), channel_id=1, source_target_pairs={{0,4},{4,8},{8,12},{12,16},{16,20},{20,24},{24,28},{1,5},{5,9},{9,... | collective-permute-start | bytes 27656 | tf_op jit(solution)/shard_map/ppermute | solution.py:22
  405.7 9.9 %collective-permute-start.65 = (f32[6,10,1]{2,1,0:T(8,128)S(1)}, f32[6,10,1]{2,1,0:T(8,128)S(1)}, u32[]{:S(2)}, u32[]{:S(2)}) collective-permute-start(f32[6,10,1]{2,1,0:T(8,128)S(1)} %get-tuple-element.50), channel_id=1, source_target_pairs={{0,1},{1,2},{2,3},{4,5},{5,6},{6,7},{8,9},{9,10},{10,11},{12,13},{... | collective-permute-start | bytes 728 | tf_op jit(solution)/shard_map/ppermute | solution.py:22
  408.7 6.9 %collective-permute-start.64 = (f32[6,10,1]{2,1,0:T(8,128)S(1)}, f32[6,10,1]{2,1,0:T(8,128)S(1)}, u32[]{:S(2)}, u32[]{:S(2)}) collective-permute-start(f32[6,10,1]{2,1,0:T(8,128)S(1)} %get-tuple-element.49), channel_id=1, source_target_pairs={{1,0},{2,1},{3,2},{5,4},{6,5},{7,6},{9,8},{10,9},{11,10},{13,12},{... | collective-permute-start | bytes 728 | tf_op jit(solution)/shard_map/ppermute | solution.py:23
  410.2 18.1 %collective-permute-start.47 = (f32[18,34,1]{2,1,0:T(8,128)S(1)}, f32[18,34,1]{2,1,0:T(8,128)S(1)}, u32[]{:S(2)}, u32[]{:S(2)}) collective-permute-start(f32[18,34,1]{2,1,0:T(8,128)S(1)} %get-tuple-element.16), channel_id=1, source_target_pairs={{0,1},{1,2},{2,3},{4,5},{5,6},{6,7},{8,9},{9,10},{10,11},{12,13},{... | collective-permute-start | bytes 7352 | tf_op jit(solution)/shard_map/ppermute | solution.py:22
  414.3 14.1 %collective-permute-start.46 = (f32[18,34,1]{2,1,0:T(8,128)S(1)}, f32[18,34,1]{2,1,0:T(8,128)S(1)}, u32[]{:S(2)}, u32[]{:S(2)}) collective-permute-start(f32[18,34,1]{2,1,0:T(8,128)S(1)} %get-tuple-element.15), channel_id=1, source_target_pairs={{1,0},{2,1},{3,2},{5,4},{6,5},{7,6},{9,8},{10,9},{11,10},{13,12},{... | collective-permute-start | bytes 7352 | tf_op jit(solution)/shard_map/ppermute | solution.py:23
  558.9 9.9 %collective-permute-start.71 = (f32[18,34,1]{2,1,0:T(8,128)S(1)}, f32[18,34,1]{2,1,0:T(8,128)S(1)}, u32[]{:S(2)}, u32[]{:S(2)}) collective-permute-start(f32[18,34,1]{2,1,0:T(8,128)S(1)} %get-tuple-element.14), channel_id=1, source_target_pairs={{0,1},{1,2},{2,3},{4,5},{5,6},{6,7},{8,9},{9,10},{10,11},{12,13},{... | collective-permute-start | bytes 7352 | tf_op jit(solution)/shard_map/ppermute | solution.py:22
  561.4 11.2 %collective-permute-start.70 = (f32[18,34,1]{2,1,0:T(8,128)S(1)}, f32[18,34,1]{2,1,0:T(8,128)S(1)}, u32[]{:S(2)}, u32[]{:S(2)}) collective-permute-start(f32[18,34,1]{2,1,0:T(8,128)S(1)} %get-tuple-element.13), channel_id=1, source_target_pairs={{1,0},{2,1},{3,2},{5,4},{6,5},{7,6},{9,8},{10,9},{11,10},{13,12},{... | collective-permute-start | bytes 7352 | tf_op jit(solution)/shard_map/ppermute | solution.py:23
  (26 other events, 172.2 us)
where the time goes:
time: 689 us; the launch traced here: 684 us
  blocking collectives  346 us (50%)
  starting transfers between devices  211 us (31%)
  local copies, waits for them, and re-layouts  57.9 us (8%)
  waiting for transfers between devices  45.6 us (7%)
  other arithmetic  18.5 us (3%)
    psum x2, blocking collectives, precond_sum(): return lax.psum(jnp.sum(residual * precond), ('gx', 'gy', 'gz'))  237 us
    ppermute x36, starting transfers between devices, padded_2(): before = lax.ppermute(last, axis, up)  140 us
    psum x1, blocking collectives, on_device(): lax.psum(jnp.sum(direction * image), ('gx', 'gy', 'gz'))  108 us
    ppermute x36, starting transfers between devices, padded_2(): after = lax.ppermute(leading, axis, down)  70.4 us
    reshape x3, local copies, waits for them, and re-layouts, block_mean(): field.reshape(first // COARSEN, COARSEN, second // COARSEN, COARSEN, thir...  31 us
    ppermute x36, waiting for transfers between devices, padded_2(): before = lax.ppermute(last, axis, up)  23.6 us
    ppermute x36, waiting for transfers between devices, padded_2(): after = lax.ppermute(leading, axis, down)  22 us
    reshape x2, local copies, waits for them, and re-layouts, expand_blocks(): return wide.reshape(first * COARSEN, second * COARSEN, third * COARSEN)  16.3 us
  transfers between devices with their start and end apart: 72, of which 24 were waited for; matrix products, arithmetic and copies ran while one was open for 4% of the time, Pallas kernels for 0%

commit v1 on v0

v1 whole, which is shorter than its diff:
```python
import functools

import jax
import jax.numpy as jnp
from jax import lax
from jax.experimental import pallas as pl
from jax.experimental.pallas import tpu as pltpu
from jax.sharding import PartitionSpec as P

ITERS = 2
FSWEEPS = 3
CSWEEPS = 4
COARSEN = 4
damping = 2.0 / 3.0
keep = 1.0 - damping

NX, NY, NZ = 16, 32, 128
HF = 3
HC = 4
CX, CY = NX // COARSEN, NY // COARSEN
EX = NX + 2 * HF
EY = 40
EC = CX + 2 * HC
ER = CY + 2 * HC
FACE = HF * NY
VMEM = pl.BlockSpec(memory_space=pltpu.VMEM)
F32 = jnp.float32


def lanes(shape):
    return lax.broadcasted_iota(jnp.int32, shape, len(shape) - 1)


def roll(x, shift, axis=-1):
    axis = axis % x.ndim
    return pltpu.roll(x, shift % x.shape[axis], axis)


def group_sum(x):
    lane = lanes(x.shape)
    x = x + jnp.where(lane % 2 == 0, roll(x, -1), roll(x, 1))
    return x + jnp.where(lane % 4 < 2, roll(x, -2), roll(x, 2))


def block_sums(planes, tmp):
    tmp[...] = group_sum(planes[0] + planes[1] + planes[2] + planes[3])
    rows = [tmp[pl.ds(k, CY, stride=COARSEN), :] for k in range(COARSEN)]
    return rows[0] + rows[1] + rows[2] + rows[3]


def start_kernel(b_ref, d_ref, v_ref, up_ref, down_ref, tmp):
    for c in range(CX):
        fine = []
        for i in range(COARSEN * c, COARSEN * (c + 1)):
            v_ref[i] = damping / (6.0 + d_ref[i])
        g = block_sums([b_ref[COARSEN * c + k] for k in range(COARSEN)], tmp) * 0.25
        cd = 6.0 + block_sums([d_ref[COARSEN * c + k] for k in range(COARSEN)], tmp) * 0.25
        vc = damping / cd
        for ref in (up_ref, down_ref):
            ref[2 * FACE + CY * c : 2 * FACE + CY * (c + 1)] = g
            ref[2 * FACE + CY * (CX + c) : 2 * FACE + CY * (CX + c + 1)] = vc
    for k in range(HF):
        for f, ref in enumerate((b_ref, v_ref)):
            down_ref[FACE * f + NY * k : FACE * f + NY * (k + 1)] = ref[k]
            up_ref[FACE * f + NY * k : FACE * f + NY * (k + 1)] = ref[NX - HF + k]


def fine_plane(k, f, own, before, after):
    if k < HF:
        return before[FACE * f + NY * k : FACE * f + NY * (k + 1)]
    if k < HF + NX:
        return own[f][k - HF]
    k = k - HF - NX
    return after[FACE * f + NY * k : FACE * f + NY * (k + 1)]


def coarse_plane(c, f, fields, mine, before, after):
    ref, c = (before, c) if c < HC else (mine, c - HC) if c < HC + CX else (after, c - HC - CX)
    at = FACE * fields + CY * (CX * f + c)
    return ref[at : at + CY]


def rows_kernel(fields, *refs):
    own, (mine, before, after, up_ref, down_ref) = refs[:fields], refs[fields:]
    for k in range(EX):
        for f in range(fields):
            plane = fine_plane(k, f, own, before, after)
            down_ref[k, 4 * f : 4 * f + HF] = plane[:HF]
            up_ref[k, 4 * f : 4 * f + HF] = plane[NY - HF :]
    for c in range(EC):
        for f in range(fields):
            plane = coarse_plane(c, f, fields, mine, before, after)
            at, row = (EX + c, 4 * f) if fields == 2 else (c, 4)
            down_ref[at, row : row + HC] = plane[:HC]
            up_ref[at, row : row + HC] = plane[CY - HC :]


def lanes_kernel(fields, *refs):
    own, refs = refs[:fields], refs[fields:]
    mine, before, after, low, high = refs[:5]
    fine, coarse, (up_ref, down_ref) = refs[5 : 5 + fields], refs[5 + fields : 5 + 2 * fields], refs[5 + 2 * fields :]
    lane = lanes((EY, NZ))
    for f in range(fields):
        up = jnp.zeros((EY, NZ), F32)
        down = jnp.zeros((EY, NZ), F32)
        for k in range(EX):
            fine[f][k, 0:8] = jnp.zeros((8, NZ), F32)
            fine[f][k, EY - 8 : EY] = jnp.zeros((8, NZ), F32)
            fine[f][k, 4 - HF : 4] = low[k, 4 * f : 4 * f + HF]
            fine[f][k, 4 : 4 + NY] = fine_plane(k, f, own, before, after)
            fine[f][k, 4 + NY : 4 + NY + HF] = high[k, 4 * f : 4 * f + HF]
            plane = fine[f][k]
            here = lane // 4 == k
            up = jnp.where(here, roll(plane, 4 * k - (NZ - 4)), up)
            down = jnp.where(here, roll(plane, 4 * k), down)
        up_ref[EY * f : EY * (f + 1)] = up
        down_ref[EY * f : EY * (f + 1)] = down
    lane = lanes((ER, NZ))
    for f in range(fields):
        for half in range(2):
            up = jnp.zeros((ER, NZ), F32)
            down = jnp.zeros((ER, NZ), F32)
            for c in range(8 * half, min(EC, 8 * half + 8)):
                at, row = (EX + c, 4 * f) if fields == 2 else (c, 4)
                coarse[f][c, 0:HC] = low[at, row : row + HC]
                coarse[f][c, HC : HC + CY] = coarse_plane(c, f, fields, mine, before, after)
                coarse[f][c, HC + CY : ER] = high[at, row : row + HC]
                plane = coarse[f][c]
                here = lane // 16 == c - 8 * half
                up = jnp.where(here, roll(plane, 16 * (c - 8 * half) - (NZ - 16)), up)
                down = jnp.where(here, roll(plane, 16 * (c - 8 * half)), down)
            at = EY * fields + ER * (2 * f + half)
            up_ref[at : at + ER] = up
            down_ref[at : at + ER] = down


def spread_fine(k, f, before, after):
    lane = lanes((EY, NZ))
    right = roll(after[EY * f : EY * (f + 1)], -4 * k)
    left = roll(before[EY * f : EY * (f + 1)], NZ - 4 - 4 * k)
    return jnp.where(lane < 4, right, jnp.where(lane >= NZ - 4, left, 0.0))


def spread_coarse(c, f, fields, before, after):
    lane = lanes((ER, NZ))
    at, place = EY * fields + ER * (2 * f + c // 8), 16 * (c % 8)
    right = roll(after[at : at + ER], -place)
    left = roll(before[at : at + ER], NZ - 16 - place)
    return jnp.where(lane < 16, right, jnp.where(lane >= NZ - 16, left, 0.0))


def crossed(block, beyond, step):
    lane = lanes(block.shape)
    below, below_beyond = roll(block, step), roll(beyond, step)
    above, above_beyond = roll(block, -step), roll(beyond, -step)
    low, high = lane < step, lane >= NZ - step
    return (
        jnp.where(low, below_beyond, below) + jnp.where(high, above_beyond, above),
        jnp.where(low, below, below_beyond) + jnp.where(high, above, above_beyond),
    )


PAD = 8


def neighbours(src, k, rows, step=1):
    at = PAD
    here = [src[part, k, at : at + rows] for part in range(2)]
    along = crossed(here[0], here[1], step)
    out = []
    for part in range(2):
        beside = src[part, k - 1, at : at + rows] + src[part, k + 1, at : at + rows]
        beside = beside + (src[part, k, at - 1 : at - 1 + rows] + src[part, k, at + 1 : at + 1 + rows])
        out.append(beside + along[part])
    return here, out


def expand(coarse, part, k, lo):
    c = (k - HF) // COARSEN + HC
    first = lax.broadcasted_iota(jnp.int32, (8, NZ), 0) < 4
    groups = []
    for j in range(EY // 8):
        row = PAD + 3 + 2 * j
        a = jnp.broadcast_to(coarse[part, c, row : row + 1], (8, NZ))
        b = jnp.broadcast_to(coarse[part, c, row + 1 : row + 2], (8, NZ))
        groups.append(jnp.where(first, a, b))
    return jnp.concatenate(groups, axis=0)


def precondition(rhs, weight, crhs, cweight, fa, fb, ca, cb):
    for ref, rows in ((fa, EY), (fb, EY), (ca, ER), (cb, ER)):
        for part in range(2):
            for k in range(ref.shape[1]):
                ref[part, k, 0:PAD] = jnp.zeros((PAD, NZ), F32)
                ref[part, k, PAD + rows :] = jnp.zeros((PAD, NZ), F32)
    for k in range(EC):
        for part in range(2):
            ca[part, k, PAD : PAD + ER] = cweight[part][k] * crhs[part][k]
    src, dst = ca, cb
    for sweep in range(1, CSWEEPS):
        for k in range(sweep, EC - sweep):
            here, beside = neighbours(src, k, ER, COARSEN)
            for part in range(2):
                dst[part, k, PAD : PAD + ER] = keep * here[part] + cweight[part][k] * (crhs[part][k] + beside[part])
        src, dst = dst, src
    coarse = src
    for k in range(EX):
        for part in range(2):
            fa[part, k, PAD : PAD + EY] = weight[part][k] * rhs[part][k]
    src, dst = fa, fb
    for sweep in range(1, FSWEEPS):
        for k in range(sweep, EX - sweep):
            here, beside = neighbours(src, k, EY)
            for part in range(2):
                new = keep * here[part] + weight[part][k] * (rhs[part][k] + beside[part])
                if sweep == FSWEEPS - 1:
                    new = new + expand(coarse, part, k, 0)
                dst[part, k, PAD : PAD + EY] = new
        src, dst = dst, src


def image_plane(src, d_ref, i):
    k, at = i + HF, PAD + 4
    here = src[0, k, at : at + NY]
    beside = src[0, k - 1, at : at + NY] + src[0, k + 1, at : at + NY]
    beside = beside + (src[0, k, at - 1 : at - 1 + NY] + src[0, k, at + 1 : at + 1 + NY])
    along, _ = crossed(here, src[1, k, at : at + NY], 1)
    return here, (6.0 + d_ref[i]) * here - (beside + along)


def add_up(x):
    return (x[0:8] + x[8:16]) + (x[16:24] + x[24:32])


def store_sums(out_ref, totals):
    row = lax.broadcasted_iota(jnp.int32, (8, NZ), 0)
    out = jnp.zeros((8, NZ), F32)
    for i, total in enumerate(totals):
        out = jnp.where(row == i, jnp.broadcast_to(jnp.sum(total, axis=0, keepdims=True), (8, NZ)), out)
    out_ref[...] = out


def first_kernel(
    b_ref, d_ref, b, v, g, vc, before, after, p_ref, q_ref, vh_ref, vch_ref, up_ref, down_ref, sum_ref,
    bh_ref, gh_ref, fa, fb, ca, cb, tmp,
):
    for k in range(EX):
        bh_ref[k] = spread_fine(k, 0, before, after)
        vh_ref[k] = spread_fine(k, 1, before, after)
    for c in range(EC):
        gh_ref[c] = spread_coarse(c, 0, 2, before, after)
        vch_ref[c] = spread_coarse(c, 1, 2, before, after)
    precondition((b, bh_ref), (v, vh_ref), (g, gh_ref), (vc, vch_ref), fa, fb, ca, cb)
    rp = jnp.zeros((8, NZ), F32)
    pq = jnp.zeros((8, NZ), F32)
    for i in range(NX):
        p, q = image_plane(fa, d_ref, i)
        p_ref[i] = p
        q_ref[i] = q
        rp = rp + add_up(b_ref[i] * p)
        pq = pq + add_up(p * q)
    store_sums(sum_ref, [rp, pq])
    for c in range(CX):
        mean = block_sums([q_ref[COARSEN * c + k] for k in range(COARSEN)], tmp) * 0.25
        for ref in (up_ref, down_ref):
            ref[FACE + CY * c : FACE + CY * (c + 1)] = mean
    for k in range(HF):
        down_ref[NY * k : NY * (k + 1)] = q_ref[k]
        up_ref[NY * k : NY * (k + 1)] = q_ref[NX - HF + k]


def second_kernel(
    b_ref, d_ref, p_ref, q_ref, q, v, vh_ref, gq, vc, vch_ref, before, after, first_ref, m_ref, im_ref, sum_ref,
    qh_ref, gh_ref, fa, fb, ca, cb,
):
    for k in range(EX):
        qh_ref[k] = spread_fine(k, 0, before, after)
    for c in range(EC):
        gh_ref[c] = spread_coarse(c, 0, 1, before, after)
    precondition((q, qh_ref), (v, vh_ref), (gq, gh_ref), (vc, vch_ref), fa, fb, ca, cb)
    sums = [jnp.zeros((8, NZ), F32)] * 4
    for i in range(NX):
        m, im = image_plane(fa, d_ref, i)
        m_ref[i] = m
        im_ref[i] = im
        pairs = ((q_ref[i], m), (b_ref[i], m), (p_ref[i], im), (m, im))
        sums = [s + add_up(x * y) for s, (x, y) in zip(sums, pairs)]
    store_sums(sum_ref, [first_ref[0:1], first_ref[1:2]] + sums)


def last_kernel(b_ref, p_ref, q_ref, m_ref, im_ref, sum_ref, x_ref, r_ref):
    rp, pq, qm, rm, pim, mim = [jnp.sum(sum_ref[i : i + 1], axis=1, keepdims=True) for i in range(6)]
    alpha = rp / pq
    rho = rp - alpha * (pq + rm) + alpha * alpha * qm
    scale = 1.0 + rho / rp
    alpha_next = rho / (scale * scale * pq - scale * alpha * (pim + qm) + alpha * alpha * mim)
    along = alpha + alpha_next * scale
    across = alpha_next * alpha
    for i in range(NX):
        x_ref[i] = along * p_ref[i] - across * m_ref[i]
        r_ref[i] = b_ref[i] - along * q_ref[i] + across * im_ref[i]


def call(kernel, outs, scratch=(), name=None):
    def run(*args):
        return pl.pallas_call(
            kernel,
            out_shape=[jax.ShapeDtypeStruct(shape, F32) for shape in outs],
            in_specs=[VMEM] * len(args),
            out_specs=[VMEM] * len(outs),
            scratch_shapes=[pltpu.VMEM(shape, F32) for shape in scratch],
            compiler_params=pltpu.CompilerParams(vmem_limit_bytes=24 * 2**20),
            name=name,
        )(*args)

    return run


def both_ways(up, down, axis):
    count = lax.axis_size(axis)
    before = lax.ppermute(up, axis, [(i, i + 1) for i in range(count - 1)])
    after = lax.ppermute(down, axis, [(i + 1, i) for i in range(count - 1)])
    return before, after


def total(x, axis):
    count = lax.axis_size(axis)
    spread = jnp.broadcast_to(x[None], (count,) + x.shape)
    return jnp.sum(lax.all_to_all(spread, axis, 0, 0, tiled=True), axis=0)


def exchange(own, up, down, fields):
    mine = up
    before, after = both_ways(up, down, "gx")
    height = EX + EC if fields == 2 else EX
    up, down = call(functools.partial(rows_kernel, fields), [(height, 8, NZ)] * 2, name="rows")(*own, mine, before, after)
    low, high = both_ways(up, down, "gy")
    message = (EY + 2 * ER) * fields
    arrays = call(
        functools.partial(lanes_kernel, fields),
        [(EX, EY, NZ)] * fields + [(EC, ER, NZ)] * fields + [(message, NZ)] * 2,
        name="lanes",
    )(*own, mine, before, after, low, high)
    return list(arrays[:-2]) + list(both_ways(arrays[-2], arrays[-1], "gz"))


def on_device(b, d):
    block, fine, coarse = (NX, NY, NZ), (EX, EY, NZ), (EC, ER, NZ)
    work = [(2, EX, EY + 2 * PAD, NZ)] * 2 + [(2, EC, ER + 2 * PAD, NZ)] * 2
    face = FACE + CX * CY
    v, up, down = call(start_kernel, [block, (2 * face, NZ), (2 * face, NZ)], [(NY, NZ)], name="start")(b, d)
    be, ve, ge, vce, before, after = exchange((b, v), up, down, 2)
    p, q, vh, vch, up, down, sums = call(
        first_kernel,
        [block, block, fine, coarse, (face, NZ), (face, NZ), (8, NZ)],
        [fine, coarse] + work + [(NY, NZ)],
        name="first",
    )(b, d, be, ve, ge, vce, before, after)
    qe, gqe, before, after = exchange((q,), up, down, 1)
    m, im, sums = call(second_kernel, [block, block, (8, NZ)], [fine, coarse] + work, name="second")(
        b, d, p, q, qe, ve, vh, gqe, vce, vch, before, after, sums
    )
    for axis in ("gz", "gy", "gx"):
        sums = total(sums, axis)
    return call(last_kernel, [block, block], name="last")(b, p, q, m, im, sums)


def solution(mesh):
    spec = P("gx", "gy", "gz")
    return jax.shard_map(on_device, mesh=mesh, in_specs=(spec, spec), out_specs=(spec, spec), check_vma=False)
```

time: 689 us -> 117 us (0.17)
  blocking collectives: 346 us -> 53 us
  starting transfers between devices: 211 us -> 33.6 us
  local copies, waits for them, and re-layouts: 57.9 us -> 1.93 us
  waiting for transfers between devices: 45.6 us -> 21 us
  other arithmetic: 18.5 us -> 0.04 us
    psum x3 -> x0, blocking collectives: 346 us -> none  [the longest x2 237 us: precond_sum(): return lax.psum(jnp.sum(residual * precond), ('gx', 'gy', 'gz'))]
    ppermute x72 -> x12, starting transfers between devices: 211 us -> 33.6 us  [the longest x6 21.3 us: both_ways(): after = lax.ppermute(down, axis, [(i + 1, i) for i in range(count - 1)])]
    all_to_all x0 -> x3, blocking collectives: none -> 53 us  [total(): return jnp.sum(lax.all_to_all(spread, axis, 0, 0, tiled=True), axis=0)]
    reshape x5 -> x0, local copies, waits for them, and re-layouts: 47.3 us -> none  [the longest x3 31 us: block_mean(): field.reshape(first // COARSEN, COARSEN, second // COARSEN, COARSEN, thir...]
    ppermute x72 -> x12, waiting for transfers between devices: 45.6 us -> 21 us  [the longest x6 15.7 us: both_ways(): after = lax.ppermute(down, axis, [(i + 1, i) for i in range(count - 1)])]
    reduce_sum x6 -> x3, other arithmetic: 15.1 us -> 0.04 us  [total(): return jnp.sum(lax.all_to_all(spread, axis, 0, 0, tiled=True), axis=0)]
    broadcast_in_dim x2 -> x3, local copies, waits for them, and re-layouts: 9.01 us -> 0.02 us  [total(): spread = jnp.broadcast_to(x[None], (count,) + x.shape)]
  transfers between devices with their start and end apart: 72 -> 12, of which waited for: 24 -> 9; matrix products, arithmetic and copies ran while one was open for 4% -> 0% of each run, Pallas kernels for 0% -> 0%
where the time goes in v1:
time: 117 us
  blocking collectives  53 us (45%)
  starting transfers between devices  33.6 us (29%)
  waiting for transfers between devices  21 us (18%)
  Pallas kernels  6.44 us (6%)
  local copies, waits for them, and re-layouts  1.93 us (2%)
    all_to_all x3, blocking collectives, total(): return jnp.sum(lax.all_to_all(spread, axis, 0, 0, tiled=True), axis=0)  53 us
    ppermute x6, starting transfers between devices, both_ways(): after = lax.ppermute(down, axis, [(i + 1, i) for i in range(count - 1)])  21.3 us
    ppermute x6, waiting for transfers between devices, both_ways(): after = lax.ppermute(down, axis, [(i + 1, i) for i in range(count - 1)])  15.7 us
    ppermute x6, starting transfers between devices, both_ways(): before = lax.ppermute(up, axis, [(i, i + 1) for i in range(count - 1)])  12.3 us
    pallas_call x8, Pallas kernels, run(): pl.pallas_call(kernel, out_shape=[jax.ShapeDtypeStruct(shape, F32) for sh...  6.44 us
    ppermute x6, waiting for transfers between devices, both_ways(): before = lax.ppermute(up, axis, [(i, i + 1) for i in range(count - 1)])  5.3 us
  transfers between devices with their start and end apart: 12, of which 9 were waited for; matrix products, arithmetic and copies ran while one was open for 0% of the time, Pallas kernels for 0%

profile of v1, /device:TPU:1, one launch (start us, length us, event | category | flops | bytes accessed | tf_op | source)
XLA Modules:
  0.0 116.8 jit_solution(16523187560513460018)
XLA Ops:
  0.6 0.0 copy-start
  0.6 0.9 copy-done
  1.6 0.0 copy-start.2
  1.6 0.9 copy-done.2
  2.5 0.2 start.1
  2.8 12.4 %collective-permute-start.1 = (f32[256,128]{1,0:T(8,128)S(1)}, f32[256,128]{1,0:T(8,128)S(1)}, u32[]{:S(2)}, u32[]{:S(2)}) collective-permute-start(f32[256,128]{1,0:T(8,128)S(1)} %get-tuple-element.31), channel_id=1, source_target_pairs={{32,0},{64,32},{96,64},{128,96},{160,128},{192,160},{224,192},{256... | collective-permute-start | bytes 393224 | tf_op jit(solution)/shard_map/ppermute | solution.py:322
  15.2 1.9 %collective-permute-start = (f32[256,128]{1,0:T(8,128)S(1)}, f32[256,128]{1,0:T(8,128)S(1)}, u32[]{:S(2)}, u32[]{:S(2)}) collective-permute-start(f32[256,128]{1,0:T(8,128)S(1)} %get-tuple-element.30.refs_2_), channel_id=1, source_target_pairs={{0,32},{32,64},{64,96},{96,128},{128,160},{160,192},{192,224},{224... | collective-permute-start | bytes 393224 | tf_op jit(solution)/shard_map/ppermute | solution.py:321
  17.1 0.0 collective-permute-done.1.refs_4_
  17.2 1.9 %collective-permute-done.refs_3_ = f32[256,128]{1,0:T(8,128)S(1)} collective-permute-done((f32[256,128]{1,0:T(8,128)S(1)}, f32[256,128]{1,0:T(8,128)S(1)}, u32[]{:S(2)}, u32[]{:S(2)}) %collective-permute-start) | collective-permute-done | bytes 131104 | tf_op jit(solution)/shard_map/ppermute | solution.py:321
  19.1 1.3 %collective-permute-start.2 = (f32[34,8,128]{2,1,0:T(8,128)S(1)}, f32[34,8,128]{2,1,0:T(8,128)S(1)}, u32[]{:S(2)}, u32[]{:S(2)}) collective-permute-start(f32[34,8,128]{2,1,0:T(8,128)S(1)} %get-tuple-element.32), channel_id=1, source_target_pairs={{0,4},{4,8},{8,12},{12,16},{16,20},{20,24},{24,28},{1,5},{5,9},{9,... | collective-permute-start | bytes 417800 | tf_op jit(solution)/shard_map/ppermute | solution.py:321
  20.4 0.0 copy-start.3
  20.4 1.4 %collective-permute-start.3 = (f32[34,8,128]{2,1,0:T(8,128)S(1)}, f32[34,8,128]{2,1,0:T(8,128)S(1)}, u32[]{:S(2)}, u32[]{:S(2)}) collective-permute-start(f32[34,8,128]{2,1,0:T(8,128)S(1)} %get-tuple-element.33), channel_id=1, source_target_pairs={{4,0},{8,4},{12,8},{16,12},{20,16},{24,20},{28,24},{5,1},{9,5},{13... | collective-permute-start | bytes 417800 | tf_op jit(solution)/shard_map/ppermute | solution.py:322
  21.9 1.7 %collective-permute-done.2.refs_5_ = f32[34,8,128]{2,1,0:T(8,128)S(1)} collective-permute-done((f32[34,8,128]{2,1,0:T(8,128)S(1)}, f32[34,8,128]{2,1,0:T(8,128)S(1)}, u32[]{:S(2)}, u32[]{:S(2)}) %collective-permute-start.2) | collective-permute-done | bytes 139296 | tf_op jit(solution)/shard_map/ppermute | solution.py:321
  23.6 4.5 %collective-permute-done.3.refs_6_ = f32[34,8,128]{2,1,0:T(8,128)S(1)} collective-permute-done((f32[34,8,128]{2,1,0:T(8,128)S(1)}, f32[34,8,128]{2,1,0:T(8,128)S(1)}, u32[]{:S(2)}, u32[]{:S(2)}) %collective-permute-start.3) | collective-permute-done | bytes 139296 | tf_op jit(solution)/shard_map/ppermute | solution.py:322
  28.1 0.7 lanes.2
  28.8 1.3 %collective-permute-start.4 = (f32[144,128]{1,0:T(8,128)S(1)}, f32[144,128]{1,0:T(8,128)S(1)}, u32[]{:S(2)}, u32[]{:S(2)}) collective-permute-start(f32[144,128]{1,0:T(8,128)S(1)} %get-tuple-element.38), channel_id=1, source_target_pairs={{0,1},{1,2},{2,3},{4,5},{5,6},{6,7},{8,9},{9,10},{10,11},{12,13},{... | collective-permute-start | bytes 221192 | tf_op jit(solution)/shard_map/ppermute | solution.py:321
  30.1 1.3 %collective-permute-start.5 = (f32[144,128]{1,0:T(8,128)S(1)}, f32[144,128]{1,0:T(8,128)S(1)}, u32[]{:S(2)}, u32[]{:S(2)}) collective-permute-start(f32[144,128]{1,0:T(8,128)S(1)} %get-tuple-element.39), channel_id=1, source_target_pairs={{1,0},{2,1},{3,2},{5,4},{6,5},{7,6},{9,8},{10,9},{11,10},{13,12},{... | collective-permute-start | bytes 221192 | tf_op jit(solution)/shard_map/ppermute | solution.py:322
  31.4 0.3 collective-permute-done.4.before
  31.7 3.5 %collective-permute-done.5.after = f32[144,128]{1,0:T(8,128)S(1)} collective-permute-done((f32[144,128]{1,0:T(8,128)S(1)}, f32[144,128]{1,0:T(8,128)S(1)}, u32[]{:S(2)}, u32[]{:S(2)}) %collective-permute-start.5) | collective-permute-done | bytes 73760 | tf_op jit(solution)/shard_map/ppermute | solution.py:322
  35.2 0.0 copy-done.3
  35.2 2.3 %first.1 = (f32[16,32,128]{2,1,0:T(8,128)S(1)}, f32[16,32,128]{2,1,0:T(8,128)S(1)}, f32[22,40,128]{2,1,0:T(8,128)S(1)}, f32[12,16,128]{2,1,0:T(8,128)S(1)}, f32[...) custom-call(f32[16,32,128]{2,1,0:T(8,128)S(1)} %copy-done, f32[16,32,128]{2,1,0:T(8,128)S(1)} %copy-done.3, ...), custom_call_target="tpu_custom_call" | custom-call | tf_op jit(solution)/shard_map/first/pallas_call | solution.py:306
  37.5 3.5 %collective-permute-start.7 = (f32[128,128]{1,0:T(8,128)S(1)}, f32[128,128]{1,0:T(8,128)S(1)}, u32[]{:S(2)}, u32[]{:S(2)}) collective-permute-start(f32[128,128]{1,0:T(8,128)S(1)} %get-tuple-element.43), channel_id=1, source_target_pairs={{32,0},{64,32},{96,64},{128,96},{160,128},{192,160},{224,192},{256... | collective-permute-start | bytes 196616 | tf_op jit(solution)/shard_map/ppermute | solution.py:322
  40.9 3.3 %collective-permute-start.6 = (f32[128,128]{1,0:T(8,128)S(1)}, f32[128,128]{1,0:T(8,128)S(1)}, u32[]{:S(2)}, u32[]{:S(2)}) collective-permute-start(f32[128,128]{1,0:T(8,128)S(1)} %get-tuple-element.42.refs_1_), channel_id=1, source_target_pairs={{0,32},{32,64},{64,96},{96,128},{128,160},{160,192},{192,224},{224... | collective-permute-start | bytes 196616 | tf_op jit(solution)/shard_map/ppermute | solution.py:321
  44.3 0.0 collective-permute-done.7.refs_3_
  44.3 1.3 %collective-permute-done.6.refs_2_ = f32[128,128]{1,0:T(8,128)S(1)} collective-permute-done((f32[128,128]{1,0:T(8,128)S(1)}, f32[128,128]{1,0:T(8,128)S(1)}, u32[]{:S(2)}, u32[]{:S(2)}) %collective-permute-start.6) | collective-permute-done | bytes 65568 | tf_op jit(solution)/shard_map/ppermute | solution.py:321
  45.6 1.3 %collective-permute-start.8 = (f32[22,8,128]{2,1,0:T(8,128)S(1)}, f32[22,8,128]{2,1,0:T(8,128)S(1)}, u32[]{:S(2)}, u32[]{:S(2)}) collective-permute-start(f32[22,8,128]{2,1,0:T(8,128)S(1)} %get-tuple-element.44), channel_id=1, source_target_pairs={{0,4},{4,8},{8,12},{12,16},{16,20},{20,24},{24,28},{1,5},{5,9},{9,... | collective-permute-start | bytes 270344 | tf_op jit(solution)/shard_map/ppermute | solution.py:321
  46.9 0.0 copy-start.1
  46.9 1.4 %collective-permute-start.9 = (f32[22,8,128]{2,1,0:T(8,128)S(1)}, f32[22,8,128]{2,1,0:T(8,128)S(1)}, u32[]{:S(2)}, u32[]{:S(2)}) collective-permute-start(f32[22,8,128]{2,1,0:T(8,128)S(1)} %get-tuple-element.45), channel_id=1, source_target_pairs={{4,0},{8,4},{12,8},{16,12},{20,16},{24,20},{28,24},{5,1},{9,5},{13... | collective-permute-start | bytes 270344 | tf_op jit(solution)/shard_map/ppermute | solution.py:322
  48.4 0.1 collective-permute-done.8.refs_4_
  48.5 4.2 %collective-permute-done.9.refs_5_ = f32[22,8,128]{2,1,0:T(8,128)S(1)} collective-permute-done((f32[22,8,128]{2,1,0:T(8,128)S(1)}, f32[22,8,128]{2,1,0:T(8,128)S(1)}, u32[]{:S(2)}, u32[]{:S(2)}) %collective-permute-start.9) | collective-permute-done | bytes 90144 | tf_op jit(solution)/shard_map/ppermute | solution.py:322
  52.7 0.4 lanes.3
  53.1 3.1 %collective-permute-start.10 = (f32[72,128]{1,0:T(8,128)S(1)}, f32[72,128]{1,0:T(8,128)S(1)}, u32[]{:S(2)}, u32[]{:S(2)}) collective-permute-start(f32[72,128]{1,0:T(8,128)S(1)} %get-tuple-element.50), channel_id=1, source_target_pairs={{0,1},{1,2},{2,3},{4,5},{5,6},{6,7},{8,9},{9,10},{10,11},{12,13},{... | collective-permute-start | bytes 110600 | tf_op jit(solution)/shard_map/ppermute | solution.py:321
  56.2 1.3 %collective-permute-start.11 = (f32[72,128]{1,0:T(8,128)S(1)}, f32[72,128]{1,0:T(8,128)S(1)}, u32[]{:S(2)}, u32[]{:S(2)}) collective-permute-start(f32[72,128]{1,0:T(8,128)S(1)} %get-tuple-element.51), channel_id=1, source_target_pairs={{1,0},{2,1},{3,2},{5,4},{6,5},{7,6},{9,8},{10,9},{11,10},{13,12},{... | collective-permute-start | bytes 110600 | tf_op jit(solution)/shard_map/ppermute | solution.py:322
  57.5 0.0 collective-permute-done.10.before
  57.5 3.4 %collective-permute-done.11.after = f32[72,128]{1,0:T(8,128)S(1)} collective-permute-done((f32[72,128]{1,0:T(8,128)S(1)}, f32[72,128]{1,0:T(8,128)S(1)}, u32[]{:S(2)}, u32[]{:S(2)}) %collective-permute-start.11) | collective-permute-done | bytes 36896 | tf_op jit(solution)/shard_map/ppermute | solution.py:322
  60.9 0.0 copy-done.1
  60.9 1.9 %second.1 = (f32[16,32,128]{2,1,0:T(8,128)S(1)}, f32[16,32,128]{2,1,0:T(8,128)S(1)}, f32[8,128]{1,0:T(8,128)S(1)}) custom-call(f32[16,32,128]{2,1,0:T(8,128)S(1)} %copy-done.1, f32[16,32,128]{2,1,0:T(8,128)S(1)} %copy-done.3, f32[16,32,128]{2,1,0:T(8,128)S(1)} %get-tuple-element.40.p_ref, f32[16,32,128]{2,1,0:T(8,128)S(1)} %get-tuple-element.41.refs_0_.q_ref, ...), custom_call_target="tpu_custom_call" | custom-call | tf_op jit(solution)/shard_map/second/pallas_call | solution.py:306
  62.8 6.6 %all_to_all.15 = f32[4,8,128]{2,1,0:T(8,128)S(1)} all-to-all(f32[4,8,128]{2,1,0:T(8,128)S(1)} %broadcast_in_dim.6), channel_id=1, replica_groups=mesh['gx'=24,'gy'=8,'gz'=4] {'gz'}, dimensions={0} | all-to-all | bytes 32768 | tf_op jit(solution)/shard_map/all_to_all | solution.py:329
  69.4 13.1 %all_to_all.16 = f32[8,8,128]{2,1,0:T(8,128)S(1)} all-to-all(f32[8,8,128]{2,1,0:T(8,128)S(1)} %broadcast_in_dim.7), channel_id=1, replica_groups=mesh['gx'=24,'gy'=8,'gz'=4] {'gy'}, dimensions={0} | all-to-all | bytes 65536 | tf_op jit(solution)/shard_map/all_to_all | solution.py:329
  82.5 33.3 %all_to_all.17 = f32[24,8,128]{2,1,0:T(8,128)S(1)} all-to-all(f32[24,8,128]{2,1,0:T(8,128)S(1)} %broadcast_in_dim.8), channel_id=1, replica_groups=mesh['gx'=24,'gy'=8,'gz'=4] {'gx'}, dimensions={0} | all-to-all | bytes 196608 | tf_op jit(solution)/shard_map/all_to_all | solution.py:329
  115.8 1.0 last.1
  (8 shorter events, 0.1 us)
Async XLA Ops:
  0.6 1.0 copy-start
  1.6 0.9 copy-start.2
  2.8 14.4 %collective-permute-start.1 = (f32[256,128]{1,0:T(8,128)S(1)}, f32[256,128]{1,0:T(8,128)S(1)}, u32[]{:S(2)}, u32[]{:S(2)}) collective-permute-start(f32[256,128]{1,0:T(8,128)S(1)} %get-tuple-element.31), channel_id=1, source_target_pairs={{32,0},{64,32},{96,64},{128,96},{160,128},{192,160},{224,192},{256... | collective-permute-start | bytes 393224 | tf_op jit(solution)/shard_map/ppermute | solution.py:322
  15.2 3.9 %collective-permute-start = (f32[256,128]{1,0:T(8,128)S(1)}, f32[256,128]{1,0:T(8,128)S(1)}, u32[]{:S(2)}, u32[]{:S(2)}) collective-permute-start(f32[256,128]{1,0:T(8,128)S(1)} %get-tuple-element.30.refs_2_), channel_id=1, source_target_pairs={{0,32},{32,64},{64,96},{96,128},{128,160},{160,192},{192,224},{224... | collective-permute-start | bytes 393224 | tf_op jit(solution)/shard_map/ppermute | solution.py:321
  19.1 4.5 %collective-permute-start.2 = (f32[34,8,128]{2,1,0:T(8,128)S(1)}, f32[34,8,128]{2,1,0:T(8,128)S(1)}, u32[]{:S(2)}, u32[]{:S(2)}) collective-permute-start(f32[34,8,128]{2,1,0:T(8,128)S(1)} %get-tuple-element.32), channel_id=1, source_target_pairs={{0,4},{4,8},{8,12},{12,16},{16,20},{20,24},{24,28},{1,5},{5,9},{9,... | collective-permute-start | bytes 417800 | tf_op jit(solution)/shard_map/ppermute | solution.py:321
  20.4 14.8 %copy-start.3 = (f32[16,32,128]{2,1,0:T(8,128)S(1)}, f32[16,32,128]{2,1,0:T(8,128)}, u32[]{:S(2)}) copy-start(f32[16,32,128]{2,1,0:T(8,128)} %d_ref.5) | copy-start | bytes 786436
  20.4 7.7 %collective-permute-start.3 = (f32[34,8,128]{2,1,0:T(8,128)S(1)}, f32[34,8,128]{2,1,0:T(8,128)S(1)}, u32[]{:S(2)}, u32[]{:S(2)}) collective-permute-start(f32[34,8,128]{2,1,0:T(8,128)S(1)} %get-tuple-element.33), channel_id=1, source_target_pairs={{4,0},{8,4},{12,8},{16,12},{20,16},{24,20},{28,24},{5,1},{9,5},{13... | collective-permute-start | bytes 417800 | tf_op jit(solution)/shard_map/ppermute | solution.py:322
  28.8 2.9 %collective-permute-start.4 = (f32[144,128]{1,0:T(8,128)S(1)}, f32[144,128]{1,0:T(8,128)S(1)}, u32[]{:S(2)}, u32[]{:S(2)}) collective-permute-start(f32[144,128]{1,0:T(8,128)S(1)} %get-tuple-element.38), channel_id=1, source_target_pairs={{0,1},{1,2},{2,3},{4,5},{5,6},{6,7},{8,9},{9,10},{10,11},{12,13},{... | collective-permute-start | bytes 221192 | tf_op jit(solution)/shard_map/ppermute | solution.py:321
  30.1 5.1 %collective-permute-start.5 = (f32[144,128]{1,0:T(8,128)S(1)}, f32[144,128]{1,0:T(8,128)S(1)}, u32[]{:S(2)}, u32[]{:S(2)}) collective-permute-start(f32[144,128]{1,0:T(8,128)S(1)} %get-tuple-element.39), channel_id=1, source_target_pairs={{1,0},{2,1},{3,2},{5,4},{6,5},{7,6},{9,8},{10,9},{11,10},{13,12},{... | collective-permute-start | bytes 221192 | tf_op jit(solution)/shard_map/ppermute | solution.py:322
  37.5 6.8 %collective-permute-start.7 = (f32[128,128]{1,0:T(8,128)S(1)}, f32[128,128]{1,0:T(8,128)S(1)}, u32[]{:S(2)}, u32[]{:S(2)}) collective-permute-start(f32[128,128]{1,0:T(8,128)S(1)} %get-tuple-element.43), channel_id=1, source_target_pairs={{32,0},{64,32},{96,64},{128,96},{160,128},{192,160},{224,192},{256... | collective-permute-start | bytes 196616 | tf_op jit(solution)/shard_map/ppermute | solution.py:322
  40.9 4.7 %collective-permute-start.6 = (f32[128,128]{1,0:T(8,128)S(1)}, f32[128,128]{1,0:T(8,128)S(1)}, u32[]{:S(2)}, u32[]{:S(2)}) collective-permute-start(f32[128,128]{1,0:T(8,128)S(1)} %get-tuple-element.42.refs_1_), channel_id=1, source_target_pairs={{0,32},{32,64},{64,96},{96,128},{128,160},{160,192},{192,224},{224... | collective-permute-start | bytes 196616 | tf_op jit(solution)/shard_map/ppermute | solution.py:321
  45.6 2.8 %collective-permute-start.8 = (f32[22,8,128]{2,1,0:T(8,128)S(1)}, f32[22,8,128]{2,1,0:T(8,128)S(1)}, u32[]{:S(2)}, u32[]{:S(2)}) collective-permute-start(f32[22,8,128]{2,1,0:T(8,128)S(1)} %get-tuple-element.44), channel_id=1, source_target_pairs={{0,4},{4,8},{8,12},{12,16},{16,20},{20,24},{24,28},{1,5},{5,9},{9,... | collective-permute-start | bytes 270344 | tf_op jit(solution)/shard_map/ppermute | solution.py:321
  46.9 14.0 %copy-start.1 = (f32[16,32,128]{2,1,0:T(8,128)S(1)}, f32[16,32,128]{2,1,0:T(8,128)}, u32[]{:S(2)}) copy-start(f32[16,32,128]{2,1,0:T(8,128)} %b_ref.7) | copy-start | bytes 786436
  46.9 5.8 %collective-permute-start.9 = (f32[22,8,128]{2,1,0:T(8,128)S(1)}, f32[22,8,128]{2,1,0:T(8,128)S(1)}, u32[]{:S(2)}, u32[]{:S(2)}) collective-permute-start(f32[22,8,128]{2,1,0:T(8,128)S(1)} %get-tuple-element.45), channel_id=1, source_target_pairs={{4,0},{8,4},{12,8},{16,12},{20,16},{24,20},{28,24},{5,1},{9,5},{13... | collective-permute-start | bytes 270344 | tf_op jit(solution)/shard_map/ppermute | solution.py:322
  53.1 4.4 %collective-permute-start.10 = (f32[72,128]{1,0:T(8,128)S(1)}, f32[72,128]{1,0:T(8,128)S(1)}, u32[]{:S(2)}, u32[]{:S(2)}) collective-permute-start(f32[72,128]{1,0:T(8,128)S(1)} %get-tuple-element.50), channel_id=1, source_target_pairs={{0,1},{1,2},{2,3},{4,5},{5,6},{6,7},{8,9},{9,10},{10,11},{12,13},{... | collective-permute-start | bytes 110600 | tf_op jit(solution)/shard_map/ppermute | solution.py:321
  56.2 4.7 %collective-permute-start.11 = (f32[72,128]{1,0:T(8,128)S(1)}, f32[72,128]{1,0:T(8,128)S(1)}, u32[]{:S(2)}, u32[]{:S(2)}) collective-permute-start(f32[72,128]{1,0:T(8,128)S(1)} %get-tuple-element.51), channel_id=1, source_target_pairs={{1,0},{2,1},{3,2},{5,4},{6,5},{7,6},{9,8},{10,9},{11,10},{13,12},{... | collective-permute-start | bytes 110600 | tf_op jit(solution)/shard_map/ppermute | solution.py:322

commit v2 on v1

--- a/solution.py
+++ b/solution.py
@@ -1,4 +1,5 @@
 import functools
+import math
 
 import jax
 import jax.numpy as jnp
@@ -48,9 +49,16 @@
     return rows[0] + rows[1] + rows[2] + rows[3]
 
 
-def start_kernel(b_ref, d_ref, v_ref, up_ref, down_ref, tmp):
+def start_kernel(b_hbm, d_hbm, b_ref, d_ref, v_ref, up_ref, down_ref, tmp, sems):
+    copies = [
+        pltpu.make_async_copy(src, dst, sems.at[i])
+        for i, (src, dst) in enumerate(((b_hbm, b_ref), (d_hbm, d_ref)))
+    ]
+    for copy in copies:
+        copy.start()
+    for copy in copies:
+        copy.wait()
     for c in range(CX):
-        fine = []
         for i in range(COARSEN * c, COARSEN * (c + 1)):
             v_ref[i] = damping / (6.0 + d_ref[i])
         g = block_sums([b_ref[COARSEN * c + k] for k in range(COARSEN)], tmp) * 0.25
@@ -65,19 +73,23 @@
             up_ref[FACE * f + NY * k : FACE * f + NY * (k + 1)] = ref[NX - HF + k]
 
 
+def inside():
+    at = lax.axis_index("gx")
+    return at > 0, at < lax.axis_size("gx") - 1
+
+
 def fine_plane(k, f, own, before, after):
-    if k < HF:
-        return before[FACE * f + NY * k : FACE * f + NY * (k + 1)]
-    if k < HF + NX:
+    if HF <= k < HF + NX:
         return own[f][k - HF]
-    k = k - HF - NX
-    return after[FACE * f + NY * k : FACE * f + NY * (k + 1)]
+    ref, ok, k = (before, inside()[0], k) if k < HF else (after, inside()[1], k - HF - NX)
+    return jnp.where(ok, ref[FACE * f + NY * k : FACE * f + NY * (k + 1)], 0.0)
 
 
 def coarse_plane(c, f, fields, mine, before, after):
-    ref, c = (before, c) if c < HC else (mine, c - HC) if c < HC + CX else (after, c - HC - CX)
+    part, c = divmod(c, HC)
     at = FACE * fields + CY * (CX * f + c)
-    return ref[at : at + CY]
+    plane = (before, mine, after)[part][at : at + CY]
+    return plane if part == 1 else jnp.where(inside()[part // 2], plane, 0.0)
 
 
 def rows_kernel(fields, *refs):
@@ -232,12 +244,17 @@
     return (x[0:8] + x[8:16]) + (x[16:24] + x[24:32])
 
 
-def store_sums(out_ref, totals):
-    row = lax.broadcasted_iota(jnp.int32, (8, NZ), 0)
-    out = jnp.zeros((8, NZ), F32)
-    for i, total in enumerate(totals):
-        out = jnp.where(row == i, jnp.broadcast_to(jnp.sum(total, axis=0, keepdims=True), (8, NZ)), out)
-    out_ref[...] = out
+SHARE = NZ // 8
+
+
+def store_sums(out_ref, totals, row=None):
+    row = jnp.zeros((1, NZ), F32) if row is None else row
+    for i, part in totals.items():
+        part = jnp.sum(part, axis=0, keepdims=True)
+        for step in (64, 32, 16):
+            part = part + roll(part, step)
+        row = jnp.where(lanes((1, NZ)) // SHARE == i, part, row)
+    out_ref[...] = row
 
 
 def first_kernel(
@@ -259,7 +276,7 @@
         q_ref[i] = q
         rp = rp + add_up(b_ref[i] * p)
         pq = pq + add_up(p * q)
-    store_sums(sum_ref, [rp, pq])
+    store_sums(sum_ref, {0: rp, 1: pq})
     for c in range(CX):
         mean = block_sums([q_ref[COARSEN * c + k] for k in range(COARSEN)], tmp) * 0.25
         for ref in (up_ref, down_ref):
@@ -285,11 +302,13 @@
         im_ref[i] = im
         pairs = ((q_ref[i], m), (b_ref[i], m), (p_ref[i], im), (m, im))
         sums = [s + add_up(x * y) for s, (x, y) in zip(sums, pairs)]
-    store_sums(sum_ref, [first_ref[0:1], first_ref[1:2]] + sums)
+    store_sums(sum_ref, dict(enumerate(sums, 2)), first_ref[...])
 
 
 def last_kernel(b_ref, p_ref, q_ref, m_ref, im_ref, sum_ref, x_ref, r_ref):
-    rp, pq, qm, rm, pim, mim = [jnp.sum(sum_ref[i : i + 1], axis=1, keepdims=True) for i in range(6)]
+    rp, pq, qm, rm, pim, mim = [
+        jnp.sum(jnp.where(lanes((1, NZ)) // SHARE == i, sum_ref[...], 0.0), axis=1, keepdims=True) for i in range(6)
+    ]
     alpha = rp / pq
     rho = rp - alpha * (pq + rm) + alpha * alpha * qm
     scale = 1.0 + rho / rp
@@ -301,14 +320,14 @@
         r_ref[i] = b_ref[i] - along * q_ref[i] + across * im_ref[i]
 
 
-def call(kernel, outs, scratch=(), name=None):
+def call(kernel, outs, scratch=(), name=None, space=pltpu.VMEM):
     def run(*args):
         return pl.pallas_call(
             kernel,
             out_shape=[jax.ShapeDtypeStruct(shape, F32) for shape in outs],
-            in_specs=[VMEM] * len(args),
+            in_specs=[pl.BlockSpec(memory_space=space)] * len(args),
             out_specs=[VMEM] * len(outs),
-            scratch_shapes=[pltpu.VMEM(shape, F32) for shape in scratch],
+            scratch_shapes=[pltpu.VMEM(shape, F32) if isinstance(shape, tuple) else shape for shape in scratch],
             compiler_params=pltpu.CompilerParams(vmem_limit_bytes=24 * 2**20),
             name=name,
         )(*args)
@@ -318,13 +337,14 @@
 
 def both_ways(up, down, axis):
     count = lax.axis_size(axis)
-    before = lax.ppermute(up, axis, [(i, i + 1) for i in range(count - 1)])
-    after = lax.ppermute(down, axis, [(i + 1, i) for i in range(count - 1)])
+    steps = [(i, (i + 1) % count) for i in range(count if axis == "gx" else count - 1)]
+    before = lax.ppermute(up, axis, steps)
+    after = lax.ppermute(down, axis, [(j, i) for i, j in steps])
     return before, after
 
 
 def total(x, axis):
-    count = lax.axis_size(axis)
+    count = math.prod(lax.axis_size(name) for name in axis)
     spread = jnp.broadcast_to(x[None], (count,) + x.shape)
     return jnp.sum(lax.all_to_all(spread, axis, 0, 0, tiled=True), axis=0)
 
@@ -348,19 +368,21 @@
     block, fine, coarse = (NX, NY, NZ), (EX, EY, NZ), (EC, ER, NZ)
     work = [(2, EX, EY + 2 * PAD, NZ)] * 2 + [(2, EC, ER + 2 * PAD, NZ)] * 2
     face = FACE + CX * CY
-    v, up, down = call(start_kernel, [block, (2 * face, NZ), (2 * face, NZ)], [(NY, NZ)], name="start")(b, d)
+    b, d, v, up, down = call(
+        start_kernel, [block] * 3 + [(2 * face, NZ)] * 2, [(NY, NZ), pltpu.SemaphoreType.DMA((2,))], name="start", space=pl.ANY
+    )(b, d)
     be, ve, ge, vce, before, after = exchange((b, v), up, down, 2)
     p, q, vh, vch, up, down, sums = call(
         first_kernel,
-        [block, block, fine, coarse, (face, NZ), (face, NZ), (8, NZ)],
+        [block, block, fine, coarse, (face, NZ), (face, NZ), (1, NZ)],
         [fine, coarse] + work + [(NY, NZ)],
         name="first",
     )(b, d, be, ve, ge, vce, before, after)
     qe, gqe, before, after = exchange((q,), up, down, 1)
-    m, im, sums = call(second_kernel, [block, block, (8, NZ)], [fine, coarse] + work, name="second")(
+    m, im, sums = call(second_kernel, [block, block, (1, NZ)], [fine, coarse] + work, name="second")(
         b, d, p, q, qe, ve, vh, gqe, vce, vch, before, after, sums
     )
-    for axis in ("gz", "gy", "gx"):
+    for axis in (("gy", "gz"), ("gx",)):
         sums = total(sums, axis)
     return call(last_kernel, [block, block], name="last")(b, p, q, m, im, sums)
 

time: 117 us -> 103 us (0.88)
  blocking collectives: 53 us -> 35.7 us
  starting transfers between devices: 33.6 us -> 36 us
    all_to_all x3 -> x2, blocking collectives: 53 us -> 35.7 us  [total(): return jnp.sum(lax.all_to_all(spread, axis, 0, 0, tiled=True), axis=0)]
    ppermute x12, starting transfers between devices: 33.6 us -> 36 us  [the longest x6 23.3 us: both_ways(): after = lax.ppermute(down, axis, [(j, i) for i, j in steps])]
  transfers between devices with their start and end apart: 12 -> 12, of which waited for: 9 -> 11; matrix products, arithmetic and copies ran while one was open for 0% -> 0% of each run, Pallas kernels for 0% -> 0%
where the time goes in v2:
time: 103 us
  starting transfers between devices  36 us (35%)
  blocking collectives  35.7 us (35%)
  waiting for transfers between devices  21.6 us (21%)
  Pallas kernels  6.73 us (7%)
  local copies, waits for them, and re-layouts  1.92 us (2%)
    all_to_all x2, blocking collectives, total(): return jnp.sum(lax.all_to_all(spread, axis, 0, 0, tiled=True), axis=0)  35.7 us
    ppermute x6, starting transfers between devices, both_ways(): after = lax.ppermute(down, axis, [(j, i) for i, j in steps])  23.3 us
    ppermute x6, waiting for transfers between devices, both_ways(): after = lax.ppermute(down, axis, [(j, i) for i, j in steps])  17.1 us
    ppermute x6, starting transfers between devices, both_ways(): before = lax.ppermute(up, axis, steps)  12.7 us
    pallas_call x8, Pallas kernels, run(): pl.pallas_call(kernel, out_shape=[jax.ShapeDtypeStruct(shape, F32) for sh...  6.73 us
    ppermute x6, waiting for transfers between devices, both_ways(): before = lax.ppermute(up, axis, steps)  4.42 us
  transfers between devices with their start and end apart: 12, of which 11 were waited for; matrix products, arithmetic and copies ran while one was open for 0% of the time, Pallas kernels for 0%

profile of v2, /device:TPU:1, one launch (start us, length us, event | category | flops | bytes accessed | tf_op | source)
XLA Modules:
  0.0 102.7 jit_solution(6555386566944355866)
XLA Ops:
  0.6 0.0 copy-start
  0.6 0.9 copy-done
  1.6 0.0 copy-start.1
  1.6 0.9 copy-done.1
  2.5 0.3 start.1
  2.9 10.5 %collective-permute-start.1 = (f32[256,128]{1,0:T(8,128)S(1)}, f32[256,128]{1,0:T(8,128)S(1)}, u32[]{:S(2)}, u32[]{:S(2)}) collective-permute-start(f32[256,128]{1,0:T(8,128)S(1)} %get-tuple-element.35), channel_id=1, source_target_pairs={{32,0},{64,32},{96,64},{128,96},{160,128},{192,160},{224,192},{256... | collective-permute-start | bytes 393224 | tf_op jit(solution)/shard_map/ppermute | solution.py:342
  13.4 0.0 collective-permute-start
  13.4 1.0 collective-permute-done.1.refs_4_
  14.4 3.0 %collective-permute-done.refs_3_ = f32[256,128]{1,0:T(8,128)S(1)} collective-permute-done((f32[256,128]{1,0:T(8,128)S(1)}, f32[256,128]{1,0:T(8,128)S(1)}, u32[]{:S(2)}, u32[]{:S(2)}) %collective-permute-start) | collective-permute-done | bytes 131104 | tf_op jit(solution)/shard_map/ppermute | solution.py:341
  17.4 3.2 %collective-permute-start.2 = (f32[34,8,128]{2,1,0:T(8,128)S(1)}, f32[34,8,128]{2,1,0:T(8,128)S(1)}, u32[]{:S(2)}, u32[]{:S(2)}) collective-permute-start(f32[34,8,128]{2,1,0:T(8,128)S(1)} %get-tuple-element.36), channel_id=1, source_target_pairs={{0,4},{4,8},{8,12},{12,16},{16,20},{20,24},{24,28},{1,5},{5,9},{9,... | collective-permute-start | bytes 417800 | tf_op jit(solution)/shard_map/ppermute | solution.py:341
  20.6 1.3 %collective-permute-start.3 = (f32[34,8,128]{2,1,0:T(8,128)S(1)}, f32[34,8,128]{2,1,0:T(8,128)S(1)}, u32[]{:S(2)}, u32[]{:S(2)}) collective-permute-start(f32[34,8,128]{2,1,0:T(8,128)S(1)} %get-tuple-element.37), channel_id=1, source_target_pairs={{4,0},{8,4},{12,8},{16,12},{20,16},{24,20},{28,24},{5,1},{9,5},{13... | collective-permute-start | bytes 417800 | tf_op jit(solution)/shard_map/ppermute | solution.py:342
  21.9 0.7 collective-permute-done.2.refs_5_
  22.6 3.8 %collective-permute-done.3.refs_6_ = f32[34,8,128]{2,1,0:T(8,128)S(1)} collective-permute-done((f32[34,8,128]{2,1,0:T(8,128)S(1)}, f32[34,8,128]{2,1,0:T(8,128)S(1)}, u32[]{:S(2)}, u32[]{:S(2)}) %collective-permute-start.3) | collective-permute-done | bytes 139296 | tf_op jit(solution)/shard_map/ppermute | solution.py:342
  26.4 0.7 lanes.2
  27.1 3.1 %collective-permute-start.4 = (f32[144,128]{1,0:T(8,128)S(1)}, f32[144,128]{1,0:T(8,128)S(1)}, u32[]{:S(2)}, u32[]{:S(2)}) collective-permute-start(f32[144,128]{1,0:T(8,128)S(1)} %get-tuple-element.42), channel_id=1, source_target_pairs={{0,1},{1,2},{2,3},{4,5},{5,6},{6,7},{8,9},{9,10},{10,11},{12,13},{... | collective-permute-start | bytes 221192 | tf_op jit(solution)/shard_map/ppermute | solution.py:341
  30.2 1.3 %collective-permute-start.5 = (f32[144,128]{1,0:T(8,128)S(1)}, f32[144,128]{1,0:T(8,128)S(1)}, u32[]{:S(2)}, u32[]{:S(2)}) collective-permute-start(f32[144,128]{1,0:T(8,128)S(1)} %get-tuple-element.43), channel_id=1, source_target_pairs={{1,0},{2,1},{3,2},{5,4},{6,5},{7,6},{9,8},{10,9},{11,10},{13,12},{... | collective-permute-start | bytes 221192 | tf_op jit(solution)/shard_map/ppermute | solution.py:342
  31.5 0.1 collective-permute-done.4.before
  31.6 3.7 %collective-permute-done.5.after = f32[144,128]{1,0:T(8,128)S(1)} collective-permute-done((f32[144,128]{1,0:T(8,128)S(1)}, f32[144,128]{1,0:T(8,128)S(1)}, u32[]{:S(2)}, u32[]{:S(2)}) %collective-permute-start.5) | collective-permute-done | bytes 73760 | tf_op jit(solution)/shard_map/ppermute | solution.py:342
  35.3 2.3 %first.1 = (f32[16,32,128]{2,1,0:T(8,128)S(1)}, f32[16,32,128]{2,1,0:T(8,128)S(1)}, f32[22,40,128]{2,1,0:T(8,128)S(1)}, f32[12,16,128]{2,1,0:T(8,128)S(1)}, f32[...) custom-call(f32[16,32,128]{2,1,0:T(8,128)S(1)} %get-tuple-element.31.refs_0_.b_ref, ...), custom_call_target="tpu_custom_call" | custom-call | tf_op jit(solution)/shard_map/first/pallas_call | solution.py:325
  37.6 7.6 %collective-permute-start.7 = (f32[128,128]{1,0:T(8,128)S(1)}, f32[128,128]{1,0:T(8,128)S(1)}, u32[]{:S(2)}, u32[]{:S(2)}) collective-permute-start(f32[128,128]{1,0:T(8,128)S(1)} %get-tuple-element.47), channel_id=1, source_target_pairs={{32,0},{64,32},{96,64},{128,96},{160,128},{192,160},{224,192},{256... | collective-permute-start | bytes 196616 | tf_op jit(solution)/shard_map/ppermute | solution.py:342
  45.2 0.0 collective-permute-start.6
  45.2 0.9 collective-permute-done.7.refs_3_
  46.1 0.4 collective-permute-done.6.refs_2_
  46.6 3.2 %collective-permute-start.8 = (f32[22,8,128]{2,1,0:T(8,128)S(1)}, f32[22,8,128]{2,1,0:T(8,128)S(1)}, u32[]{:S(2)}, u32[]{:S(2)}) collective-permute-start(f32[22,8,128]{2,1,0:T(8,128)S(1)} %get-tuple-element.48), channel_id=1, source_target_pairs={{0,4},{4,8},{8,12},{12,16},{16,20},{20,24},{24,28},{1,5},{5,9},{9,... | collective-permute-start | bytes 270344 | tf_op jit(solution)/shard_map/ppermute | solution.py:341
  49.8 1.3 %collective-permute-start.9 = (f32[22,8,128]{2,1,0:T(8,128)S(1)}, f32[22,8,128]{2,1,0:T(8,128)S(1)}, u32[]{:S(2)}, u32[]{:S(2)}) collective-permute-start(f32[22,8,128]{2,1,0:T(8,128)S(1)} %get-tuple-element.49), channel_id=1, source_target_pairs={{4,0},{8,4},{12,8},{16,12},{20,16},{24,20},{28,24},{5,1},{9,5},{13... | collective-permute-start | bytes 270344 | tf_op jit(solution)/shard_map/ppermute | solution.py:342
  51.1 0.2 collective-permute-done.8.refs_4_
  51.4 4.3 %collective-permute-done.9.refs_5_ = f32[22,8,128]{2,1,0:T(8,128)S(1)} collective-permute-done((f32[22,8,128]{2,1,0:T(8,128)S(1)}, f32[22,8,128]{2,1,0:T(8,128)S(1)}, u32[]{:S(2)}, u32[]{:S(2)}) %collective-permute-start.9) | collective-permute-done | bytes 90144 | tf_op jit(solution)/shard_map/ppermute | solution.py:342
  55.7 0.4 lanes.3
  56.1 3.1 %collective-permute-start.10 = (f32[72,128]{1,0:T(8,128)S(1)}, f32[72,128]{1,0:T(8,128)S(1)}, u32[]{:S(2)}, u32[]{:S(2)}) collective-permute-start(f32[72,128]{1,0:T(8,128)S(1)} %get-tuple-element.54), channel_id=1, source_target_pairs={{0,1},{1,2},{2,3},{4,5},{5,6},{6,7},{8,9},{9,10},{10,11},{12,13},{... | collective-permute-start | bytes 110600 | tf_op jit(solution)/shard_map/ppermute | solution.py:341
  59.2 1.3 %collective-permute-start.11 = (f32[72,128]{1,0:T(8,128)S(1)}, f32[72,128]{1,0:T(8,128)S(1)}, u32[]{:S(2)}, u32[]{:S(2)}) collective-permute-start(f32[72,128]{1,0:T(8,128)S(1)} %get-tuple-element.55), channel_id=1, source_target_pairs={{1,0},{2,1},{3,2},{5,4},{6,5},{7,6},{9,8},{10,9},{11,10},{13,12},{... | collective-permute-start | bytes 110600 | tf_op jit(solution)/shard_map/ppermute | solution.py:342
  60.5 0.0 collective-permute-done.10.before
  60.5 3.4 %collective-permute-done.11.after = f32[72,128]{1,0:T(8,128)S(1)} collective-permute-done((f32[72,128]{1,0:T(8,128)S(1)}, f32[72,128]{1,0:T(8,128)S(1)}, u32[]{:S(2)}, u32[]{:S(2)}) %collective-permute-start.11) | collective-permute-done | bytes 36896 | tf_op jit(solution)/shard_map/ppermute | solution.py:342
  63.9 2.0 %second.1 = (f32[16,32,128]{2,1,0:T(8,128)S(1)}, f32[16,32,128]{2,1,0:T(8,128)S(1)}, f32[1,128]{1,0:T(1,128)S(1)}) custom-call(f32[16,32,128]{2,1,0:T(8,128)S(1)} %get-tuple-element.31.refs_0_.b_ref, f32[16,32,128]{2,1,0:T(8,128)S(1)} %get-tuple-element.32.d_ref, f32[16,32,128]{2,1,0:T(8,128)S(1)} %get-tuple-element.44.p_ref, ...), custom_call_target="tpu_custom_call" | custom-call | tf_op jit(solution)/shard_map/second/pallas_call | solution.py:325
  66.0 16.1 %all_to_all.10 = f32[32,1,128]{2,1,0:T(1,128)S(1)} all-to-all(f32[32,1,128]{2,1,0:T(1,128)S(1)} %broadcast_in_dim.7), channel_id=1, replica_groups=mesh['gx'=24,'gy'=8,'gz'=4] {'gy','gz'}, dimensions={0} | all-to-all | bytes 32768 | tf_op jit(solution)/shard_map/all_to_all | solution.py:349
  82.1 19.6 %all_to_all.11 = f32[24,1,128]{2,1,0:T(1,128)S(1)} all-to-all(f32[24,1,128]{2,1,0:T(1,128)S(1)} %broadcast_in_dim.16), channel_id=1, replica_groups=mesh['gx'=24,'gy'=8,'gz'=4] {'gx'}, dimensions={0} | all-to-all | bytes 24576 | tf_op jit(solution)/shard_map/all_to_all | solution.py:349
  101.7 1.0 last.1
  (6 shorter events, 0.1 us)
Async XLA Ops:
  0.6 1.0 copy-start
  1.6 0.9 copy-start.1
  2.9 11.5 %collective-permute-start.1 = (f32[256,128]{1,0:T(8,128)S(1)}, f32[256,128]{1,0:T(8,128)S(1)}, u32[]{:S(2)}, u32[]{:S(2)}) collective-permute-start(f32[256,128]{1,0:T(8,128)S(1)} %get-tuple-element.35), channel_id=1, source_target_pairs={{32,0},{64,32},{96,64},{128,96},{160,128},{192,160},{224,192},{256... | collective-permute-start | bytes 393224 | tf_op jit(solution)/shard_map/ppermute | solution.py:342
  13.4 3.9 %collective-permute-start = (f32[256,128]{1,0:T(8,128)S(1)}, f32[256,128]{1,0:T(8,128)S(1)}, u32[]{:S(2)}, u32[]{:S(2)}) collective-permute-start(f32[256,128]{1,0:T(8,128)S(1)} %get-tuple-element.34.refs_2_), channel_id=1, source_target_pairs={{0,32},{32,64},{64,96},{96,128},{128,160},{160,192},{192,224},{224... | collective-permute-start | bytes 393224 | tf_op jit(solution)/shard_map/ppermute | solution.py:341
  17.4 5.2 %collective-permute-start.2 = (f32[34,8,128]{2,1,0:T(8,128)S(1)}, f32[34,8,128]{2,1,0:T(8,128)S(1)}, u32[]{:S(2)}, u32[]{:S(2)}) collective-permute-start(f32[34,8,128]{2,1,0:T(8,128)S(1)} %get-tuple-element.36), channel_id=1, source_target_pairs={{0,4},{4,8},{8,12},{12,16},{16,20},{20,24},{24,28},{1,5},{5,9},{9,... | collective-permute-start | bytes 417800 | tf_op jit(solution)/shard_map/ppermute | solution.py:341
  20.6 5.8 %collective-permute-start.3 = (f32[34,8,128]{2,1,0:T(8,128)S(1)}, f32[34,8,128]{2,1,0:T(8,128)S(1)}, u32[]{:S(2)}, u32[]{:S(2)}) collective-permute-start(f32[34,8,128]{2,1,0:T(8,128)S(1)} %get-tuple-element.37), channel_id=1, source_target_pairs={{4,0},{8,4},{12,8},{16,12},{20,16},{24,20},{28,24},{5,1},{9,5},{13... | collective-permute-start | bytes 417800 | tf_op jit(solution)/shard_map/ppermute | solution.py:342
  27.1 4.5 %collective-permute-start.4 = (f32[144,128]{1,0:T(8,128)S(1)}, f32[144,128]{1,0:T(8,128)S(1)}, u32[]{:S(2)}, u32[]{:S(2)}) collective-permute-start(f32[144,128]{1,0:T(8,128)S(1)} %get-tuple-element.42), channel_id=1, source_target_pairs={{0,1},{1,2},{2,3},{4,5},{5,6},{6,7},{8,9},{9,10},{10,11},{12,13},{... | collective-permute-start | bytes 221192 | tf_op jit(solution)/shard_map/ppermute | solution.py:341
  30.2 5.1 %collective-permute-start.5 = (f32[144,128]{1,0:T(8,128)S(1)}, f32[144,128]{1,0:T(8,128)S(1)}, u32[]{:S(2)}, u32[]{:S(2)}) collective-permute-start(f32[144,128]{1,0:T(8,128)S(1)} %get-tuple-element.43), channel_id=1, source_target_pairs={{1,0},{2,1},{3,2},{5,4},{6,5},{7,6},{9,8},{10,9},{11,10},{13,12},{... | collective-permute-start | bytes 221192 | tf_op jit(solution)/shard_map/ppermute | solution.py:342
  37.6 8.5 %collective-permute-start.7 = (f32[128,128]{1,0:T(8,128)S(1)}, f32[128,128]{1,0:T(8,128)S(1)}, u32[]{:S(2)}, u32[]{:S(2)}) collective-permute-start(f32[128,128]{1,0:T(8,128)S(1)} %get-tuple-element.47), channel_id=1, source_target_pairs={{32,0},{64,32},{96,64},{128,96},{160,128},{192,160},{224,192},{256... | collective-permute-start | bytes 196616 | tf_op jit(solution)/shard_map/ppermute | solution.py:342
  45.2 1.3 %collective-permute-start.6 = (f32[128,128]{1,0:T(8,128)S(1)}, f32[128,128]{1,0:T(8,128)S(1)}, u32[]{:S(2)}, u32[]{:S(2)}) collective-permute-start(f32[128,128]{1,0:T(8,128)S(1)} %get-tuple-element.46.refs_1_), channel_id=1, source_target_pairs={{0,32},{32,64},{64,96},{96,128},{128,160},{160,192},{192,224},{224... | collective-permute-start | bytes 196616 | tf_op jit(solution)/shard_map/ppermute | solution.py:341
  46.6 4.8 %collective-permute-start.8 = (f32[22,8,128]{2,1,0:T(8,128)S(1)}, f32[22,8,128]{2,1,0:T(8,128)S(1)}, u32[]{:S(2)}, u32[]{:S(2)}) collective-permute-start(f32[22,8,128]{2,1,0:T(8,128)S(1)} %get-tuple-element.48), channel_id=1, source_target_pairs={{0,4},{4,8},{8,12},{12,16},{16,20},{20,24},{24,28},{1,5},{5,9},{9,... | collective-permute-start | bytes 270344 | tf_op jit(solution)/shard_map/ppermute | solution.py:341
  49.8 5.9 %collective-permute-start.9 = (f32[22,8,128]{2,1,0:T(8,128)S(1)}, f32[22,8,128]{2,1,0:T(8,128)S(1)}, u32[]{:S(2)}, u32[]{:S(2)}) collective-permute-start(f32[22,8,128]{2,1,0:T(8,128)S(1)} %get-tuple-element.49), channel_id=1, source_target_pairs={{4,0},{8,4},{12,8},{16,12},{20,16},{24,20},{28,24},{5,1},{9,5},{13... | collective-permute-start | bytes 270344 | tf_op jit(solution)/shard_map/ppermute | solution.py:342
  56.1 4.4 %collective-permute-start.10 = (f32[72,128]{1,0:T(8,128)S(1)}, f32[72,128]{1,0:T(8,128)S(1)}, u32[]{:S(2)}, u32[]{:S(2)}) collective-permute-start(f32[72,128]{1,0:T(8,128)S(1)} %get-tuple-element.54), channel_id=1, source_target_pairs={{0,1},{1,2},{2,3},{4,5},{5,6},{6,7},{8,9},{9,10},{10,11},{12,13},{... | collective-permute-start | bytes 110600 | tf_op jit(solution)/shard_map/ppermute | solution.py:341
  59.2 4.7 %collective-permute-start.11 = (f32[72,128]{1,0:T(8,128)S(1)}, f32[72,128]{1,0:T(8,128)S(1)}, u32[]{:S(2)}, u32[]{:S(2)}) collective-permute-start(f32[72,128]{1,0:T(8,128)S(1)} %get-tuple-element.55), channel_id=1, source_target_pairs={{1,0},{2,1},{3,2},{5,4},{6,5},{7,6},{9,8},{10,9},{11,10},{13,12},{... | collective-permute-start | bytes 110600 | tf_op jit(solution)/shard_map/ppermute | solution.py:342

commit v3 on v2

v3 whole, which is shorter than its diff:
```python
import functools
import math

import jax
import jax.numpy as jnp
from jax import lax
from jax.experimental import pallas as pl
from jax.experimental.pallas import tpu as pltpu
from jax.sharding import PartitionSpec as P

ITERS = 2
FSWEEPS = 3
CSWEEPS = 4
COARSEN = 4
damping = 2.0 / 3.0
keep = 1.0 - damping

NX, NY, NZ = 16, 32, 128
HF = 3
HC = 4
DEEP = 20
DEEPC = 32
CX, CY = NX // COARSEN, NY // COARSEN
EX = NX + 2 * HF
EY = 40
EC = CX + 2 * HC
ER = CY + 2 * HC
FACE = HF * NY
PER = NZ // DEEP
TILES = -(-EX // PER)
VMEM = pl.BlockSpec(memory_space=pltpu.VMEM)
F32 = jnp.float32


def lanes(shape):
    return lax.broadcasted_iota(jnp.int32, shape, len(shape) - 1)


def roll(x, shift, axis=-1):
    axis = axis % x.ndim
    return pltpu.roll(x, shift % x.shape[axis], axis)


def group_sum(x):
    lane = lanes(x.shape)
    x = x + jnp.where(lane % 2 == 0, roll(x, -1), roll(x, 1))
    return x + jnp.where(lane % 4 < 2, roll(x, -2), roll(x, 2))


def block_sums(planes, tmp):
    tmp[...] = group_sum(planes[0] + planes[1] + planes[2] + planes[3])
    rows = [tmp[pl.ds(k, CY, stride=COARSEN), :] for k in range(COARSEN)]
    return rows[0] + rows[1] + rows[2] + rows[3]


def merge(planes):
    lane = lanes(planes[0].shape)
    out = planes[0]
    for c in range(1, 4):
        out = jnp.where(lane % 4 == c, planes[c], out)
    return out


def unmerge(tile, c):
    return group_sum(jnp.where(lanes(tile.shape) % 4 == c, tile, 0.0))


def edges(x, width):
    lane = lanes(x.shape)
    return jnp.where((lane < width) | (lane >= NZ - width), x, 0.0)


def inside():
    at = lax.axis_index("gx")
    return at > 0, at < lax.axis_size("gx") - 1


def layer(k, f, own, before, after):
    if HF <= k < HF + NX:
        return own[f][k - HF]
    ref, ok, k = (before, inside()[0], k) if k < HF else (after, inside()[1], k - HF - NX)
    return jnp.where(ok, ref[FACE * f + NY * k : FACE * f + NY * (k + 1)], 0.0)


def tile_of(group, at, mine, before, after):
    tile = (before, mine, after)[group][at : at + CY]
    return tile if group == 1 else jnp.where(inside()[group // 2], tile, 0.0)


def with_rows(tile, low, high):
    return jnp.concatenate([low[CY - HC :], tile, high[:HC]], axis=0)


def start_kernel(b_ref, d_ref, v_ref, up_ref, down_ref, tmp):
    for i in range(NX):
        v_ref[i] = damping / (6.0 + d_ref[i])
    g, vc = [], []
    for c in range(CX):
        g.append(block_sums([b_ref[COARSEN * c + k] for k in range(COARSEN)], tmp) * 0.25)
        cd = 6.0 + block_sums([d_ref[COARSEN * c + k] for k in range(COARSEN)], tmp) * 0.25
        vc.append(damping / cd)
    for ref in (up_ref, down_ref):
        for f, planes in enumerate((g, vc)):
            ref[2 * FACE + CY * f : 2 * FACE + CY * (f + 1)] = merge(planes)
    for k in range(HF):
        for f, ref in enumerate((b_ref, v_ref)):
            down_ref[FACE * f + NY * k : FACE * f + NY * (k + 1)] = ref[k]
            up_ref[FACE * f + NY * k : FACE * f + NY * (k + 1)] = ref[NX - HF + k]


def rows_kernel(b, v, mine, before, after, up_ref, down_ref):
    for k in range(EX):
        for f in range(2):
            plane = layer(k, f, (b, v), before, after)
            down_ref[k, HF * f : HF * (f + 1)] = plane[:HF]
            up_ref[k, HF * f : HF * (f + 1)] = plane[NY - HF :]
    for f in range(2):
        for group in range(3):
            tile = tile_of(group, 2 * FACE + CY * f, mine, before, after)
            down_ref[EX + 3 * f + group] = tile
            up_ref[EX + 3 * f + group] = tile


def lanes_kernel(b, v, mine, before, after, low, high, be, ve, ge, vce, up_ref, down_ref):
    lane = lanes((EY, NZ))
    for f, out in enumerate((be, ve)):
        for tile in range(TILES):
            up = jnp.zeros((EY, NZ), F32)
            down = jnp.zeros((EY, NZ), F32)
            for k in range(PER * tile, min(EX, PER * (tile + 1))):
                out[k, 0:8] = jnp.zeros((8, NZ), F32)
                out[k, EY - 8 : EY] = jnp.zeros((8, NZ), F32)
                out[k, 4 - HF : 4] = low[k, HF * f : HF * (f + 1)]
                out[k, 4 : 4 + NY] = layer(k, f, (b, v), before, after)
                out[k, 4 + NY : 4 + NY + HF] = high[k, HF * f : HF * (f + 1)]
                plane, place = out[k], DEEP * (k % PER)
                here = (lane >= place) & (lane < place + DEEP)
                up = jnp.where(here, roll(plane, place - (NZ - DEEP)), up)
                down = jnp.where(here, roll(plane, place), down)
            at = EY * (TILES * f + tile)
            up_ref[at : at + EY] = up
            down_ref[at : at + EY] = down
    lane = lanes((ER, NZ))
    for f, out in enumerate((ge, vce)):
        up = jnp.zeros((ER, NZ), F32)
        down = jnp.zeros((ER, NZ), F32)
        for group in range(3):
            at = EX + 3 * f + group
            tile = with_rows(tile_of(group, 2 * FACE + CY * f, mine, before, after), low[at], high[at])
            out[group] = tile
            here = lane // DEEPC == group
            up = jnp.where(here, roll(tile, DEEPC * (group + 1) - NZ), up)
            down = jnp.where(here, roll(tile, DEEPC * group), down)
        at = 2 * EY * TILES + ER * f
        up_ref[at : at + ER] = up
        down_ref[at : at + ER] = down


def beyond_fine(k, f, before, after):
    lane = lanes((EY, NZ))
    at, place = EY * (TILES * f + k // PER), DEEP * (k % PER)
    right = roll(after[at : at + EY], -place)
    left = roll(before[at : at + EY], NZ - DEEP - place)
    return jnp.where(lane < DEEP, right, jnp.where(lane >= NZ - DEEP, left, 0.0))


def beyond_coarse(group, f, before, after):
    lane = lanes((ER, NZ))
    at = 2 * EY * TILES + ER * f
    right = roll(after[at : at + ER], -DEEPC * group)
    left = roll(before[at : at + ER], NZ - DEEPC * (group + 1))
    return jnp.where(lane < DEEPC, right, jnp.where(lane >= NZ - DEEPC, left, 0.0))


def crossed(block, beyond, step):
    lane = lanes(block.shape)
    below, below_beyond = roll(block, step), roll(beyond, step)
    above, above_beyond = roll(block, -step), roll(beyond, -step)
    low, high = lane < step, lane >= NZ - step
    return (
        jnp.where(low, below_beyond, below) + jnp.where(high, above_beyond, above),
        jnp.where(low, below, below_beyond) + jnp.where(high, above, above_beyond),
    )


PAD = 8


def neighbours(src, k, rows, step=1):
    at = PAD
    here = [src[part, k, at : at + rows] for part in range(2)]
    along = crossed(here[0], here[1], step)
    out = []
    for part in range(2):
        beside = src[part, k - 1, at : at + rows] + src[part, k + 1, at : at + rows]
        beside = beside + (src[part, k, at - 1 : at - 1 + rows] + src[part, k, at + 1 : at + 1 + rows])
        out.append(beside + along[part])
    return here, out


def expand(coarse, part, k, lo):
    c = (k - HF) // COARSEN + HC
    first = lax.broadcasted_iota(jnp.int32, (8, NZ), 0) < 4
    groups = []
    for j in range(EY // 8):
        row = PAD + 3 + 2 * j
        a = jnp.broadcast_to(coarse[part, c, row : row + 1], (8, NZ))
        b = jnp.broadcast_to(coarse[part, c, row + 1 : row + 2], (8, NZ))
        groups.append(jnp.where(first, a, b))
    return jnp.concatenate(groups, axis=0)


def precondition(rhs, weight, crhs, cweight, fa, fb, ca, cb):
    for ref, rows in ((fa, EY), (fb, EY), (ca, ER), (cb, ER)):
        for part in range(2):
            for k in range(ref.shape[1]):
                ref[part, k, 0:PAD] = jnp.zeros((PAD, NZ), F32)
                ref[part, k, PAD + rows :] = jnp.zeros((PAD, NZ), F32)
    for k in range(EC):
        for part in range(2):
            ca[part, k, PAD : PAD + ER] = cweight[part, k] * crhs[part, k]
    src, dst = ca, cb
    for sweep in range(1, CSWEEPS):
        for k in range(sweep, EC - sweep):
            here, beside = neighbours(src, k, ER, COARSEN)
            for part in range(2):
                dst[part, k, PAD : PAD + ER] = keep * here[part] + cweight[part, k] * (crhs[part, k] + beside[part])
        src, dst = dst, src
    coarse = src
    for k in range(EX):
        for part in range(2):
            fa[part, k, PAD : PAD + EY] = weight[part][k] * rhs[part][k]
    src, dst = fa, fb
    for sweep in range(1, FSWEEPS):
        for k in range(sweep, EX - sweep):
            here, beside = neighbours(src, k, EY)
            for part in range(2):
                new = keep * here[part] + weight[part][k] * (rhs[part][k] + beside[part])
                if sweep == FSWEEPS - 1:
                    new = new + expand(coarse, part, k, 0)
                dst[part, k, PAD : PAD + EY] = new
        src, dst = dst, src


def image_plane(src, i):
    k, at = i + HF, PAD + 4
    here = [src[part, k, at : at + NY] for part in range(2)]
    along = crossed(here[0], here[1], 1)
    out = []
    for part in range(2):
        beside = src[part, k - 1, at : at + NY] + src[part, k + 1, at : at + NY]
        beside = beside + (src[part, k, at - 1 : at - 1 + NY] + src[part, k, at + 1 : at + 1 + NY])
        out.append(beside + along[part])
    return here, out


def add_up(x):
    return (x[0:8] + x[8:16]) + (x[16:24] + x[24:32])


SHARE = NZ // 8


def store_sums(out_ref, totals, row=None):
    row = jnp.zeros((1, NZ), F32) if row is None else row
    for i, part in totals.items():
        part = jnp.sum(part, axis=0, keepdims=True)
        for step in (64, 32, 16):
            part = part + roll(part, step)
        row = jnp.where(lanes((1, NZ)) // SHARE == i, part, row)
    out_ref[...] = row


NEAR = 4
NEARC = 16


def first_kernel(
    b_ref, d_ref, b, v, gm, vcm, before, after, p_ref, q_ref, qh_ref, vh_ref, vcx_ref, up_ref, down_ref, sum_ref,
    bh, gx, fa, fb, ca, cb, tmp,
):
    for k in range(EX):
        bh[k] = beyond_fine(k, 0, before, after)
        vh_ref[k] = beyond_fine(k, 1, before, after)
    for f, (tiles, out) in enumerate(((gm, gx), (vcm, vcx_ref))):
        for group in range(3):
            for part, tile in enumerate((tiles[group], beyond_coarse(group, f, before, after))):
                for c in range(4):
                    out[part, 4 * group + c] = unmerge(tile, c)
    precondition((b, bh), (v, vh_ref), gx, vcx_ref, fa, fb, ca, cb)
    rp = jnp.zeros((8, NZ), F32)
    pq = jnp.zeros((8, NZ), F32)
    for i in range(NX):
        (p, ph), (beside, beside_h) = image_plane(fa, i)
        q = (6.0 + d_ref[i]) * p - beside
        weight = vh_ref[i + HF, 4 : 4 + NY]
        within = weight > 0.0
        p_ref[i] = p
        q_ref[i] = q
        qh_ref[i] = jnp.where(within, damping / jnp.where(within, weight, 1.0) * ph - beside_h, 0.0)
        rp = rp + add_up(b_ref[i] * p)
        pq = pq + add_up(p * q)
    store_sums(sum_ref, {0: rp, 1: pq})
    for part, field in enumerate((q_ref, qh_ref)):
        means = [
            block_sums([field[COARSEN * c + k] for k in range(COARSEN)], tmp) * 0.25 for c in range(CX)
        ]
        tile = merge(means)
        if part == 1:
            tile = roll(tile, NEARC)
        for ref in (up_ref, down_ref):
            ref[FACE + NY + CY * part : FACE + NY + CY * (part + 1)] = tile
    lane = lanes((NY, NZ))
    for ref, first in ((down_ref, 0), (up_ref, NX - HF)):
        packed = jnp.zeros((NY, NZ), F32)
        for k in range(HF):
            ref[NY * k : NY * (k + 1)] = q_ref[first + k]
            packed = jnp.where(lane // (2 * NEAR) == k, roll(qh_ref[first + k], NEAR + 2 * NEAR * k), packed)
        ref[FACE : FACE + NY] = packed


def layer_beyond(k, own, before, after):
    if HF <= k < HF + NX:
        return own[k - HF]
    ref, ok, k = (before, inside()[0], k) if k < HF else (after, inside()[1], k - HF - NX)
    return jnp.where(ok, edges(roll(ref[FACE : FACE + NY], -NEAR - 2 * NEAR * k), NEAR), 0.0)


SIDE = NZ // (2 * NEAR)
PAIRS = EX // 2


def second_rows_kernel(q, qh, mine, before, after, up_ref, down_ref):
    for k in range(EX):
        plane = layer(k, 0, (q,), before, after)
        row = HF * (k % 2)
        down_ref[k // 2, row : row + HF] = plane[:HF]
        up_ref[k // 2, row : row + HF] = plane[NY - HF :]
    lane = lanes((8, NZ))
    wide = jnp.zeros((8, NZ), F32)
    for group in range(3):
        tile = tile_of(group, FACE + NY, mine, before, after)
        beyond = tile_of(group, FACE + NY + CY, mine, before, after)
        wide = jnp.where(lane // (2 * NEARC) == group, roll(beyond, 2 * NEARC * group), wide)
        for ref in (up_ref, down_ref):
            ref[PAIRS + group] = tile
    for ref, rows in ((up_ref, slice(NY - 8, NY)), (down_ref, slice(0, 8))):
        ref[PAIRS + 5] = wide
        for half in range(2):
            packed = jnp.zeros((8, NZ), F32)
            for k in range(SIDE * half, min(EX, SIDE * (half + 1))):
                plane = layer_beyond(k, qh, before, after)[rows]
                packed = jnp.where(lane // (2 * NEAR) == k % SIDE, roll(plane, NEAR + 2 * NEAR * (k % SIDE)), packed)
            ref[PAIRS + 3 + half] = packed


def second_kernel(
    b_ref, d_ref, p_ref, q_ref, qh_ref, v, vh_ref, vcx_ref, mine, before, after, low, high, first_ref,
    m_ref, im_ref, sum_ref, q, qh, gx, fa, fb, ca, cb,
):
    for k in range(EX):
        row, place = HF * (k % 2), -NEAR - 2 * NEAR * (k % SIDE)
        for out in (q, qh):
            out[k, 0:8] = jnp.zeros((8, NZ), F32)
            out[k, EY - 8 : EY] = jnp.zeros((8, NZ), F32)
        q[k, 4 - HF : 4] = low[k // 2, row : row + HF]
        q[k, 4 : 4 + NY] = layer(k, 0, (q_ref,), before, after)
        q[k, 4 + NY : 4 + NY + HF] = high[k // 2, row : row + HF]
        tile = PAIRS + 3 + k // SIDE
        qh[k, 4 - HF : 4] = edges(roll(low[tile], place), NEAR)[8 - HF :]
        qh[k, 4 : 4 + NY] = layer_beyond(k, qh_ref, before, after)
        qh[k, 4 + NY : 4 + NY + HF] = edges(roll(high[tile], place), NEAR)[:HF]
    for group in range(3):
        at = FACE + NY
        tile = with_rows(tile_of(group, at, mine, before, after), low[PAIRS + group], high[PAIRS + group])
        wide = [roll(ref[PAIRS + 5], -2 * NEARC * group) for ref in (low, high)]
        beyond = with_rows(tile_of(group, at + CY, mine, before, after), *wide)
        for part, merged in enumerate((tile, edges(roll(beyond, -NEARC), NEARC))):
            for c in range(4):
                gx[part, 4 * group + c] = unmerge(merged, c)
    precondition((q, qh), (v, vh_ref), gx, vcx_ref, fa, fb, ca, cb)
    sums = [jnp.zeros((8, NZ), F32)] * 4
    for i in range(NX):
        (m, _), (beside, _) = image_plane(fa, i)
        im = (6.0 + d_ref[i]) * m - beside
        m_ref[i] = m
        im_ref[i] = im
        pairs = ((q_ref[i], m), (b_ref[i], m), (p_ref[i], im), (m, im))
        sums = [s + add_up(x * y) for s, (x, y) in zip(sums, pairs)]
    store_sums(sum_ref, dict(enumerate(sums, 2)), first_ref[...])


def last_kernel(b_ref, p_ref, q_ref, m_ref, im_ref, sum_ref, x_ref, r_ref):
    rp, pq, qm, rm, pim, mim = [
        jnp.sum(jnp.where(lanes((1, NZ)) // SHARE == i, sum_ref[...], 0.0), axis=1, keepdims=True) for i in range(6)
    ]
    alpha = rp / pq
    rho = rp - alpha * (pq + rm) + alpha * alpha * qm
    scale = 1.0 + rho / rp
    alpha_next = rho / (scale * scale * pq - scale * alpha * (pim + qm) + alpha * alpha * mim)
    along = alpha + alpha_next * scale
    across = alpha_next * alpha
    for i in range(NX):
        x_ref[i] = along * p_ref[i] - across * m_ref[i]
        r_ref[i] = b_ref[i] - along * q_ref[i] + across * im_ref[i]


def call(kernel, outs, scratch=(), name=None, space=pltpu.VMEM):
    def run(*args):
        return pl.pallas_call(
            kernel,
            out_shape=[jax.ShapeDtypeStruct(shape, F32) for shape in outs],
            in_specs=[pl.BlockSpec(memory_space=space)] * len(args),
            out_specs=[VMEM] * len(outs),
            scratch_shapes=[pltpu.VMEM(shape, F32) if isinstance(shape, tuple) else shape for shape in scratch],
            compiler_params=pltpu.CompilerParams(vmem_limit_bytes=24 * 2**20),
            name=name,
        )(*args)

    return run


def both_ways(up, down, axis):
    count = lax.axis_size(axis)
    steps = [(i, (i + 1) % count) for i in range(count if axis == "gx" else count - 1)]
    before = lax.ppermute(up, axis, steps)
    after = lax.ppermute(down, axis, [(j, i) for i, j in steps])
    return before, after


def total(x, axis):
    count = math.prod(lax.axis_size(name) for name in axis)
    spread = jnp.broadcast_to(x[None], (count,) + x.shape)
    return jnp.sum(lax.all_to_all(spread, axis, 0, 0, tiled=True), axis=0)


def on_device(b, d):
    block, fine, coarse = (NX, NY, NZ), (EX, EY, NZ), (2, EC, ER, NZ)
    work = [(2, EX, EY + 2 * PAD, NZ)] * 2 + [(2, EC, ER + 2 * PAD, NZ)] * 2
    v, up, down = call(start_kernel, [block] + [(2 * FACE + 2 * CY, NZ)] * 2, [(NY, NZ)], name="start")(b, d)
    mine = up
    before, after = both_ways(up, down, "gx")
    up, down = call(rows_kernel, [(EX + 6, 8, NZ)] * 2, name="rows")(b, v, mine, before, after)
    low, high = both_ways(up, down, "gy")
    be, ve, gm, vcm, up, down = call(
        lanes_kernel, [fine] * 2 + [(3, ER, NZ)] * 2 + [(2 * (EY * TILES + ER), NZ)] * 2, name="lanes"
    )(b, v, mine, before, after, low, high)
    before, after = both_ways(up, down, "gz")
    p, q, qh, vh, vcx, up, down, sums = call(
        first_kernel,
        [block] * 3 + [fine, coarse] + [(FACE + NY + 2 * CY, NZ)] * 2 + [(1, NZ)],
        [fine, coarse] + work + [(NY, NZ)],
        name="first",
    )(b, d, be, ve, gm, vcm, before, after)
    mine = up
    before, after = both_ways(up, down, "gx")
    up, down = call(second_rows_kernel, [(PAIRS + 6, 8, NZ)] * 2, name="second_rows")(q, qh, mine, before, after)
    low, high = both_ways(up, down, "gy")
    m, im, sums = call(second_kernel, [block, block, (1, NZ)], [fine, fine, coarse] + work, name="second")(
        b, d, p, q, qh, ve, vh, vcx, mine, before, after, low, high, sums
    )
    for axis in (("gy", "gz"), ("gx",)):
        sums = total(sums, axis)
    return call(last_kernel, [block, block], name="last")(b, p, q, m, im, sums)


def solution(mesh):
    spec = P("gx", "gy", "gz")
    return jax.shard_map(on_device, mesh=mesh, in_specs=(spec, spec), out_specs=(spec, spec), check_vma=False)
```

time: 103 us -> 101 us (0.981)
  Pallas kernels: 6.73 us -> 11.5 us
  starting transfers between devices: 36 us -> 31.5 us
  waiting for transfers between devices: 21.6 us -> 18.9 us
    pallas_call x8 -> x7, Pallas kernels: 6.73 us -> 11.5 us  [run(): pl.pallas_call(kernel, out_shape=[jax.ShapeDtypeStruct(shape, F32) for sh...]
    ppermute x6 -> x5, waiting for transfers between devices: 17.1 us -> 13.9 us  [both_ways(): after = lax.ppermute(down, axis, [(j, i) for i, j in steps])]
    ppermute x6 -> x5, starting transfers between devices: 12.7 us -> 9.54 us  [both_ways(): before = lax.ppermute(up, axis, steps)]
    ppermute x6 -> x5, starting transfers between devices: 23.3 us -> 21.9 us  [both_ways(): after = lax.ppermute(down, axis, [(j, i) for i, j in steps])]
    ppermute x6 -> x5, waiting for transfers between devices: 4.42 us -> 4.94 us  [both_ways(): before = lax.ppermute(up, axis, steps)]
  transfers between devices with their start and end apart: 12 -> 10, of which waited for: 11 -> 9; matrix products, arithmetic and copies ran while one was open for 0% -> 0% of each run, Pallas kernels for 0% -> 0%
where the time goes in v3:
time: 101 us; the launch traced here: 100 us
  blocking collectives  35.7 us (35%)
  starting transfers between devices  31.5 us (31%)
  waiting for transfers between devices  18.9 us (19%)
  Pallas kernels  11.5 us (11%)
  local copies, waits for them, and re-layouts  1.93 us (2%)
    all_to_all x2, blocking collectives, total(): return jnp.sum(lax.all_to_all(spread, axis, 0, 0, tiled=True), axis=0)  35.7 us
    ppermute x5, starting transfers between devices, both_ways(): after = lax.ppermute(down, axis, [(j, i) for i, j in steps])  21.9 us
    ppermute x5, waiting for transfers between devices, both_ways(): after = lax.ppermute(down, axis, [(j, i) for i, j in steps])  13.9 us
    pallas_call x7, Pallas kernels, run(): pl.pallas_call(kernel, out_shape=[jax.ShapeDtypeStruct(shape, F32) for sh...  11.5 us
    ppermute x5, starting transfers between devices, both_ways(): before = lax.ppermute(up, axis, steps)  9.54 us
    ppermute x5, waiting for transfers between devices, both_ways(): before = lax.ppermute(up, axis, steps)  4.94 us
  transfers between devices with their start and end apart: 10, of which 9 were waited for; matrix products, arithmetic and copies ran while one was open for 0% of the time, Pallas kernels for 0%

profile of v3, /device:TPU:1, one launch (start us, length us, event | category | flops | bytes accessed | tf_op | source)
XLA Modules:
  0.0 100.2 jit_solution(12651547664732910735)
XLA Ops:
  0.6 0.0 copy-start
  0.6 0.9 copy-done
  1.6 0.0 copy-start.2
  1.6 0.9 copy-done.2
  2.5 0.2 start.1
  2.8 10.5 %collective-permute-start.1 = (f32[208,128]{1,0:T(8,128)S(1)}, f32[208,128]{1,0:T(8,128)S(1)}, u32[]{:S(2)}, u32[]{:S(2)}) collective-permute-start(f32[208,128]{1,0:T(8,128)S(1)} %get-tuple-element.28), channel_id=1, source_target_pairs={{32,0},{64,32},{96,64},{128,96},{160,128},{192,160},{224,192},{256... | collective-permute-start | bytes 319496 | tf_op jit(solution)/shard_map/ppermute | solution.py:427
  13.3 0.0 collective-permute-start
  13.3 1.0 collective-permute-done.1.after
  14.3 3.0 %collective-permute-done.before = f32[208,128]{1,0:T(8,128)S(1)} collective-permute-done((f32[208,128]{1,0:T(8,128)S(1)}, f32[208,128]{1,0:T(8,128)S(1)}, u32[]{:S(2)}, u32[]{:S(2)}) %collective-permute-start) | collective-permute-done | bytes 106528 | tf_op jit(solution)/shard_map/ppermute | solution.py:426
  17.3 3.2 %collective-permute-start.2 = (f32[28,8,128]{2,1,0:T(8,128)S(1)}, f32[28,8,128]{2,1,0:T(8,128)S(1)}, u32[]{:S(2)}, u32[]{:S(2)}) collective-permute-start(f32[28,8,128]{2,1,0:T(8,128)S(1)} %get-tuple-element.29), channel_id=1, source_target_pairs={{0,4},{4,8},{8,12},{12,16},{16,20},{20,24},{24,28},{1,5},{5,9},{9,... | collective-permute-start | bytes 344072 | tf_op jit(solution)/shard_map/ppermute | solution.py:426
  20.5 0.0 copy-start.3
  20.5 1.4 %collective-permute-start.3 = (f32[28,8,128]{2,1,0:T(8,128)S(1)}, f32[28,8,128]{2,1,0:T(8,128)S(1)}, u32[]{:S(2)}, u32[]{:S(2)}) collective-permute-start(f32[28,8,128]{2,1,0:T(8,128)S(1)} %get-tuple-element.30), channel_id=1, source_target_pairs={{4,0},{8,4},{12,8},{16,12},{20,16},{24,20},{28,24},{5,1},{9,5},{13... | collective-permute-start | bytes 344072 | tf_op jit(solution)/shard_map/ppermute | solution.py:427
  21.9 0.3 collective-permute-done.2.low
  22.2 3.9 %collective-permute-done.3.high = f32[28,8,128]{2,1,0:T(8,128)S(1)} collective-permute-done((f32[28,8,128]{2,1,0:T(8,128)S(1)}, f32[28,8,128]{2,1,0:T(8,128)S(1)}, u32[]{:S(2)}, u32[]{:S(2)}) %collective-permute-start.3) | collective-permute-done | bytes 114720 | tf_op jit(solution)/shard_map/ppermute | solution.py:427
  26.2 0.6 lanes.1
  26.7 3.1 %collective-permute-start.4 = (f32[352,128]{1,0:T(8,128)S(1)}, f32[352,128]{1,0:T(8,128)S(1)}, u32[]{:S(2)}, u32[]{:S(2)}) collective-permute-start(f32[352,128]{1,0:T(8,128)S(1)} %get-tuple-element.35), channel_id=1, source_target_pairs={{0,1},{1,2},{2,3},{4,5},{5,6},{6,7},{8,9},{9,10},{10,11},{12,13},{... | collective-permute-start | bytes 540680 | tf_op jit(solution)/shard_map/ppermute | solution.py:426
  29.9 1.3 %collective-permute-start.5 = (f32[352,128]{1,0:T(8,128)S(1)}, f32[352,128]{1,0:T(8,128)S(1)}, u32[]{:S(2)}, u32[]{:S(2)}) collective-permute-start(f32[352,128]{1,0:T(8,128)S(1)} %get-tuple-element.36), channel_id=1, source_target_pairs={{1,0},{2,1},{3,2},{5,4},{6,5},{7,6},{9,8},{10,9},{11,10},{13,12},{... | collective-permute-start | bytes 540680 | tf_op jit(solution)/shard_map/ppermute | solution.py:427
  31.2 1.1 %collective-permute-done.4.before = f32[352,128]{1,0:T(8,128)S(1)} collective-permute-done((f32[352,128]{1,0:T(8,128)S(1)}, f32[352,128]{1,0:T(8,128)S(1)}, u32[]{:S(2)}, u32[]{:S(2)}) %collective-permute-start.4) | collective-permute-done | bytes 180256 | tf_op jit(solution)/shard_map/ppermute | solution.py:426
  32.3 3.8 %collective-permute-done.5.after = f32[352,128]{1,0:T(8,128)S(1)} collective-permute-done((f32[352,128]{1,0:T(8,128)S(1)}, f32[352,128]{1,0:T(8,128)S(1)}, u32[]{:S(2)}, u32[]{:S(2)}) %collective-permute-start.5) | collective-permute-done | bytes 180256 | tf_op jit(solution)/shard_map/ppermute | solution.py:427
  36.1 0.0 copy-done.3
  36.1 6.2 %first.1 = (f32[16,32,128]{2,1,0:T(8,128)S(1)}, f32[16,32,128]{2,1,0:T(8,128)S(1)}, f32[16,32,128]{2,1,0:T(8,128)S(1)}, f32[22,40,128]{2,1,0:T(8,128)S(1)}, f32[...) custom-call(f32[16,32,128]{2,1,0:T(8,128)S(1)} %copy-done, ...), custom_call_target="tpu_custom_call" | custom-call | tf_op jit(solution)/shard_map/first/pallas_call | solution.py:410
  42.3 7.4 %collective-permute-start.7 = (f32[144,128]{1,0:T(8,128)S(1)}, f32[144,128]{1,0:T(8,128)S(1)}, u32[]{:S(2)}, u32[]{:S(2)}) collective-permute-start(f32[144,128]{1,0:T(8,128)S(1)} %get-tuple-element.43), channel_id=1, source_target_pairs={{32,0},{64,32},{96,64},{128,96},{160,128},{192,160},{224,192},{256... | collective-permute-start | bytes 221192 | tf_op jit(solution)/shard_map/ppermute | solution.py:427
  49.7 0.0 collective-permute-start.6
  49.7 0.9 collective-permute-done.7.after
  50.6 0.5 collective-permute-done.6.before
  51.1 0.0 copy-start.1
  51.1 0.2 second_rows.1
  51.3 3.2 %collective-permute-start.8 = (f32[17,8,128]{2,1,0:T(8,128)S(1)}, f32[17,8,128]{2,1,0:T(8,128)S(1)}, u32[]{:S(2)}, u32[]{:S(2)}) collective-permute-start(f32[17,8,128]{2,1,0:T(8,128)S(1)} %get-tuple-element.44), channel_id=1, source_target_pairs={{0,4},{4,8},{8,12},{12,16},{16,20},{20,24},{24,28},{1,5},{5,9},{9,... | collective-permute-start | bytes 208904 | tf_op jit(solution)/shard_map/ppermute | solution.py:426
  54.5 1.3 %collective-permute-start.9 = (f32[17,8,128]{2,1,0:T(8,128)S(1)}, f32[17,8,128]{2,1,0:T(8,128)S(1)}, u32[]{:S(2)}, u32[]{:S(2)}) collective-permute-start(f32[17,8,128]{2,1,0:T(8,128)S(1)} %get-tuple-element.45), channel_id=1, source_target_pairs={{4,0},{8,4},{12,8},{16,12},{20,16},{24,20},{28,24},{5,1},{9,5},{13... | collective-permute-start | bytes 208904 | tf_op jit(solution)/shard_map/ppermute | solution.py:427
  55.8 0.0 collective-permute-done.8.low
  55.9 4.3 %collective-permute-done.9.high = f32[17,8,128]{2,1,0:T(8,128)S(1)} collective-permute-done((f32[17,8,128]{2,1,0:T(8,128)S(1)}, f32[17,8,128]{2,1,0:T(8,128)S(1)}, u32[]{:S(2)}, u32[]{:S(2)}) %collective-permute-start.9) | collective-permute-done | bytes 69664 | tf_op jit(solution)/shard_map/ppermute | solution.py:427
  60.2 0.0 copy-done.1
  60.2 3.3 %second.1 = (f32[16,32,128]{2,1,0:T(8,128)S(1)}, f32[16,32,128]{2,1,0:T(8,128)S(1)}, f32[1,128]{1,0:T(1,128)S(1)}) custom-call(f32[16,32,128]{2,1,0:T(8,128)S(1)} %copy-done.1, f32[16,32,128]{2,1,0:T(8,128)S(1)} %copy-done.3, f32[16,32,128]{2,1,0:T(8,128)S(1)} %get-tuple-element.37.p_ref, f32[16,32,128]{2,1,0:T(8,128)S(1)} %get-tuple-element.38.q.q_ref, ...), custom_call_target="tpu_custom_call" | custom-call | tf_op jit(solution)/shard_map/second/pallas_call | solution.py:410
  63.5 17.3 %all_to_all.10 = f32[32,1,128]{2,1,0:T(1,128)S(1)} all-to-all(f32[32,1,128]{2,1,0:T(1,128)S(1)} %broadcast_in_dim.7), channel_id=1, replica_groups=mesh['gx'=24,'gy'=8,'gz'=4] {'gy','gz'}, dimensions={0} | all-to-all | bytes 32768 | tf_op jit(solution)/shard_map/all_to_all | solution.py:434
  80.8 18.4 %all_to_all.11 = f32[24,1,128]{2,1,0:T(1,128)S(1)} all-to-all(f32[24,1,128]{2,1,0:T(1,128)S(1)} %broadcast_in_dim.16), channel_id=1, replica_groups=mesh['gx'=24,'gy'=8,'gz'=4] {'gx'}, dimensions={0} | all-to-all | bytes 24576 | tf_op jit(solution)/shard_map/all_to_all | solution.py:434
  99.2 1.0 last.1
  (5 shorter events, 0.1 us)
Async XLA Ops:
  0.6 1.0 copy-start
  1.6 0.9 copy-start.2
  2.8 11.5 %collective-permute-start.1 = (f32[208,128]{1,0:T(8,128)S(1)}, f32[208,128]{1,0:T(8,128)S(1)}, u32[]{:S(2)}, u32[]{:S(2)}) collective-permute-start(f32[208,128]{1,0:T(8,128)S(1)} %get-tuple-element.28), channel_id=1, source_target_pairs={{32,0},{64,32},{96,64},{128,96},{160,128},{192,160},{224,192},{256... | collective-permute-start | bytes 319496 | tf_op jit(solution)/shard_map/ppermute | solution.py:427
  13.3 3.9 %collective-permute-start = (f32[208,128]{1,0:T(8,128)S(1)}, f32[208,128]{1,0:T(8,128)S(1)}, u32[]{:S(2)}, u32[]{:S(2)}) collective-permute-start(f32[208,128]{1,0:T(8,128)S(1)} %get-tuple-element.27.mine), channel_id=1, source_target_pairs={{0,32},{32,64},{64,96},{96,128},{128,160},{160,192},{192,224},{224... | collective-permute-start | bytes 319496 | tf_op jit(solution)/shard_map/ppermute | solution.py:426
  17.3 5.0 %collective-permute-start.2 = (f32[28,8,128]{2,1,0:T(8,128)S(1)}, f32[28,8,128]{2,1,0:T(8,128)S(1)}, u32[]{:S(2)}, u32[]{:S(2)}) collective-permute-start(f32[28,8,128]{2,1,0:T(8,128)S(1)} %get-tuple-element.29), channel_id=1, source_target_pairs={{0,4},{4,8},{8,12},{12,16},{16,20},{20,24},{24,28},{1,5},{5,9},{9,... | collective-permute-start | bytes 344072 | tf_op jit(solution)/shard_map/ppermute | solution.py:426
  20.5 15.6 %copy-start.3 = (f32[16,32,128]{2,1,0:T(8,128)S(1)}, f32[16,32,128]{2,1,0:T(8,128)}, u32[]{:S(2)}) copy-start(f32[16,32,128]{2,1,0:T(8,128)} %d_ref.5) | copy-start | bytes 786436
  20.5 5.7 %collective-permute-start.3 = (f32[28,8,128]{2,1,0:T(8,128)S(1)}, f32[28,8,128]{2,1,0:T(8,128)S(1)}, u32[]{:S(2)}, u32[]{:S(2)}) collective-permute-start(f32[28,8,128]{2,1,0:T(8,128)S(1)} %get-tuple-element.30), channel_id=1, source_target_pairs={{4,0},{8,4},{12,8},{16,12},{20,16},{24,20},{28,24},{5,1},{9,5},{13... | collective-permute-start | bytes 344072 | tf_op jit(solution)/shard_map/ppermute | solution.py:427
  26.7 5.5 %collective-permute-start.4 = (f32[352,128]{1,0:T(8,128)S(1)}, f32[352,128]{1,0:T(8,128)S(1)}, u32[]{:S(2)}, u32[]{:S(2)}) collective-permute-start(f32[352,128]{1,0:T(8,128)S(1)} %get-tuple-element.35), channel_id=1, source_target_pairs={{0,1},{1,2},{2,3},{4,5},{5,6},{6,7},{8,9},{9,10},{10,11},{12,13},{... | collective-permute-start | bytes 540680 | tf_op jit(solution)/shard_map/ppermute | solution.py:426
  29.9 6.2 %collective-permute-start.5 = (f32[352,128]{1,0:T(8,128)S(1)}, f32[352,128]{1,0:T(8,128)S(1)}, u32[]{:S(2)}, u32[]{:S(2)}) collective-permute-start(f32[352,128]{1,0:T(8,128)S(1)} %get-tuple-element.36), channel_id=1, source_target_pairs={{1,0},{2,1},{3,2},{5,4},{6,5},{7,6},{9,8},{10,9},{11,10},{13,12},{... | collective-permute-start | bytes 540680 | tf_op jit(solution)/shard_map/ppermute | solution.py:427
  42.3 8.3 %collective-permute-start.7 = (f32[144,128]{1,0:T(8,128)S(1)}, f32[144,128]{1,0:T(8,128)S(1)}, u32[]{:S(2)}, u32[]{:S(2)}) collective-permute-start(f32[144,128]{1,0:T(8,128)S(1)} %get-tuple-element.43), channel_id=1, source_target_pairs={{32,0},{64,32},{96,64},{128,96},{160,128},{192,160},{224,192},{256... | collective-permute-start | bytes 221192 | tf_op jit(solution)/shard_map/ppermute | solution.py:427
  49.7 1.4 %collective-permute-start.6 = (f32[144,128]{1,0:T(8,128)S(1)}, f32[144,128]{1,0:T(8,128)S(1)}, u32[]{:S(2)}, u32[]{:S(2)}) collective-permute-start(f32[144,128]{1,0:T(8,128)S(1)} %get-tuple-element.42.mine), channel_id=1, source_target_pairs={{0,32},{32,64},{64,96},{96,128},{128,160},{160,192},{192,224},{224... | collective-permute-start | bytes 221192 | tf_op jit(solution)/shard_map/ppermute | solution.py:426
  51.1 9.0 %copy-start.1 = (f32[16,32,128]{2,1,0:T(8,128)S(1)}, f32[16,32,128]{2,1,0:T(8,128)}, u32[]{:S(2)}) copy-start(f32[16,32,128]{2,1,0:T(8,128)} %b_ref.7) | copy-start | bytes 786436
  51.3 4.6 %collective-permute-start.8 = (f32[17,8,128]{2,1,0:T(8,128)S(1)}, f32[17,8,128]{2,1,0:T(8,128)S(1)}, u32[]{:S(2)}, u32[]{:S(2)}) collective-permute-start(f32[17,8,128]{2,1,0:T(8,128)S(1)} %get-tuple-element.44), channel_id=1, source_target_pairs={{0,4},{4,8},{8,12},{12,16},{16,20},{20,24},{24,28},{1,5},{5,9},{9,... | collective-permute-start | bytes 208904 | tf_op jit(solution)/shard_map/ppermute | solution.py:426
  54.5 5.7 %collective-permute-start.9 = (f32[17,8,128]{2,1,0:T(8,128)S(1)}, f32[17,8,128]{2,1,0:T(8,128)S(1)}, u32[]{:S(2)}, u32[]{:S(2)}) collective-permute-start(f32[17,8,128]{2,1,0:T(8,128)S(1)} %get-tuple-element.45), channel_id=1, source_target_pairs={{4,0},{8,4},{12,8},{16,12},{20,16},{24,20},{28,24},{5,1},{9,5},{13... | collective-permute-start | bytes 208904 | tf_op jit(solution)/shard_map/ppermute | solution.py:427

commit v4 on v3

--- a/solution.py
+++ b/solution.py
@@ -61,8 +61,16 @@
     return out
 
 
-def unmerge(tile, c):
-    return group_sum(jnp.where(lanes(tile.shape) % 4 == c, tile, 0.0))
+def unmerge(tile):
+    lane = lanes(tile.shape) % 4
+    moved = {step: roll(tile, -step) if step else tile for step in range(-3, 4)}
+    planes = []
+    for c in range(4):
+        out = moved[c]
+        for at in range(1, 4):
+            out = jnp.where(lane == at, moved[c - at], out)
+        planes.append(out)
+    return planes
 
 
 def edges(x, width):
@@ -91,7 +99,8 @@
     return jnp.concatenate([low[CY - HC :], tile, high[:HC]], axis=0)
 
 
-def start_kernel(b_ref, d_ref, v_ref, up_ref, down_ref, tmp):
+def start_kernel(bd_ref, v_ref, up_ref, down_ref, tmp):
+    b_ref, d_ref = bd_ref.at[0], bd_ref.at[1]
     for i in range(NX):
         v_ref[i] = damping / (6.0 + d_ref[i])
     g, vc = [], []
@@ -109,16 +118,28 @@
 
 
 def rows_kernel(b, v, mine, before, after, up_ref, down_ref):
-    for k in range(EX):
+    for k in range(1, EX - 1):
         for f in range(2):
             plane = layer(k, f, (b, v), before, after)
-            down_ref[k, HF * f : HF * (f + 1)] = plane[:HF]
-            up_ref[k, HF * f : HF * (f + 1)] = plane[NY - HF :]
+            down_ref[k - 1, HF * f : HF * (f + 1)] = plane[:HF]
+            up_ref[k - 1, HF * f : HF * (f + 1)] = plane[NY - HF :]
     for f in range(2):
         for group in range(3):
             tile = tile_of(group, 2 * FACE + CY * f, mine, before, after)
-            down_ref[EX + 3 * f + group] = tile
-            up_ref[EX + 3 * f + group] = tile
+            down_ref[EX - 2 + 3 * f + group] = tile
+            up_ref[EX - 2 + 3 * f + group] = tile
+
+
+def slots(lane, width, place):
+    first = (lane >= width * place) & (lane < width * (place + 1))
+    last = lane >= NZ - width if place == 0 else (lane >= width * (place - 1)) & (lane < width * place)
+    return first, last
+
+
+def unpack(before, after, width, place):
+    lane = lanes(after.shape)
+    both = jnp.where(slots(lane, width, place)[0], after, before)
+    return edges(roll(both, -width * place), width)
 
 
 def lanes_kernel(b, v, mine, before, after, low, high, be, ve, ge, vce, up_ref, down_ref):
@@ -130,13 +151,14 @@
             for k in range(PER * tile, min(EX, PER * (tile + 1))):
                 out[k, 0:8] = jnp.zeros((8, NZ), F32)
                 out[k, EY - 8 : EY] = jnp.zeros((8, NZ), F32)
-                out[k, 4 - HF : 4] = low[k, HF * f : HF * (f + 1)]
                 out[k, 4 : 4 + NY] = layer(k, f, (b, v), before, after)
-                out[k, 4 + NY : 4 + NY + HF] = high[k, HF * f : HF * (f + 1)]
-                plane, place = out[k], DEEP * (k % PER)
-                here = (lane >= place) & (lane < place + DEEP)
-                up = jnp.where(here, roll(plane, place - (NZ - DEEP)), up)
-                down = jnp.where(here, roll(plane, place), down)
+                if 0 < k < EX - 1:
+                    out[k, 4 - HF : 4] = low[k - 1, HF * f : HF * (f + 1)]
+                    out[k, 4 + NY : 4 + NY + HF] = high[k - 1, HF * f : HF * (f + 1)]
+                moved = roll(out[k], DEEP * (k % PER))
+                first, last = slots(lane, DEEP, k % PER)
+                up = jnp.where(last, moved, up)
+                down = jnp.where(first, moved, down)
             at = EY * (TILES * f + tile)
             up_ref[at : at + EY] = up
             down_ref[at : at + EY] = down
@@ -145,31 +167,26 @@
         up = jnp.zeros((ER, NZ), F32)
         down = jnp.zeros((ER, NZ), F32)
         for group in range(3):
-            at = EX + 3 * f + group
+            at = EX - 2 + 3 * f + group
             tile = with_rows(tile_of(group, 2 * FACE + CY * f, mine, before, after), low[at], high[at])
             out[group] = tile
-            here = lane // DEEPC == group
-            up = jnp.where(here, roll(tile, DEEPC * (group + 1) - NZ), up)
-            down = jnp.where(here, roll(tile, DEEPC * group), down)
+            moved = roll(tile, DEEPC * group)
+            first, last = slots(lane, DEEPC, group)
+            up = jnp.where(last, moved, up)
+            down = jnp.where(first, moved, down)
         at = 2 * EY * TILES + ER * f
         up_ref[at : at + ER] = up
         down_ref[at : at + ER] = down
 
 
 def beyond_fine(k, f, before, after):
-    lane = lanes((EY, NZ))
-    at, place = EY * (TILES * f + k // PER), DEEP * (k % PER)
-    right = roll(after[at : at + EY], -place)
-    left = roll(before[at : at + EY], NZ - DEEP - place)
-    return jnp.where(lane < DEEP, right, jnp.where(lane >= NZ - DEEP, left, 0.0))
+    at = EY * (TILES * f + k // PER)
+    return unpack(before[at : at + EY], after[at : at + EY], DEEP, k % PER)
 
 
 def beyond_coarse(group, f, before, after):
-    lane = lanes((ER, NZ))
     at = 2 * EY * TILES + ER * f
-    right = roll(after[at : at + ER], -DEEPC * group)
-    left = roll(before[at : at + ER], NZ - DEEPC * (group + 1))
-    return jnp.where(lane < DEEPC, right, jnp.where(lane >= NZ - DEEPC, left, 0.0))
+    return unpack(before[at : at + ER], after[at : at + ER], DEEPC, group)
 
 
 def crossed(block, beyond, step):
@@ -285,8 +302,8 @@
     for f, (tiles, out) in enumerate(((gm, gx), (vcm, vcx_ref))):
         for group in range(3):
             for part, tile in enumerate((tiles[group], beyond_coarse(group, f, before, after))):
-                for c in range(4):
-                    out[part, 4 * group + c] = unmerge(tile, c)
+                for c, plane in enumerate(unmerge(tile)):
+                    out[part, 4 * group + c] = plane
     precondition((b, bh), (v, vh_ref), gx, vcx_ref, fa, fb, ca, cb)
     rp = jnp.zeros((8, NZ), F32)
     pq = jnp.zeros((8, NZ), F32)
@@ -327,15 +344,15 @@
 
 
 SIDE = NZ // (2 * NEAR)
-PAIRS = EX // 2
+PAIRS = EX // 2 - 1
 
 
 def second_rows_kernel(q, qh, mine, before, after, up_ref, down_ref):
-    for k in range(EX):
+    for k in range(1, EX - 1):
         plane = layer(k, 0, (q,), before, after)
-        row = HF * (k % 2)
-        down_ref[k // 2, row : row + HF] = plane[:HF]
-        up_ref[k // 2, row : row + HF] = plane[NY - HF :]
+        at, row = (k - 1) // 2, HF * ((k - 1) % 2)
+        down_ref[at, row : row + HF] = plane[:HF]
+        up_ref[at, row : row + HF] = plane[NY - HF :]
     lane = lanes((8, NZ))
     wide = jnp.zeros((8, NZ), F32)
     for group in range(3):
@@ -359,13 +376,14 @@
     m_ref, im_ref, sum_ref, q, qh, gx, fa, fb, ca, cb,
 ):
     for k in range(EX):
-        row, place = HF * (k % 2), -NEAR - 2 * NEAR * (k % SIDE)
+        at, row, place = (k - 1) // 2, HF * ((k - 1) % 2), -NEAR - 2 * NEAR * (k % SIDE)
         for out in (q, qh):
             out[k, 0:8] = jnp.zeros((8, NZ), F32)
             out[k, EY - 8 : EY] = jnp.zeros((8, NZ), F32)
-        q[k, 4 - HF : 4] = low[k // 2, row : row + HF]
         q[k, 4 : 4 + NY] = layer(k, 0, (q_ref,), before, after)
-        q[k, 4 + NY : 4 + NY + HF] = high[k // 2, row : row + HF]
+        if 0 < k < EX - 1:
+            q[k, 4 - HF : 4] = low[at, row : row + HF]
+            q[k, 4 + NY : 4 + NY + HF] = high[at, row : row + HF]
         tile = PAIRS + 3 + k // SIDE
         qh[k, 4 - HF : 4] = edges(roll(low[tile], place), NEAR)[8 - HF :]
         qh[k, 4 : 4 + NY] = layer_beyond(k, qh_ref, before, after)
@@ -376,8 +394,8 @@
         wide = [roll(ref[PAIRS + 5], -2 * NEARC * group) for ref in (low, high)]
         beyond = with_rows(tile_of(group, at + CY, mine, before, after), *wide)
         for part, merged in enumerate((tile, edges(roll(beyond, -NEARC), NEARC))):
-            for c in range(4):
-                gx[part, 4 * group + c] = unmerge(merged, c)
+            for c, plane in enumerate(unmerge(merged)):
+                gx[part, 4 * group + c] = plane
     precondition((q, qh), (v, vh_ref), gx, vcx_ref, fa, fb, ca, cb)
     sums = [jnp.zeros((8, NZ), F32)] * 4
     for i in range(NX):
@@ -390,7 +408,10 @@
     store_sums(sum_ref, dict(enumerate(sums, 2)), first_ref[...])
 
 
-def last_kernel(b_ref, p_ref, q_ref, m_ref, im_ref, sum_ref, x_ref, r_ref):
+PARTS = 4
+
+
+def last_kernel(b_ref, p_ref, q_ref, m_ref, im_ref, sum_ref, x_out, r_out, x_ref, r_ref, sems):
     rp, pq, qm, rm, pim, mim = [
         jnp.sum(jnp.where(lanes((1, NZ)) // SHARE == i, sum_ref[...], 0.0), axis=1, keepdims=True) for i in range(6)
     ]
@@ -400,18 +421,27 @@
     alpha_next = rho / (scale * scale * pq - scale * alpha * (pim + qm) + alpha * alpha * mim)
     along = alpha + alpha_next * scale
     across = alpha_next * alpha
-    for i in range(NX):
-        x_ref[i] = along * p_ref[i] - across * m_ref[i]
-        r_ref[i] = b_ref[i] - along * q_ref[i] + across * im_ref[i]
-
-
-def call(kernel, outs, scratch=(), name=None, space=pltpu.VMEM):
+    copies = []
+    for part in range(PARTS):
+        planes = range(NX // PARTS * part, NX // PARTS * (part + 1))
+        for i in planes:
+            x_ref[i] = along * p_ref[i] - across * m_ref[i]
+            r_ref[i] = b_ref[i] - along * q_ref[i] + across * im_ref[i]
+        at = pl.ds(planes[0], len(planes))
+        for which, (src, dst) in enumerate(((x_ref, x_out), (r_ref, r_out))):
+            copies.append(pltpu.make_async_copy(src.at[at], dst.at[at], sems.at[2 * part + which]))
+            copies[-1].start()
+    for copy in copies:
+        copy.wait()
+
+
+def call(kernel, outs, scratch=(), name=None, out_space=pltpu.VMEM):
     def run(*args):
         return pl.pallas_call(
             kernel,
             out_shape=[jax.ShapeDtypeStruct(shape, F32) for shape in outs],
-            in_specs=[pl.BlockSpec(memory_space=space)] * len(args),
-            out_specs=[VMEM] * len(outs),
+            in_specs=[VMEM] * len(args),
+            out_specs=[pl.BlockSpec(memory_space=out_space)] * len(outs),
             scratch_shapes=[pltpu.VMEM(shape, F32) if isinstance(shape, tuple) else shape for shape in scratch],
             compiler_params=pltpu.CompilerParams(vmem_limit_bytes=24 * 2**20),
             name=name,
@@ -437,10 +467,11 @@
 def on_device(b, d):
     block, fine, coarse = (NX, NY, NZ), (EX, EY, NZ), (2, EC, ER, NZ)
     work = [(2, EX, EY + 2 * PAD, NZ)] * 2 + [(2, EC, ER + 2 * PAD, NZ)] * 2
-    v, up, down = call(start_kernel, [block] + [(2 * FACE + 2 * CY, NZ)] * 2, [(NY, NZ)], name="start")(b, d)
+    bd = lax.optimization_barrier(jnp.stack([b, d]))
+    v, up, down = call(start_kernel, [block] + [(2 * FACE + 2 * CY, NZ)] * 2, [(NY, NZ)], name="start")(bd)
     mine = up
     before, after = both_ways(up, down, "gx")
-    up, down = call(rows_kernel, [(EX + 6, 8, NZ)] * 2, name="rows")(b, v, mine, before, after)
+    up, down = call(rows_kernel, [(EX + 4, 8, NZ)] * 2, name="rows")(b, v, mine, before, after)
     low, high = both_ways(up, down, "gy")
     be, ve, gm, vcm, up, down = call(
         lanes_kernel, [fine] * 2 + [(3, ER, NZ)] * 2 + [(2 * (EY * TILES + ER), NZ)] * 2, name="lanes"
@@ -461,7 +492,13 @@
     )
     for axis in (("gy", "gz"), ("gx",)):
         sums = total(sums, axis)
-    return call(last_kernel, [block, block], name="last")(b, p, q, m, im, sums)
+    return call(
+        last_kernel,
+        [block, block],
+        [block, block, pltpu.SemaphoreType.DMA((2 * PARTS,))],
+        name="last",
+        out_space=pl.ANY,
+    )(b, p, q, m, im, sums)
 
 
 def solution(mesh):

time: 101 us -> 94.8 us (0.939)
  Pallas kernels: 11.5 us -> 6.64 us
  local copies, waits for them, and re-layouts: 1.93 us -> 0.04 us
  other arithmetic: 0.04 us -> 1.1 us
    pallas_call x7, Pallas kernels: 11.5 us -> 6.64 us  [run(): pl.pallas_call(kernel, out_shape=[jax.ShapeDtypeStruct(shape, F32) for sh...]
    unnamed x8 -> x4, local copies, waits for them, and re-layouts: 1.9 us -> 0.01 us
    another operation x0 -> x1, other arithmetic: none -> 1.07 us  [on_device(): bd = lax.optimization_barrier(jnp.stack([b, d]))]
where the time goes in v4:
time: 94.8 us; the launch traced here: 94.4 us
  blocking collectives  35.7 us (38%)
  starting transfers between devices  31.5 us (33%)
  waiting for transfers between devices  18.7 us (20%)
  Pallas kernels  6.64 us (7%)
  other arithmetic  1.1 us (1%)
    all_to_all x2, blocking collectives, total(): return jnp.sum(lax.all_to_all(spread, axis, 0, 0, tiled=True), axis=0)  35.7 us
    ppermute x5, starting transfers between devices, both_ways(): after = lax.ppermute(down, axis, [(j, i) for i, j in steps])  21.9 us
    ppermute x5, waiting for transfers between devices, both_ways(): after = lax.ppermute(down, axis, [(j, i) for i, j in steps])  13.9 us
    ppermute x5, starting transfers between devices, both_ways(): before = lax.ppermute(up, axis, steps)  9.54 us
    pallas_call x7, Pallas kernels, run(): pl.pallas_call(kernel, out_shape=[jax.ShapeDtypeStruct(shape, F32) for sh...  6.64 us
    ppermute x5, waiting for transfers between devices, both_ways(): before = lax.ppermute(up, axis, steps)  4.83 us
  transfers between devices with their start and end apart: 10, of which 9 were waited for; matrix products, arithmetic and copies ran while one was open for 0% of the time, Pallas kernels for 0%

profile of v4, /device:TPU:1, one launch (start us, length us, event | category | flops | bytes accessed | tf_op | source)
XLA Modules:
  0.0 94.4 jit_solution(11452142193026960205)
XLA Ops:
  0.6 1.1 %pad_maximum_fusion.bd_ref = f32[2,16,32,128]{3,2,1,0:T(8,128)S(1)} fusion(f32[1,16,32,128]{3,2,1,0:T(8,128)} %bitcast.7, f32[1,16,32,128]{3,2,1,0:T(8,128)} %bitcast.6), kind=kLoop, calls=%fused_computation | loop fusion | flops 131072 | bytes 1048576 | tf_op jit(solution)/shard_map/stack | solution.py:470
  1.7 0.0 copy-start
  1.7 0.2 start.1
  2.0 10.5 %collective-permute-start.1 = (f32[208,128]{1,0:T(8,128)S(1)}, f32[208,128]{1,0:T(8,128)S(1)}, u32[]{:S(2)}, u32[]{:S(2)}) collective-permute-start(f32[208,128]{1,0:T(8,128)S(1)} %get-tuple-element.28), channel_id=1, source_target_pairs={{32,0},{64,32},{96,64},{128,96},{160,128},{192,160},{224,192},{256... | collective-permute-start | bytes 319496 | tf_op jit(solution)/shard_map/ppermute | solution.py:457
  12.5 0.0 collective-permute-start
  12.5 1.0 %collective-permute-done.1.after = f32[208,128]{1,0:T(8,128)S(1)} collective-permute-done((f32[208,128]{1,0:T(8,128)S(1)}, f32[208,128]{1,0:T(8,128)S(1)}, u32[]{:S(2)}, u32[]{:S(2)}) %collective-permute-start.1) | collective-permute-done | bytes 106528 | tf_op jit(solution)/shard_map/ppermute | solution.py:457
  13.4 3.0 %collective-permute-done.before = f32[208,128]{1,0:T(8,128)S(1)} collective-permute-done((f32[208,128]{1,0:T(8,128)S(1)}, f32[208,128]{1,0:T(8,128)S(1)}, u32[]{:S(2)}, u32[]{:S(2)}) %collective-permute-start) | collective-permute-done | bytes 106528 | tf_op jit(solution)/shard_map/ppermute | solution.py:456
  16.4 0.0 copy-done
  16.4 3.2 %collective-permute-start.2 = (f32[26,8,128]{2,1,0:T(8,128)S(1)}, f32[26,8,128]{2,1,0:T(8,128)S(1)}, u32[]{:S(2)}, u32[]{:S(2)}) collective-permute-start(f32[26,8,128]{2,1,0:T(8,128)S(1)} %get-tuple-element.29), channel_id=1, source_target_pairs={{0,4},{4,8},{8,12},{12,16},{16,20},{20,24},{24,28},{1,5},{5,9},{9,... | collective-permute-start | bytes 319496 | tf_op jit(solution)/shard_map/ppermute | solution.py:456
  19.7 0.0 copy-start.1
  19.7 1.4 %collective-permute-start.3 = (f32[26,8,128]{2,1,0:T(8,128)S(1)}, f32[26,8,128]{2,1,0:T(8,128)S(1)}, u32[]{:S(2)}, u32[]{:S(2)}) collective-permute-start(f32[26,8,128]{2,1,0:T(8,128)S(1)} %get-tuple-element.30), channel_id=1, source_target_pairs={{4,0},{8,4},{12,8},{16,12},{20,16},{24,20},{28,24},{5,1},{9,5},{13... | collective-permute-start | bytes 319496 | tf_op jit(solution)/shard_map/ppermute | solution.py:457
  21.1 0.2 collective-permute-done.2.low
  21.3 3.9 %collective-permute-done.3.high = f32[26,8,128]{2,1,0:T(8,128)S(1)} collective-permute-done((f32[26,8,128]{2,1,0:T(8,128)S(1)}, f32[26,8,128]{2,1,0:T(8,128)S(1)}, u32[]{:S(2)}, u32[]{:S(2)}) %collective-permute-start.3) | collective-permute-done | bytes 106528 | tf_op jit(solution)/shard_map/ppermute | solution.py:457
  25.2 0.3 lanes.1
  25.6 3.1 %collective-permute-start.4 = (f32[352,128]{1,0:T(8,128)S(1)}, f32[352,128]{1,0:T(8,128)S(1)}, u32[]{:S(2)}, u32[]{:S(2)}) collective-permute-start(f32[352,128]{1,0:T(8,128)S(1)} %get-tuple-element.35), channel_id=1, source_target_pairs={{0,1},{1,2},{2,3},{4,5},{5,6},{6,7},{8,9},{9,10},{10,11},{12,13},{... | collective-permute-start | bytes 540680 | tf_op jit(solution)/shard_map/ppermute | solution.py:456
  28.7 1.3 %collective-permute-start.5 = (f32[352,128]{1,0:T(8,128)S(1)}, f32[352,128]{1,0:T(8,128)S(1)}, u32[]{:S(2)}, u32[]{:S(2)}) collective-permute-start(f32[352,128]{1,0:T(8,128)S(1)} %get-tuple-element.36), channel_id=1, source_target_pairs={{1,0},{2,1},{3,2},{5,4},{6,5},{7,6},{9,8},{10,9},{11,10},{13,12},{... | collective-permute-start | bytes 540680 | tf_op jit(solution)/shard_map/ppermute | solution.py:457
  30.0 1.1 %collective-permute-done.4.before = f32[352,128]{1,0:T(8,128)S(1)} collective-permute-done((f32[352,128]{1,0:T(8,128)S(1)}, f32[352,128]{1,0:T(8,128)S(1)}, u32[]{:S(2)}, u32[]{:S(2)}) %collective-permute-start.4) | collective-permute-done | bytes 180256 | tf_op jit(solution)/shard_map/ppermute | solution.py:456
  31.1 3.8 %collective-permute-done.5.after = f32[352,128]{1,0:T(8,128)S(1)} collective-permute-done((f32[352,128]{1,0:T(8,128)S(1)}, f32[352,128]{1,0:T(8,128)S(1)}, u32[]{:S(2)}, u32[]{:S(2)}) %collective-permute-start.5) | collective-permute-done | bytes 180256 | tf_op jit(solution)/shard_map/ppermute | solution.py:457
  34.9 0.0 copy-done.1
  35.0 2.7 %first.1 = (f32[16,32,128]{2,1,0:T(8,128)S(1)}, f32[16,32,128]{2,1,0:T(8,128)S(1)}, f32[16,32,128]{2,1,0:T(8,128)S(1)}, f32[22,40,128]{2,1,0:T(8,128)S(1)}, f32[...) custom-call(f32[16,32,128]{2,1,0:T(8,128)S(1)} %copy-done, ...), custom_call_target="tpu_custom_call" | custom-call | tf_op jit(solution)/shard_map/first/pallas_call | solution.py:440
  37.7 7.4 %collective-permute-start.7 = (f32[144,128]{1,0:T(8,128)S(1)}, f32[144,128]{1,0:T(8,128)S(1)}, u32[]{:S(2)}, u32[]{:S(2)}) collective-permute-start(f32[144,128]{1,0:T(8,128)S(1)} %get-tuple-element.43), channel_id=1, source_target_pairs={{32,0},{64,32},{96,64},{128,96},{160,128},{192,160},{224,192},{256... | collective-permute-start | bytes 221192 | tf_op jit(solution)/shard_map/ppermute | solution.py:457
  45.1 0.0 collective-permute-start.6
  45.1 0.9 collective-permute-done.7.after
  46.0 0.5 collective-permute-done.6.before
  46.5 0.2 second_rows.1
  46.6 3.2 %collective-permute-start.8 = (f32[16,8,128]{2,1,0:T(8,128)S(1)}, f32[16,8,128]{2,1,0:T(8,128)S(1)}, u32[]{:S(2)}, u32[]{:S(2)}) collective-permute-start(f32[16,8,128]{2,1,0:T(8,128)S(1)} %get-tuple-element.44), channel_id=1, source_target_pairs={{0,4},{4,8},{8,12},{12,16},{16,20},{20,24},{24,28},{1,5},{5,9},{9,... | collective-permute-start | bytes 196616 | tf_op jit(solution)/shard_map/ppermute | solution.py:456
  49.8 1.3 %collective-permute-start.9 = (f32[16,8,128]{2,1,0:T(8,128)S(1)}, f32[16,8,128]{2,1,0:T(8,128)S(1)}, u32[]{:S(2)}, u32[]{:S(2)}) collective-permute-start(f32[16,8,128]{2,1,0:T(8,128)S(1)} %get-tuple-element.45), channel_id=1, source_target_pairs={{4,0},{8,4},{12,8},{16,12},{20,16},{24,20},{28,24},{5,1},{9,5},{13... | collective-permute-start | bytes 196616 | tf_op jit(solution)/shard_map/ppermute | solution.py:457
  51.1 0.0 collective-permute-done.8.low
  51.2 4.3 %collective-permute-done.9.high = f32[16,8,128]{2,1,0:T(8,128)S(1)} collective-permute-done((f32[16,8,128]{2,1,0:T(8,128)S(1)}, f32[16,8,128]{2,1,0:T(8,128)S(1)}, u32[]{:S(2)}, u32[]{:S(2)}) %collective-permute-start.9) | collective-permute-done | bytes 65568 | tf_op jit(solution)/shard_map/ppermute | solution.py:457
  55.5 2.2 %second.1 = (f32[16,32,128]{2,1,0:T(8,128)S(1)}, f32[16,32,128]{2,1,0:T(8,128)S(1)}, f32[1,128]{1,0:T(1,128)S(1)}) custom-call(f32[16,32,128]{2,1,0:T(8,128)S(1)} %copy-done, f32[16,32,128]{2,1,0:T(8,128)S(1)} %copy-done.1, f32[16,32,128]{2,1,0:T(8,128)S(1)} %get-tuple-element.37.p_ref, f32[16,32,128]{2,1,0:T(8,128)S(1)} %get-tuple-element.38.q.q_ref, ...), custom_call_target="tpu_custom_call" | custom-call | tf_op jit(solution)/shard_map/second/pallas_call | solution.py:440
  57.7 17.3 %all_to_all.10 = f32[32,1,128]{2,1,0:T(1,128)S(1)} all-to-all(f32[32,1,128]{2,1,0:T(1,128)S(1)} %broadcast_in_dim.7), channel_id=1, replica_groups=mesh['gx'=24,'gy'=8,'gz'=4] {'gy','gz'}, dimensions={0} | all-to-all | bytes 32768 | tf_op jit(solution)/shard_map/all_to_all | solution.py:464
  75.0 18.4 %all_to_all.11 = f32[24,1,128]{2,1,0:T(1,128)S(1)} all-to-all(f32[24,1,128]{2,1,0:T(1,128)S(1)} %broadcast_in_dim.16), channel_id=1, replica_groups=mesh['gx'=24,'gy'=8,'gz'=4] {'gx'}, dimensions={0} | all-to-all | bytes 24576 | tf_op jit(solution)/shard_map/all_to_all | solution.py:464
  93.5 1.0 %last.1 = (f32[16,32,128]{2,1,0:T(8,128)}, f32[16,32,128]{2,1,0:T(8,128)}) custom-call(f32[16,32,128]{2,1,0:T(8,128)S(1)} %copy-done, f32[16,32,128]{2,1,0:T(8,128)S(1)} %get-tuple-element.37.p_ref, f32[16,32,128]{2,1,0:T(8,128)S(1)} %get-tuple-element.38.q.q_ref, f32[16,32,128]{2,1,0:T(8,128)S(1)} %get-tuple-element.47.m_ref, ...), custom_call_target="tpu_custom_call" | custom-call | tf_op jit(solution)/shard_map/last/pallas_call | solution.py:440
  (5 shorter events, 0.1 us)
Async XLA Ops:
  1.7 14.7 %copy-start = (f32[16,32,128]{2,1,0:T(8,128)S(1)}, f32[16,32,128]{2,1,0:T(8,128)}, u32[]{:S(2)}) copy-start(f32[16,32,128]{2,1,0:T(8,128)} %b_ref.5) | copy-start | bytes 786436
  2.0 11.5 %collective-permute-start.1 = (f32[208,128]{1,0:T(8,128)S(1)}, f32[208,128]{1,0:T(8,128)S(1)}, u32[]{:S(2)}, u32[]{:S(2)}) collective-permute-start(f32[208,128]{1,0:T(8,128)S(1)} %get-tuple-element.28), channel_id=1, source_target_pairs={{32,0},{64,32},{96,64},{128,96},{160,128},{192,160},{224,192},{256... | collective-permute-start | bytes 319496 | tf_op jit(solution)/shard_map/ppermute | solution.py:457
  12.5 3.9 %collective-permute-start = (f32[208,128]{1,0:T(8,128)S(1)}, f32[208,128]{1,0:T(8,128)S(1)}, u32[]{:S(2)}, u32[]{:S(2)}) collective-permute-start(f32[208,128]{1,0:T(8,128)S(1)} %get-tuple-element.27.mine), channel_id=1, source_target_pairs={{0,32},{32,64},{64,96},{96,128},{128,160},{160,192},{192,224},{224... | collective-permute-start | bytes 319496 | tf_op jit(solution)/shard_map/ppermute | solution.py:456
  16.4 4.9 %collective-permute-start.2 = (f32[26,8,128]{2,1,0:T(8,128)S(1)}, f32[26,8,128]{2,1,0:T(8,128)S(1)}, u32[]{:S(2)}, u32[]{:S(2)}) collective-permute-start(f32[26,8,128]{2,1,0:T(8,128)S(1)} %get-tuple-element.29), channel_id=1, source_target_pairs={{0,4},{4,8},{8,12},{12,16},{16,20},{20,24},{24,28},{1,5},{5,9},{9,... | collective-permute-start | bytes 319496 | tf_op jit(solution)/shard_map/ppermute | solution.py:456
  19.7 15.3 %copy-start.1 = (f32[16,32,128]{2,1,0:T(8,128)S(1)}, f32[16,32,128]{2,1,0:T(8,128)}, u32[]{:S(2)}) copy-start(f32[16,32,128]{2,1,0:T(8,128)} %d_ref.3) | copy-start | bytes 786436
  19.7 5.6 %collective-permute-start.3 = (f32[26,8,128]{2,1,0:T(8,128)S(1)}, f32[26,8,128]{2,1,0:T(8,128)S(1)}, u32[]{:S(2)}, u32[]{:S(2)}) collective-permute-start(f32[26,8,128]{2,1,0:T(8,128)S(1)} %get-tuple-element.30), channel_id=1, source_target_pairs={{4,0},{8,4},{12,8},{16,12},{20,16},{24,20},{28,24},{5,1},{9,5},{13... | collective-permute-start | bytes 319496 | tf_op jit(solution)/shard_map/ppermute | solution.py:457
  25.6 5.5 %collective-permute-start.4 = (f32[352,128]{1,0:T(8,128)S(1)}, f32[352,128]{1,0:T(8,128)S(1)}, u32[]{:S(2)}, u32[]{:S(2)}) collective-permute-start(f32[352,128]{1,0:T(8,128)S(1)} %get-tuple-element.35), channel_id=1, source_target_pairs={{0,1},{1,2},{2,3},{4,5},{5,6},{6,7},{8,9},{9,10},{10,11},{12,13},{... | collective-permute-start | bytes 540680 | tf_op jit(solution)/shard_map/ppermute | solution.py:456
  28.7 6.2 %collective-permute-start.5 = (f32[352,128]{1,0:T(8,128)S(1)}, f32[352,128]{1,0:T(8,128)S(1)}, u32[]{:S(2)}, u32[]{:S(2)}) collective-permute-start(f32[352,128]{1,0:T(8,128)S(1)} %get-tuple-element.36), channel_id=1, source_target_pairs={{1,0},{2,1},{3,2},{5,4},{6,5},{7,6},{9,8},{10,9},{11,10},{13,12},{... | collective-permute-start | bytes 540680 | tf_op jit(solution)/shard_map/ppermute | solution.py:457
  37.7 8.3 %collective-permute-start.7 = (f32[144,128]{1,0:T(8,128)S(1)}, f32[144,128]{1,0:T(8,128)S(1)}, u32[]{:S(2)}, u32[]{:S(2)}) collective-permute-start(f32[144,128]{1,0:T(8,128)S(1)} %get-tuple-element.43), channel_id=1, source_target_pairs={{32,0},{64,32},{96,64},{128,96},{160,128},{192,160},{224,192},{256... | collective-permute-start | bytes 221192 | tf_op jit(solution)/shard_map/ppermute | solution.py:457
  45.1 1.4 %collective-permute-start.6 = (f32[144,128]{1,0:T(8,128)S(1)}, f32[144,128]{1,0:T(8,128)S(1)}, u32[]{:S(2)}, u32[]{:S(2)}) collective-permute-start(f32[144,128]{1,0:T(8,128)S(1)} %get-tuple-element.42.mine), channel_id=1, source_target_pairs={{0,32},{32,64},{64,96},{96,128},{128,160},{160,192},{192,224},{224... | collective-permute-start | bytes 221192 | tf_op jit(solution)/shard_map/ppermute | solution.py:456
  46.6 4.5 %collective-permute-start.8 = (f32[16,8,128]{2,1,0:T(8,128)S(1)}, f32[16,8,128]{2,1,0:T(8,128)S(1)}, u32[]{:S(2)}, u32[]{:S(2)}) collective-permute-start(f32[16,8,128]{2,1,0:T(8,128)S(1)} %get-tuple-element.44), channel_id=1, source_target_pairs={{0,4},{4,8},{8,12},{12,16},{16,20},{20,24},{24,28},{1,5},{5,9},{9,... | collective-permute-start | bytes 196616 | tf_op jit(solution)/shard_map/ppermute | solution.py:456
  49.8 5.6 %collective-permute-start.9 = (f32[16,8,128]{2,1,0:T(8,128)S(1)}, f32[16,8,128]{2,1,0:T(8,128)S(1)}, u32[]{:S(2)}, u32[]{:S(2)}) collective-permute-start(f32[16,8,128]{2,1,0:T(8,128)S(1)} %get-tuple-element.45), channel_id=1, source_target_pairs={{4,0},{8,4},{12,8},{16,12},{20,16},{24,20},{28,24},{5,1},{9,5},{13... | collective-permute-start | bytes 196616 | tf_op jit(solution)/shard_map/ppermute | solution.py:457

commit v5 on v4

--- a/solution.py
+++ b/solution.py
@@ -452,10 +452,14 @@
 
 def both_ways(up, down, axis):
     count = lax.axis_size(axis)
-    steps = [(i, (i + 1) % count) for i in range(count if axis == "gx" else count - 1)]
-    before = lax.ppermute(up, axis, steps)
-    after = lax.ppermute(down, axis, [(j, i) for i, j in steps])
-    return before, after
+    if axis == "gx":
+        steps = [(i, (i + 1) % count) for i in range(count)]
+        return lax.ppermute(up, axis, steps), lax.ppermute(down, axis, [(j, i) for i, j in steps])
+    even = lax.axis_index(axis) % 2 == 0
+    one = lax.ppermute(jnp.where(even, up, down), axis, [(i, i ^ 1) for i in range(count) if i ^ 1 < count])
+    swaps = [(i, i + 1) for i in range(1, count - 1, 2)]
+    two = lax.ppermute(jnp.where(even, down, up), axis, swaps + [(j, i) for i, j in swaps])
+    return jnp.where(even, two, one), jnp.where(even, one, two)
 
 
 def total(x, axis):

time: 94.8 us -> 95.1 us (level)
  waiting for transfers between devices: 18.7 us -> 10.1 us
  blocking collectives: 35.7 us -> 43.9 us
    ppermute x10, waiting for transfers between devices: 18.7 us -> 10.1 us  [the longest x3 4.8 us: both_ways(): lax.ppermute(jnp.where(even, up, down), axis, [(i, i ^ 1) for i in range(...]
    all_to_all x2, blocking collectives: 35.7 us -> 43.9 us  [total(): return jnp.sum(lax.all_to_all(spread, axis, 0, 0, tiled=True), axis=0)]
  transfers between devices with their start and end apart: 10 -> 10, of which waited for: 9 -> 7; matrix products, arithmetic and copies ran while one was open for 0% -> 0% of each run, Pallas kernels for 0% -> 0%
where the time goes in v5:
time: 95.1 us; the launch traced here: 94.8 us
  blocking collectives  43.9 us (46%)
  starting transfers between devices  32.1 us (34%)
  waiting for transfers between devices  10.1 us (11%)
  Pallas kernels  6.59 us (7%)
  other arithmetic  1.22 us (1%)
    all_to_all x2, blocking collectives, total(): return jnp.sum(lax.all_to_all(spread, axis, 0, 0, tiled=True), axis=0)  43.9 us
    ppermute x2, starting transfers between devices, both_ways(): lax.ppermute(down, axis, [(j, i) for i, j in steps])  17.4 us
    ppermute x3, starting transfers between devices, both_ways(): lax.ppermute(jnp.where(even, up, down), axis, [(i, i ^ 1) for i in range(...  12.6 us
    pallas_call x7, Pallas kernels, run(): pl.pallas_call(kernel, out_shape=[jax.ShapeDtypeStruct(shape, F32) for sh...  6.59 us
    ppermute x3, waiting for transfers between devices, both_ways(): lax.ppermute(jnp.where(even, up, down), axis, [(i, i ^ 1) for i in range(...  4.8 us
    ppermute x2, waiting for transfers between devices, both_ways(): lax.ppermute(up, axis, steps)  3.45 us
    ppermute x3, starting transfers between devices, both_ways(): lax.ppermute(jnp.where(even, down, up), axis, swaps + [(j, i) for i, j in...  2.14 us
  transfers between devices with their start and end apart: 10, of which 7 were waited for; matrix products, arithmetic and copies ran while one was open for 0% of the time, Pallas kernels for 0%

profile of v5, /device:TPU:1, one launch (start us, length us, event | category | flops | bytes accessed | tf_op | source)
XLA Modules:
  0.0 94.8 jit_solution(6400917237484522188)
XLA Ops:
  0.6 1.1 %pad_maximum_fusion.bd_ref = f32[2,16,32,128]{3,2,1,0:T(8,128)S(1)} fusion(f32[1,16,32,128]{3,2,1,0:T(8,128)} %bitcast.7, f32[1,16,32,128]{3,2,1,0:T(8,128)} %bitcast.6), kind=kLoop, calls=%fused_computation | loop fusion | flops 131072 | bytes 1048576 | tf_op jit(solution)/shard_map/stack | solution.py:474
  1.7 0.0 copy-start
  1.7 0.2 start.1
  2.0 10.5 %collective-permute-start.1 = (f32[208,128]{1,0:T(8,128)S(1)}, f32[208,128]{1,0:T(8,128)S(1)}, u32[]{:S(2)}, u32[]{:S(2)}) collective-permute-start(f32[208,128]{1,0:T(8,128)S(1)} %get-tuple-element.28), channel_id=1, source_target_pairs={{32,0},{64,32},{96,64},{128,96},{160,128},{192,160},{224,192},{256... | collective-permute-start | bytes 319496 | tf_op jit(solution)/shard_map/ppermute | solution.py:457
  12.5 0.0 collective-permute-start
  12.5 1.0 %collective-permute-done.1.after = f32[208,128]{1,0:T(8,128)S(1)} collective-permute-done((f32[208,128]{1,0:T(8,128)S(1)}, f32[208,128]{1,0:T(8,128)S(1)}, u32[]{:S(2)}, u32[]{:S(2)}) %collective-permute-start.1) | collective-permute-done | bytes 106528 | tf_op jit(solution)/shard_map/ppermute | solution.py:457
  13.4 3.0 %collective-permute-done.before = f32[208,128]{1,0:T(8,128)S(1)} collective-permute-done((f32[208,128]{1,0:T(8,128)S(1)}, f32[208,128]{1,0:T(8,128)S(1)}, u32[]{:S(2)}, u32[]{:S(2)}) %collective-permute-start) | collective-permute-done | bytes 106528 | tf_op jit(solution)/shard_map/ppermute | solution.py:457
  16.4 0.0 copy-done
  16.5 3.2 %collective-permute-start.3 = (f32[26,8,128]{2,1,0:T(8,128)S(1)}, f32[26,8,128]{2,1,0:T(8,128)S(1)}, u32[]{:S(2)}, u32[]{:S(2)}) collective-permute-start(f32[26,8,128]{2,1,0:T(8,128)S(1)} %get-tuple-element.56), channel_id=1, source_target_pairs={{0,4},{4,0},{8,12},{12,8},{16,20},{20,16},{24,28},{28,24},{1,5},{5... | collective-permute-start | bytes 319496 | tf_op jit(solution)/shard_map/ppermute | solution.py:459
  19.7 0.7 collective-permute-start.2
  20.4 1.5 %collective-permute-done.3 = f32[26,8,128]{2,1,0:T(8,128)S(1)} collective-permute-done((f32[26,8,128]{2,1,0:T(8,128)S(1)}, f32[26,8,128]{2,1,0:T(8,128)S(1)}, u32[]{:S(2)}, u32[]{:S(2)}) %collective-permute-start.3) | collective-permute-done | bytes 106528 | tf_op jit(solution)/shard_map/ppermute | solution.py:459
  21.9 0.0 collective-permute-done.2
  21.9 0.3 lanes.1
  22.3 3.1 %collective-permute-start.5 = (f32[352,128]{1,0:T(8,128)S(1)}, f32[352,128]{1,0:T(8,128)S(1)}, u32[]{:S(2)}, u32[]{:S(2)}) collective-permute-start(f32[352,128]{1,0:T(8,128)S(1)} %get-tuple-element.52), channel_id=1, source_target_pairs={{0,1},{1,0},{2,3},{3,2},{4,5},{5,4},{6,7},{7,6},{8,9},{9,8},{10,11... | collective-permute-start | bytes 540680 | tf_op jit(solution)/shard_map/ppermute | solution.py:459
  25.4 0.0 copy-start.1
  25.4 0.8 collective-permute-start.4
  26.2 2.3 %collective-permute-done.5 = f32[352,128]{1,0:T(8,128)S(1)} collective-permute-done((f32[352,128]{1,0:T(8,128)S(1)}, f32[352,128]{1,0:T(8,128)S(1)}, u32[]{:S(2)}, u32[]{:S(2)}) %collective-permute-start.5) | collective-permute-done | bytes 180256 | tf_op jit(solution)/shard_map/ppermute | solution.py:459
  28.5 0.0 collective-permute-done.4
  28.6 0.0 copy-done.1
  28.6 2.7 %first.1 = (f32[16,32,128]{2,1,0:T(8,128)S(1)}, f32[16,32,128]{2,1,0:T(8,128)S(1)}, f32[16,32,128]{2,1,0:T(8,128)S(1)}, f32[22,40,128]{2,1,0:T(8,128)S(1)}, f32[...) custom-call(f32[16,32,128]{2,1,0:T(8,128)S(1)} %copy-done, ...), custom_call_target="tpu_custom_call" | custom-call | tf_op jit(solution)/shard_map/first/pallas_call | solution.py:440
  31.3 6.8 %collective-permute-start.7 = (f32[144,128]{1,0:T(8,128)S(1)}, f32[144,128]{1,0:T(8,128)S(1)}, u32[]{:S(2)}, u32[]{:S(2)}) collective-permute-start(f32[144,128]{1,0:T(8,128)S(1)} %get-tuple-element.43), channel_id=1, source_target_pairs={{32,0},{64,32},{96,64},{128,96},{160,128},{192,160},{224,192},{256... | collective-permute-start | bytes 221192 | tf_op jit(solution)/shard_map/ppermute | solution.py:457
  38.1 0.0 collective-permute-start.6
  38.1 0.9 collective-permute-done.7.after
  39.0 0.5 collective-permute-done.6.before
  39.5 0.2 second_rows.1
  39.7 6.3 %collective-permute-start.9 = (f32[16,8,128]{2,1,0:T(8,128)S(1)}, f32[16,8,128]{2,1,0:T(8,128)S(1)}, u32[]{:S(2)}, u32[]{:S(2)}) collective-permute-start(f32[16,8,128]{2,1,0:T(8,128)S(1)} %get-tuple-element.60), channel_id=1, source_target_pairs={{0,4},{4,0},{8,12},{12,8},{16,20},{20,16},{24,28},{28,24},{1,5},{5... | collective-permute-start | bytes 196616 | tf_op jit(solution)/shard_map/ppermute | solution.py:459
  46.0 0.7 collective-permute-start.8
  46.6 1.0 %collective-permute-done.9 = f32[16,8,128]{2,1,0:T(8,128)S(1)} collective-permute-done((f32[16,8,128]{2,1,0:T(8,128)S(1)}, f32[16,8,128]{2,1,0:T(8,128)S(1)}, u32[]{:S(2)}, u32[]{:S(2)}) %collective-permute-start.9) | collective-permute-done | bytes 65568 | tf_op jit(solution)/shard_map/ppermute | solution.py:459
  47.6 0.0 collective-permute-done.8
  47.6 2.2 %second.1 = (f32[16,32,128]{2,1,0:T(8,128)S(1)}, f32[16,32,128]{2,1,0:T(8,128)S(1)}, f32[1,128]{1,0:T(1,128)S(1)}) custom-call(f32[16,32,128]{2,1,0:T(8,128)S(1)} %copy-done, f32[16,32,128]{2,1,0:T(8,128)S(1)} %copy-done.1, f32[16,32,128]{2,1,0:T(8,128)S(1)} %get-tuple-element.37.p_ref, f32[16,32,128]{2,1,0:T(8,128)S(1)} %get-tuple-element.38.q.q_ref, ...), custom_call_target="tpu_custom_call" | custom-call | tf_op jit(solution)/shard_map/second/pallas_call | solution.py:440
  49.8 25.3 %all_to_all.10 = f32[32,1,128]{2,1,0:T(1,128)S(1)} all-to-all(f32[32,1,128]{2,1,0:T(1,128)S(1)} %broadcast_in_dim.7), channel_id=1, replica_groups=mesh['gx'=24,'gy'=8,'gz'=4] {'gy','gz'}, dimensions={0} | all-to-all | bytes 32768 | tf_op jit(solution)/shard_map/all_to_all | solution.py:468
  75.2 18.6 %all_to_all.11 = f32[24,1,128]{2,1,0:T(1,128)S(1)} all-to-all(f32[24,1,128]{2,1,0:T(1,128)S(1)} %broadcast_in_dim.16), channel_id=1, replica_groups=mesh['gx'=24,'gy'=8,'gz'=4] {'gx'}, dimensions={0} | all-to-all | bytes 24576 | tf_op jit(solution)/shard_map/all_to_all | solution.py:468
  93.8 1.0 %last.1 = (f32[16,32,128]{2,1,0:T(8,128)}, f32[16,32,128]{2,1,0:T(8,128)}) custom-call(f32[16,32,128]{2,1,0:T(8,128)S(1)} %copy-done, f32[16,32,128]{2,1,0:T(8,128)S(1)} %get-tuple-element.37.p_ref, f32[16,32,128]{2,1,0:T(8,128)S(1)} %get-tuple-element.38.q.q_ref, f32[16,32,128]{2,1,0:T(8,128)S(1)} %get-tuple-element.47.m_ref, ...), custom_call_target="tpu_custom_call" | custom-call | tf_op jit(solution)/shard_map/last/pallas_call | solution.py:440
  (11 shorter events, 0.2 us)
Async XLA Ops:
  1.7 14.7 %copy-start = (f32[16,32,128]{2,1,0:T(8,128)S(1)}, f32[16,32,128]{2,1,0:T(8,128)}, u32[]{:S(2)}) copy-start(f32[16,32,128]{2,1,0:T(8,128)} %b_ref.5) | copy-start | bytes 786436
  2.0 11.5 %collective-permute-start.1 = (f32[208,128]{1,0:T(8,128)S(1)}, f32[208,128]{1,0:T(8,128)S(1)}, u32[]{:S(2)}, u32[]{:S(2)}) collective-permute-start(f32[208,128]{1,0:T(8,128)S(1)} %get-tuple-element.28), channel_id=1, source_target_pairs={{32,0},{64,32},{96,64},{128,96},{160,128},{192,160},{224,192},{256... | collective-permute-start | bytes 319496 | tf_op jit(solution)/shard_map/ppermute | solution.py:457
  12.5 3.9 %collective-permute-start = (f32[208,128]{1,0:T(8,128)S(1)}, f32[208,128]{1,0:T(8,128)S(1)}, u32[]{:S(2)}, u32[]{:S(2)}) collective-permute-start(f32[208,128]{1,0:T(8,128)S(1)} %get-tuple-element.27.mine), channel_id=1, source_target_pairs={{0,32},{32,64},{64,96},{96,128},{128,160},{160,192},{192,224},{224... | collective-permute-start | bytes 319496 | tf_op jit(solution)/shard_map/ppermute | solution.py:457
  16.5 5.4 %collective-permute-start.3 = (f32[26,8,128]{2,1,0:T(8,128)S(1)}, f32[26,8,128]{2,1,0:T(8,128)S(1)}, u32[]{:S(2)}, u32[]{:S(2)}) collective-permute-start(f32[26,8,128]{2,1,0:T(8,128)S(1)} %get-tuple-element.56), channel_id=1, source_target_pairs={{0,4},{4,0},{8,12},{12,8},{16,20},{20,16},{24,28},{28,24},{1,5},{5... | collective-permute-start | bytes 319496 | tf_op jit(solution)/shard_map/ppermute | solution.py:459
  19.7 2.2 %collective-permute-start.2 = (f32[26,8,128]{2,1,0:T(8,128)S(1)}, f32[26,8,128]{2,1,0:T(8,128)S(1)}, u32[]{:S(2)}, u32[]{:S(2)}) collective-permute-start(f32[26,8,128]{2,1,0:T(8,128)S(1)} %get-tuple-element.57), channel_id=1, source_target_pairs={{4,8},{12,16},{20,24},{8,4},{16,12},{24,20},{5,9},{13,17},{21,25},... | collective-permute-start | bytes 319496 | tf_op jit(solution)/shard_map/ppermute | solution.py:461
  22.3 6.2 %collective-permute-start.5 = (f32[352,128]{1,0:T(8,128)S(1)}, f32[352,128]{1,0:T(8,128)S(1)}, u32[]{:S(2)}, u32[]{:S(2)}) collective-permute-start(f32[352,128]{1,0:T(8,128)S(1)} %get-tuple-element.52), channel_id=1, source_target_pairs={{0,1},{1,0},{2,3},{3,2},{4,5},{5,4},{6,7},{7,6},{8,9},{9,8},{10,11... | collective-permute-start | bytes 540680 | tf_op jit(solution)/shard_map/ppermute | solution.py:459
  25.4 3.1 %copy-start.1 = (f32[16,32,128]{2,1,0:T(8,128)S(1)}, f32[16,32,128]{2,1,0:T(8,128)}, u32[]{:S(2)}) copy-start(f32[16,32,128]{2,1,0:T(8,128)} %d_ref.3) | copy-start | bytes 786436
  25.4 3.1 %collective-permute-start.4 = (f32[352,128]{1,0:T(8,128)S(1)}, f32[352,128]{1,0:T(8,128)S(1)}, u32[]{:S(2)}, u32[]{:S(2)}) collective-permute-start(f32[352,128]{1,0:T(8,128)S(1)} %get-tuple-element.53), channel_id=1, source_target_pairs={{1,2},{2,1},{5,6},{6,5},{9,10},{10,9},{13,14},{14,13},{17,18},{18,... | collective-permute-start | bytes 540680 | tf_op jit(solution)/shard_map/ppermute | solution.py:461
  31.3 7.8 %collective-permute-start.7 = (f32[144,128]{1,0:T(8,128)S(1)}, f32[144,128]{1,0:T(8,128)S(1)}, u32[]{:S(2)}, u32[]{:S(2)}) collective-permute-start(f32[144,128]{1,0:T(8,128)S(1)} %get-tuple-element.43), channel_id=1, source_target_pairs={{32,0},{64,32},{96,64},{128,96},{160,128},{192,160},{224,192},{256... | collective-permute-start | bytes 221192 | tf_op jit(solution)/shard_map/ppermute | solution.py:457
  38.1 1.4 %collective-permute-start.6 = (f32[144,128]{1,0:T(8,128)S(1)}, f32[144,128]{1,0:T(8,128)S(1)}, u32[]{:S(2)}, u32[]{:S(2)}) collective-permute-start(f32[144,128]{1,0:T(8,128)S(1)} %get-tuple-element.42.mine), channel_id=1, source_target_pairs={{0,32},{32,64},{64,96},{96,128},{128,160},{160,192},{192,224},{224... | collective-permute-start | bytes 221192 | tf_op jit(solution)/shard_map/ppermute | solution.py:457
  39.7 7.9 %collective-permute-start.9 = (f32[16,8,128]{2,1,0:T(8,128)S(1)}, f32[16,8,128]{2,1,0:T(8,128)S(1)}, u32[]{:S(2)}, u32[]{:S(2)}) collective-permute-start(f32[16,8,128]{2,1,0:T(8,128)S(1)} %get-tuple-element.60), channel_id=1, source_target_pairs={{0,4},{4,0},{8,12},{12,8},{16,20},{20,16},{24,28},{28,24},{1,5},{5... | collective-permute-start | bytes 196616 | tf_op jit(solution)/shard_map/ppermute | solution.py:459
  46.0 1.6 %collective-permute-start.8 = (f32[16,8,128]{2,1,0:T(8,128)S(1)}, f32[16,8,128]{2,1,0:T(8,128)S(1)}, u32[]{:S(2)}, u32[]{:S(2)}) collective-permute-start(f32[16,8,128]{2,1,0:T(8,128)S(1)} %get-tuple-element.61), channel_id=1, source_target_pairs={{4,8},{12,16},{20,24},{8,4},{16,12},{24,20},{5,9},{13,17},{21,25},... | collective-permute-start | bytes 196616 | tf_op jit(solution)/shard_map/ppermute | solution.py:461

commit v6 on v4

--- a/solution.py
+++ b/solution.py
@@ -26,8 +26,11 @@
 EC = CX + 2 * HC
 ER = CY + 2 * HC
 FACE = HF * NY
+COARSE = FACE + (HF - 1) * NY
 PER = NZ // DEEP
-TILES = -(-EX // PER)
+PLACES = [(0, k) for k in range(EX)] + [(1, k) for k in range(1, EX - 1)]
+TILES = -(-len(PLACES) // PER)
+ROWS = HF * (EX - 2)
 VMEM = pl.BlockSpec(memory_space=pltpu.VMEM)
 F32 = jnp.float32
 
@@ -86,7 +89,7 @@
 def layer(k, f, own, before, after):
     if HF <= k < HF + NX:
         return own[f][k - HF]
-    ref, ok, k = (before, inside()[0], k) if k < HF else (after, inside()[1], k - HF - NX)
+    ref, ok, k = (before, inside()[0], k - f) if k < HF else (after, inside()[1], k - HF - NX)
     return jnp.where(ok, ref[FACE * f + NY * k : FACE * f + NY * (k + 1)], 0.0)
 
 
@@ -96,7 +99,7 @@
 
 
 def with_rows(tile, low, high):
-    return jnp.concatenate([low[CY - HC :], tile, high[:HC]], axis=0)
+    return jnp.concatenate([low, tile, high], axis=0)
 
 
 def start_kernel(bd_ref, v_ref, up_ref, down_ref, tmp):
@@ -110,24 +113,29 @@
         vc.append(damping / cd)
     for ref in (up_ref, down_ref):
         for f, planes in enumerate((g, vc)):
-            ref[2 * FACE + CY * f : 2 * FACE + CY * (f + 1)] = merge(planes)
+            ref[COARSE + CY * f : COARSE + CY * (f + 1)] = merge(planes)
     for k in range(HF):
-        for f, ref in enumerate((b_ref, v_ref)):
-            down_ref[FACE * f + NY * k : FACE * f + NY * (k + 1)] = ref[k]
-            up_ref[FACE * f + NY * k : FACE * f + NY * (k + 1)] = ref[NX - HF + k]
+        for ref, plane, far in ((down_ref, k, HF - 1), (up_ref, NX - HF + k, 0)):
+            value, weight = b_ref[plane], v_ref[plane]
+            ref[NY * k : NY * (k + 1)] = weight * value if k == far else value
+            if k != far:
+                at = FACE + NY * (k if ref is down_ref else k - 1)
+                ref[at : at + NY] = weight
 
 
 def rows_kernel(b, v, mine, before, after, up_ref, down_ref):
     for k in range(1, EX - 1):
         for f in range(2):
             plane = layer(k, f, (b, v), before, after)
-            down_ref[k - 1, HF * f : HF * (f + 1)] = plane[:HF]
-            up_ref[k - 1, HF * f : HF * (f + 1)] = plane[NY - HF :]
+            at = ROWS * f + HF * (k - 1)
+            down_ref[at : at + HF] = plane[:HF]
+            up_ref[at : at + HF] = plane[NY - HF :]
     for f in range(2):
         for group in range(3):
-            tile = tile_of(group, 2 * FACE + CY * f, mine, before, after)
-            down_ref[EX - 2 + 3 * f + group] = tile
-            up_ref[EX - 2 + 3 * f + group] = tile
+            tile = tile_of(group, COARSE + CY * f, mine, before, after)
+            at = 2 * ROWS + HC * (3 * f + group)
+            down_ref[at : at + HC] = tile[:HC]
+            up_ref[at : at + HC] = tile[CY - HC :]
 
 
 def slots(lane, width, place):
@@ -143,49 +151,51 @@
 
 
 def lanes_kernel(b, v, mine, before, after, low, high, be, ve, ge, vce, up_ref, down_ref):
+    for f, k in PLACES:
+        out = (be, ve)[f]
+        out[k, 0:8] = jnp.zeros((8, NZ), F32)
+        out[k, EY - 8 : EY] = jnp.zeros((8, NZ), F32)
+        out[k, 4 : 4 + NY] = layer(k, f, (b, v), before, after)
+        if 0 < k < EX - 1:
+            at = ROWS * f + HF * (k - 1)
+            out[k, 4 - HF : 4] = low[at : at + HF]
+            out[k, 4 + NY : 4 + NY + HF] = high[at : at + HF]
     lane = lanes((EY, NZ))
-    for f, out in enumerate((be, ve)):
-        for tile in range(TILES):
-            up = jnp.zeros((EY, NZ), F32)
-            down = jnp.zeros((EY, NZ), F32)
-            for k in range(PER * tile, min(EX, PER * (tile + 1))):
-                out[k, 0:8] = jnp.zeros((8, NZ), F32)
-                out[k, EY - 8 : EY] = jnp.zeros((8, NZ), F32)
-                out[k, 4 : 4 + NY] = layer(k, f, (b, v), before, after)
-                if 0 < k < EX - 1:
-                    out[k, 4 - HF : 4] = low[k - 1, HF * f : HF * (f + 1)]
-                    out[k, 4 + NY : 4 + NY + HF] = high[k - 1, HF * f : HF * (f + 1)]
-                moved = roll(out[k], DEEP * (k % PER))
-                first, last = slots(lane, DEEP, k % PER)
-                up = jnp.where(last, moved, up)
-                down = jnp.where(first, moved, down)
-            at = EY * (TILES * f + tile)
-            up_ref[at : at + EY] = up
-            down_ref[at : at + EY] = down
+    for tile in range(TILES):
+        up = jnp.zeros((EY, NZ), F32)
+        down = jnp.zeros((EY, NZ), F32)
+        for place, (f, k) in enumerate(PLACES[PER * tile : PER * (tile + 1)]):
+            moved = roll((be, ve)[f][k], DEEP * place)
+            first, last = slots(lane, DEEP, place)
+            up = jnp.where(last, moved, up)
+            down = jnp.where(first, moved, down)
+        up_ref[EY * tile : EY * (tile + 1)] = up
+        down_ref[EY * tile : EY * (tile + 1)] = down
     lane = lanes((ER, NZ))
     for f, out in enumerate((ge, vce)):
         up = jnp.zeros((ER, NZ), F32)
         down = jnp.zeros((ER, NZ), F32)
         for group in range(3):
-            at = EX - 2 + 3 * f + group
-            tile = with_rows(tile_of(group, 2 * FACE + CY * f, mine, before, after), low[at], high[at])
+            at = 2 * ROWS + HC * (3 * f + group)
+            tile = tile_of(group, COARSE + CY * f, mine, before, after)
+            tile = with_rows(tile, low[at : at + HC], high[at : at + HC])
             out[group] = tile
             moved = roll(tile, DEEPC * group)
             first, last = slots(lane, DEEPC, group)
             up = jnp.where(last, moved, up)
             down = jnp.where(first, moved, down)
-        at = 2 * EY * TILES + ER * f
+        at = EY * TILES + ER * f
         up_ref[at : at + ER] = up
         down_ref[at : at + ER] = down
 
 
 def beyond_fine(k, f, before, after):
-    at = EY * (TILES * f + k // PER)
-    return unpack(before[at : at + EY], after[at : at + EY], DEEP, k % PER)
+    tile, place = divmod(PLACES.index((f, k)), PER)
+    return unpack(before[EY * tile : EY * (tile + 1)], after[EY * tile : EY * (tile + 1)], DEEP, place)
 
 
 def beyond_coarse(group, f, before, after):
-    at = 2 * EY * TILES + ER * f
+    at = EY * TILES + ER * f
     return unpack(before[at : at + ER], after[at : at + ER], DEEPC, group)
 
 
@@ -246,7 +256,8 @@
     coarse = src
     for k in range(EX):
         for part in range(2):
-            fa[part, k, PAD : PAD + EY] = weight[part][k] * rhs[part][k]
+            value = rhs[part][k]
+            fa[part, k, PAD : PAD + EY] = weight[part][k] * value if 0 < k < EX - 1 else value
     src, dst = fa, fb
     for sweep in range(1, FSWEEPS):
         for k in range(sweep, EX - sweep):
@@ -296,9 +307,8 @@
     b_ref, d_ref, b, v, gm, vcm, before, after, p_ref, q_ref, qh_ref, vh_ref, vcx_ref, up_ref, down_ref, sum_ref,
     bh, gx, fa, fb, ca, cb, tmp,
 ):
-    for k in range(EX):
-        bh[k] = beyond_fine(k, 0, before, after)
-        vh_ref[k] = beyond_fine(k, 1, before, after)
+    for f, k in PLACES:
+        (bh, vh_ref)[f][k] = beyond_fine(k, f, before, after)
     for f, (tiles, out) in enumerate(((gm, gx), (vcm, vcx_ref))):
         for group in range(3):
             for part, tile in enumerate((tiles[group], beyond_coarse(group, f, before, after))):
@@ -328,11 +338,15 @@
         for ref in (up_ref, down_ref):
             ref[FACE + NY + CY * part : FACE + NY + CY * (part + 1)] = tile
     lane = lanes((NY, NZ))
-    for ref, first in ((down_ref, 0), (up_ref, NX - HF)):
+    for ref, first, far in ((down_ref, 0, HF - 1), (up_ref, NX - HF, 0)):
         packed = jnp.zeros((NY, NZ), F32)
         for k in range(HF):
-            ref[NY * k : NY * (k + 1)] = q_ref[first + k]
-            packed = jnp.where(lane // (2 * NEAR) == k, roll(qh_ref[first + k], NEAR + 2 * NEAR * k), packed)
+            value, beyond = q_ref[first + k], qh_ref[first + k]
+            if k == far:
+                value = value * v[HF + first + k, 4 : 4 + NY]
+                beyond = beyond * vh_ref[HF + first + k, 4 : 4 + NY]
+            ref[NY * k : NY * (k + 1)] = value
+            packed = jnp.where(lane // (2 * NEAR) == k, roll(beyond, NEAR + 2 * NEAR * k), packed)
         ref[FACE : FACE + NY] = packed
 
 
@@ -344,31 +358,32 @@
 
 
 SIDE = NZ // (2 * NEAR)
-PAIRS = EX // 2 - 1
+WIDE = ROWS + 3 * HC
 
 
 def second_rows_kernel(q, qh, mine, before, after, up_ref, down_ref):
     for k in range(1, EX - 1):
         plane = layer(k, 0, (q,), before, after)
-        at, row = (k - 1) // 2, HF * ((k - 1) % 2)
-        down_ref[at, row : row + HF] = plane[:HF]
-        up_ref[at, row : row + HF] = plane[NY - HF :]
+        at = HF * (k - 1)
+        down_ref[at : at + HF] = plane[:HF]
+        up_ref[at : at + HF] = plane[NY - HF :]
     lane = lanes((8, NZ))
     wide = jnp.zeros((8, NZ), F32)
     for group in range(3):
         tile = tile_of(group, FACE + NY, mine, before, after)
         beyond = tile_of(group, FACE + NY + CY, mine, before, after)
         wide = jnp.where(lane // (2 * NEARC) == group, roll(beyond, 2 * NEARC * group), wide)
-        for ref in (up_ref, down_ref):
-            ref[PAIRS + group] = tile
+        at = ROWS + HC * group
+        down_ref[at : at + HC] = tile[:HC]
+        up_ref[at : at + HC] = tile[CY - HC :]
     for ref, rows in ((up_ref, slice(NY - 8, NY)), (down_ref, slice(0, 8))):
-        ref[PAIRS + 5] = wide
+        ref[WIDE + 16 : WIDE + 24] = wide
         for half in range(2):
             packed = jnp.zeros((8, NZ), F32)
             for k in range(SIDE * half, min(EX, SIDE * (half + 1))):
                 plane = layer_beyond(k, qh, before, after)[rows]
                 packed = jnp.where(lane // (2 * NEAR) == k % SIDE, roll(plane, NEAR + 2 * NEAR * (k % SIDE)), packed)
-            ref[PAIRS + 3 + half] = packed
+            ref[WIDE + 8 * half : WIDE + 8 * (half + 1)] = packed
 
 
 def second_kernel(
@@ -376,23 +391,24 @@
     m_ref, im_ref, sum_ref, q, qh, gx, fa, fb, ca, cb,
 ):
     for k in range(EX):
-        at, row, place = (k - 1) // 2, HF * ((k - 1) % 2), -NEAR - 2 * NEAR * (k % SIDE)
+        at, place = HF * (k - 1), -NEAR - 2 * NEAR * (k % SIDE)
         for out in (q, qh):
             out[k, 0:8] = jnp.zeros((8, NZ), F32)
             out[k, EY - 8 : EY] = jnp.zeros((8, NZ), F32)
         q[k, 4 : 4 + NY] = layer(k, 0, (q_ref,), before, after)
         if 0 < k < EX - 1:
-            q[k, 4 - HF : 4] = low[at, row : row + HF]
-            q[k, 4 + NY : 4 + NY + HF] = high[at, row : row + HF]
-        tile = PAIRS + 3 + k // SIDE
+            q[k, 4 - HF : 4] = low[at : at + HF]
+            q[k, 4 + NY : 4 + NY + HF] = high[at : at + HF]
+        tile = slice(WIDE + 8 * (k // SIDE), WIDE + 8 * (k // SIDE + 1))
         qh[k, 4 - HF : 4] = edges(roll(low[tile], place), NEAR)[8 - HF :]
         qh[k, 4 : 4 + NY] = layer_beyond(k, qh_ref, before, after)
         qh[k, 4 + NY : 4 + NY + HF] = edges(roll(high[tile], place), NEAR)[:HF]
     for group in range(3):
-        at = FACE + NY
-        tile = with_rows(tile_of(group, at, mine, before, after), low[PAIRS + group], high[PAIRS + group])
-        wide = [roll(ref[PAIRS + 5], -2 * NEARC * group) for ref in (low, high)]
-        beyond = with_rows(tile_of(group, at + CY, mine, before, after), *wide)
+        at, row = FACE + NY, ROWS + HC * group
+        tile = with_rows(tile_of(group, at, mine, before, after), low[row : row + HC], high[row : row + HC])
+        wide = [roll(ref[WIDE + 16 : WIDE + 24], -2 * NEARC * group) for ref in (low, high)]
+        beyond = tile_of(group, at + CY, mine, before, after)
+        beyond = with_rows(beyond, wide[0][CY - HC :], wide[1][:HC])
         for part, merged in enumerate((tile, edges(roll(beyond, -NEARC), NEARC))):
             for c, plane in enumerate(unmerge(merged)):
                 gx[part, 4 * group + c] = plane
@@ -468,13 +484,13 @@
     block, fine, coarse = (NX, NY, NZ), (EX, EY, NZ), (2, EC, ER, NZ)
     work = [(2, EX, EY + 2 * PAD, NZ)] * 2 + [(2, EC, ER + 2 * PAD, NZ)] * 2
     bd = lax.optimization_barrier(jnp.stack([b, d]))
-    v, up, down = call(start_kernel, [block] + [(2 * FACE + 2 * CY, NZ)] * 2, [(NY, NZ)], name="start")(bd)
+    v, up, down = call(start_kernel, [block] + [(COARSE + 2 * CY, NZ)] * 2, [(NY, NZ)], name="start")(bd)
     mine = up
     before, after = both_ways(up, down, "gx")
-    up, down = call(rows_kernel, [(EX + 4, 8, NZ)] * 2, name="rows")(b, v, mine, before, after)
+    up, down = call(rows_kernel, [(2 * ROWS + 6 * HC, NZ)] * 2, name="rows")(b, v, mine, before, after)
     low, high = both_ways(up, down, "gy")
     be, ve, gm, vcm, up, down = call(
-        lanes_kernel, [fine] * 2 + [(3, ER, NZ)] * 2 + [(2 * (EY * TILES + ER), NZ)] * 2, name="lanes"
+        lanes_kernel, [fine] * 2 + [(3, ER, NZ)] * 2 + [(EY * TILES + 2 * ER, NZ)] * 2, name="lanes"
     )(b, v, mine, before, after, low, high)
     before, after = both_ways(up, down, "gz")
     p, q, qh, vh, vcx, up, down, sums = call(
@@ -485,7 +501,7 @@
     )(b, d, be, ve, gm, vcm, before, after)
     mine = up
     before, after = both_ways(up, down, "gx")
-    up, down = call(second_rows_kernel, [(PAIRS + 6, 8, NZ)] * 2, name="second_rows")(q, qh, mine, before, after)
+    up, down = call(second_rows_kernel, [(WIDE + 24, NZ)] * 2, name="second_rows")(q, qh, mine, before, after)
     low, high = both_ways(up, down, "gy")
     m, im, sums = call(second_kernel, [block, block, (1, NZ)], [fine, fine, coarse] + work, name="second")(
         b, d, p, q, qh, ve, vh, vcx, mine, before, after, low, high, sums

time: 94.8 us -> 93.9 us (level)
  transfers between devices with their start and end apart: 10 -> 10, of which waited for: 9 -> 8; matrix products, arithmetic and copies ran while one was open for 0% -> 0% of each run, Pallas kernels for 0% -> 0%
where the time goes in v6:
time: 93.9 us; the launch traced here: 93.5 us
  blocking collectives  35.7 us (38%)
  starting transfers between devices  31.3 us (33%)
  waiting for transfers between devices  17.9 us (19%)
  Pallas kernels  6.65 us (7%)
  other arithmetic  1.1 us (1%)
    all_to_all x2, blocking collectives, total(): return jnp.sum(lax.all_to_all(spread, axis, 0, 0, tiled=True), axis=0)  35.7 us
    ppermute x5, starting transfers between devices, both_ways(): after = lax.ppermute(down, axis, [(j, i) for i, j in steps])  21.8 us
    ppermute x5, waiting for transfers between devices, both_ways(): after = lax.ppermute(down, axis, [(j, i) for i, j in steps])  13.6 us
    ppermute x5, starting transfers between devices, both_ways(): before = lax.ppermute(up, axis, steps)  9.54 us
    pallas_call x7, Pallas kernels, run(): pl.pallas_call(kernel, out_shape=[jax.ShapeDtypeStruct(shape, F32) for sh...  6.65 us
    ppermute x5, waiting for transfers between devices, both_ways(): before = lax.ppermute(up, axis, steps)  4.35 us
  transfers between devices with their start and end apart: 10, of which 8 were waited for; matrix products, arithmetic and copies ran while one was open for 0% of the time, Pallas kernels for 0%

profile of v6, /device:TPU:1, one launch (start us, length us, event | category | flops | bytes accessed | tf_op | source)
XLA Modules:
  0.0 93.5 jit_solution(13120915864600042255)
XLA Ops:
  0.6 1.1 %pad_maximum_fusion.bd_ref = f32[2,16,32,128]{3,2,1,0:T(8,128)S(1)} fusion(f32[1,16,32,128]{3,2,1,0:T(8,128)} %bitcast.7, f32[1,16,32,128]{3,2,1,0:T(8,128)} %bitcast.6), kind=kLoop, calls=%fused_computation | loop fusion | flops 131072 | bytes 1048576 | tf_op jit(solution)/shard_map/stack | solution.py:486
  1.7 0.0 copy-start
  1.7 0.2 start.1
  2.0 10.5 %collective-permute-start.1 = (f32[176,128]{1,0:T(8,128)S(1)}, f32[176,128]{1,0:T(8,128)S(1)}, u32[]{:S(2)}, u32[]{:S(2)}) collective-permute-start(f32[176,128]{1,0:T(8,128)S(1)} %get-tuple-element.28), channel_id=1, source_target_pairs={{32,0},{64,32},{96,64},{128,96},{160,128},{192,160},{224,192},{256... | collective-permute-start | bytes 270344 | tf_op jit(solution)/shard_map/ppermute | solution.py:473
  12.5 0.0 collective-permute-start
  12.5 0.9 collective-permute-done.1.after
  13.4 3.0 %collective-permute-done.before = f32[176,128]{1,0:T(8,128)S(1)} collective-permute-done((f32[176,128]{1,0:T(8,128)S(1)}, f32[176,128]{1,0:T(8,128)S(1)}, u32[]{:S(2)}, u32[]{:S(2)}) %collective-permute-start) | collective-permute-done | bytes 90144 | tf_op jit(solution)/shard_map/ppermute | solution.py:472
  16.4 0.0 copy-done
  16.4 3.2 %collective-permute-start.2 = (f32[144,128]{1,0:T(8,128)S(1)}, f32[144,128]{1,0:T(8,128)S(1)}, u32[]{:S(2)}, u32[]{:S(2)}) collective-permute-start(f32[144,128]{1,0:T(8,128)S(1)} %get-tuple-element.29), channel_id=1, source_target_pairs={{0,4},{4,8},{8,12},{12,16},{16,20},{20,24},{24,28},{1,5},{5,9},{9,... | collective-permute-start | bytes 221192 | tf_op jit(solution)/shard_map/ppermute | solution.py:472
  19.6 0.0 copy-start.1
  19.6 1.4 %collective-permute-start.3 = (f32[144,128]{1,0:T(8,128)S(1)}, f32[144,128]{1,0:T(8,128)S(1)}, u32[]{:S(2)}, u32[]{:S(2)}) collective-permute-start(f32[144,128]{1,0:T(8,128)S(1)} %get-tuple-element.30), channel_id=1, source_target_pairs={{4,0},{8,4},{12,8},{16,12},{20,16},{24,20},{28,24},{5,1},{9,5},{13... | collective-permute-start | bytes 221192 | tf_op jit(solution)/shard_map/ppermute | solution.py:473
  21.1 0.0 collective-permute-done.2.low
  21.1 3.8 %collective-permute-done.3.high = f32[144,128]{1,0:T(8,128)S(1)} collective-permute-done((f32[144,128]{1,0:T(8,128)S(1)}, f32[144,128]{1,0:T(8,128)S(1)}, u32[]{:S(2)}, u32[]{:S(2)}) %collective-permute-start.3) | collective-permute-done | bytes 73760 | tf_op jit(solution)/shard_map/ppermute | solution.py:473
  24.9 0.3 lanes.1
  25.2 3.1 %collective-permute-start.4 = (f32[312,128]{1,0:T(8,128)S(1)}, f32[312,128]{1,0:T(8,128)S(1)}, u32[]{:S(2)}, u32[]{:S(2)}) collective-permute-start(f32[312,128]{1,0:T(8,128)S(1)} %get-tuple-element.35), channel_id=1, source_target_pairs={{0,1},{1,2},{2,3},{4,5},{5,6},{6,7},{8,9},{9,10},{10,11},{12,13},{... | collective-permute-start | bytes 479240 | tf_op jit(solution)/shard_map/ppermute | solution.py:472
  28.3 1.3 %collective-permute-start.5 = (f32[312,128]{1,0:T(8,128)S(1)}, f32[312,128]{1,0:T(8,128)S(1)}, u32[]{:S(2)}, u32[]{:S(2)}) collective-permute-start(f32[312,128]{1,0:T(8,128)S(1)} %get-tuple-element.36), channel_id=1, source_target_pairs={{1,0},{2,1},{3,2},{5,4},{6,5},{7,6},{9,8},{10,9},{11,10},{13,12},{... | collective-permute-start | bytes 479240 | tf_op jit(solution)/shard_map/ppermute | solution.py:473
  29.6 0.9 collective-permute-done.4.before
  30.5 3.8 %collective-permute-done.5.after = f32[312,128]{1,0:T(8,128)S(1)} collective-permute-done((f32[312,128]{1,0:T(8,128)S(1)}, f32[312,128]{1,0:T(8,128)S(1)}, u32[]{:S(2)}, u32[]{:S(2)}) %collective-permute-start.5) | collective-permute-done | bytes 159776 | tf_op jit(solution)/shard_map/ppermute | solution.py:473
  34.3 0.0 copy-done.1
  34.3 2.7 %first.1 = (f32[16,32,128]{2,1,0:T(8,128)S(1)}, f32[16,32,128]{2,1,0:T(8,128)S(1)}, f32[16,32,128]{2,1,0:T(8,128)S(1)}, f32[22,40,128]{2,1,0:T(8,128)S(1)}, f32[...) custom-call(f32[16,32,128]{2,1,0:T(8,128)S(1)} %copy-done, ...), custom_call_target="tpu_custom_call" | custom-call | tf_op jit(solution)/shard_map/first/pallas_call | solution.py:456
  37.1 7.2 %collective-permute-start.7 = (f32[144,128]{1,0:T(8,128)S(1)}, f32[144,128]{1,0:T(8,128)S(1)}, u32[]{:S(2)}, u32[]{:S(2)}) collective-permute-start(f32[144,128]{1,0:T(8,128)S(1)} %get-tuple-element.43), channel_id=1, source_target_pairs={{32,0},{64,32},{96,64},{128,96},{160,128},{192,160},{224,192},{256... | collective-permute-start | bytes 221192 | tf_op jit(solution)/shard_map/ppermute | solution.py:473
  44.3 0.0 collective-permute-start.6
  44.3 0.9 collective-permute-done.7.after
  45.2 0.5 collective-permute-done.6.before
  45.7 0.2 second_rows.1
  45.9 3.2 %collective-permute-start.8 = (f32[96,128]{1,0:T(8,128)S(1)}, f32[96,128]{1,0:T(8,128)S(1)}, u32[]{:S(2)}, u32[]{:S(2)}) collective-permute-start(f32[96,128]{1,0:T(8,128)S(1)} %get-tuple-element.44), channel_id=1, source_target_pairs={{0,4},{4,8},{8,12},{12,16},{16,20},{20,24},{24,28},{1,5},{5,9},{9,... | collective-permute-start | bytes 147464 | tf_op jit(solution)/shard_map/ppermute | solution.py:472
  49.1 1.3 %collective-permute-start.9 = (f32[96,128]{1,0:T(8,128)S(1)}, f32[96,128]{1,0:T(8,128)S(1)}, u32[]{:S(2)}, u32[]{:S(2)}) collective-permute-start(f32[96,128]{1,0:T(8,128)S(1)} %get-tuple-element.45), channel_id=1, source_target_pairs={{4,0},{8,4},{12,8},{16,12},{20,16},{24,20},{28,24},{5,1},{9,5},{13... | collective-permute-start | bytes 147464 | tf_op jit(solution)/shard_map/ppermute | solution.py:473
  50.4 0.0 collective-permute-done.8.low
  50.4 4.1 %collective-permute-done.9.high = f32[96,128]{1,0:T(8,128)S(1)} collective-permute-done((f32[96,128]{1,0:T(8,128)S(1)}, f32[96,128]{1,0:T(8,128)S(1)}, u32[]{:S(2)}, u32[]{:S(2)}) %collective-permute-start.9) | collective-permute-done | bytes 49184 | tf_op jit(solution)/shard_map/ppermute | solution.py:473
  54.6 2.2 %second.1 = (f32[16,32,128]{2,1,0:T(8,128)S(1)}, f32[16,32,128]{2,1,0:T(8,128)S(1)}, f32[1,128]{1,0:T(1,128)S(1)}) custom-call(f32[16,32,128]{2,1,0:T(8,128)S(1)} %copy-done, f32[16,32,128]{2,1,0:T(8,128)S(1)} %copy-done.1, f32[16,32,128]{2,1,0:T(8,128)S(1)} %get-tuple-element.37.p_ref, f32[16,32,128]{2,1,0:T(8,128)S(1)} %get-tuple-element.38.q.q_ref, ...), custom_call_target="tpu_custom_call" | custom-call | tf_op jit(solution)/shard_map/second/pallas_call | solution.py:456
  56.8 17.3 %all_to_all.10 = f32[32,1,128]{2,1,0:T(1,128)S(1)} all-to-all(f32[32,1,128]{2,1,0:T(1,128)S(1)} %broadcast_in_dim.7), channel_id=1, replica_groups=mesh['gx'=24,'gy'=8,'gz'=4] {'gy','gz'}, dimensions={0} | all-to-all | bytes 32768 | tf_op jit(solution)/shard_map/all_to_all | solution.py:480
  74.1 18.4 %all_to_all.11 = f32[24,1,128]{2,1,0:T(1,128)S(1)} all-to-all(f32[24,1,128]{2,1,0:T(1,128)S(1)} %broadcast_in_dim.16), channel_id=1, replica_groups=mesh['gx'=24,'gy'=8,'gz'=4] {'gx'}, dimensions={0} | all-to-all | bytes 24576 | tf_op jit(solution)/shard_map/all_to_all | solution.py:480
  92.6 1.0 %last.1 = (f32[16,32,128]{2,1,0:T(8,128)}, f32[16,32,128]{2,1,0:T(8,128)}) custom-call(f32[16,32,128]{2,1,0:T(8,128)S(1)} %copy-done, f32[16,32,128]{2,1,0:T(8,128)S(1)} %get-tuple-element.37.p_ref, f32[16,32,128]{2,1,0:T(8,128)S(1)} %get-tuple-element.38.q.q_ref, f32[16,32,128]{2,1,0:T(8,128)S(1)} %get-tuple-element.47.m_ref, ...), custom_call_target="tpu_custom_call" | custom-call | tf_op jit(solution)/shard_map/last/pallas_call | solution.py:456
  (5 shorter events, 0.1 us)
Async XLA Ops:
  1.7 14.7 %copy-start = (f32[16,32,128]{2,1,0:T(8,128)S(1)}, f32[16,32,128]{2,1,0:T(8,128)}, u32[]{:S(2)}) copy-start(f32[16,32,128]{2,1,0:T(8,128)} %b_ref.5) | copy-start | bytes 786436
  2.0 11.5 %collective-permute-start.1 = (f32[176,128]{1,0:T(8,128)S(1)}, f32[176,128]{1,0:T(8,128)S(1)}, u32[]{:S(2)}, u32[]{:S(2)}) collective-permute-start(f32[176,128]{1,0:T(8,128)S(1)} %get-tuple-element.28), channel_id=1, source_target_pairs={{32,0},{64,32},{96,64},{128,96},{160,128},{192,160},{224,192},{256... | collective-permute-start | bytes 270344 | tf_op jit(solution)/shard_map/ppermute | solution.py:473
  12.5 3.9 %collective-permute-start = (f32[176,128]{1,0:T(8,128)S(1)}, f32[176,128]{1,0:T(8,128)S(1)}, u32[]{:S(2)}, u32[]{:S(2)}) collective-permute-start(f32[176,128]{1,0:T(8,128)S(1)} %get-tuple-element.27.mine), channel_id=1, source_target_pairs={{0,32},{32,64},{64,96},{96,128},{128,160},{160,192},{192,224},{224... | collective-permute-start | bytes 270344 | tf_op jit(solution)/shard_map/ppermute | solution.py:472
  16.4 4.7 %collective-permute-start.2 = (f32[144,128]{1,0:T(8,128)S(1)}, f32[144,128]{1,0:T(8,128)S(1)}, u32[]{:S(2)}, u32[]{:S(2)}) collective-permute-start(f32[144,128]{1,0:T(8,128)S(1)} %get-tuple-element.29), channel_id=1, source_target_pairs={{0,4},{4,8},{8,12},{12,16},{16,20},{20,24},{24,28},{1,5},{5,9},{9,... | collective-permute-start | bytes 221192 | tf_op jit(solution)/shard_map/ppermute | solution.py:472
  19.6 14.7 %copy-start.1 = (f32[16,32,128]{2,1,0:T(8,128)S(1)}, f32[16,32,128]{2,1,0:T(8,128)}, u32[]{:S(2)}) copy-start(f32[16,32,128]{2,1,0:T(8,128)} %d_ref.3) | copy-start | bytes 786436
  19.6 5.2 %collective-permute-start.3 = (f32[144,128]{1,0:T(8,128)S(1)}, f32[144,128]{1,0:T(8,128)S(1)}, u32[]{:S(2)}, u32[]{:S(2)}) collective-permute-start(f32[144,128]{1,0:T(8,128)S(1)} %get-tuple-element.30), channel_id=1, source_target_pairs={{4,0},{8,4},{12,8},{16,12},{20,16},{24,20},{28,24},{5,1},{9,5},{13... | collective-permute-start | bytes 221192 | tf_op jit(solution)/shard_map/ppermute | solution.py:473
  25.2 5.3 %collective-permute-start.4 = (f32[312,128]{1,0:T(8,128)S(1)}, f32[312,128]{1,0:T(8,128)S(1)}, u32[]{:S(2)}, u32[]{:S(2)}) collective-permute-start(f32[312,128]{1,0:T(8,128)S(1)} %get-tuple-element.35), channel_id=1, source_target_pairs={{0,1},{1,2},{2,3},{4,5},{5,6},{6,7},{8,9},{9,10},{10,11},{12,13},{... | collective-permute-start | bytes 479240 | tf_op jit(solution)/shard_map/ppermute | solution.py:472
  28.3 6.0 %collective-permute-start.5 = (f32[312,128]{1,0:T(8,128)S(1)}, f32[312,128]{1,0:T(8,128)S(1)}, u32[]{:S(2)}, u32[]{:S(2)}) collective-permute-start(f32[312,128]{1,0:T(8,128)S(1)} %get-tuple-element.36), channel_id=1, source_target_pairs={{1,0},{2,1},{3,2},{5,4},{6,5},{7,6},{9,8},{10,9},{11,10},{13,12},{... | collective-permute-start | bytes 479240 | tf_op jit(solution)/shard_map/ppermute | solution.py:473
  37.1 8.2 %collective-permute-start.7 = (f32[144,128]{1,0:T(8,128)S(1)}, f32[144,128]{1,0:T(8,128)S(1)}, u32[]{:S(2)}, u32[]{:S(2)}) collective-permute-start(f32[144,128]{1,0:T(8,128)S(1)} %get-tuple-element.43), channel_id=1, source_target_pairs={{32,0},{64,32},{96,64},{128,96},{160,128},{192,160},{224,192},{256... | collective-permute-start | bytes 221192 | tf_op jit(solution)/shard_map/ppermute | solution.py:473
  44.3 1.4 %collective-permute-start.6 = (f32[144,128]{1,0:T(8,128)S(1)}, f32[144,128]{1,0:T(8,128)S(1)}, u32[]{:S(2)}, u32[]{:S(2)}) collective-permute-start(f32[144,128]{1,0:T(8,128)S(1)} %get-tuple-element.42.mine), channel_id=1, source_target_pairs={{0,32},{32,64},{64,96},{96,128},{128,160},{160,192},{192,224},{224... | collective-permute-start | bytes 221192 | tf_op jit(solution)/shard_map/ppermute | solution.py:472
  45.9 4.5 %collective-permute-start.8 = (f32[96,128]{1,0:T(8,128)S(1)}, f32[96,128]{1,0:T(8,128)S(1)}, u32[]{:S(2)}, u32[]{:S(2)}) collective-permute-start(f32[96,128]{1,0:T(8,128)S(1)} %get-tuple-element.44), channel_id=1, source_target_pairs={{0,4},{4,8},{8,12},{12,16},{16,20},{20,24},{24,28},{1,5},{5,9},{9,... | collective-permute-start | bytes 147464 | tf_op jit(solution)/shard_map/ppermute | solution.py:472
  49.1 5.5 %collective-permute-start.9 = (f32[96,128]{1,0:T(8,128)S(1)}, f32[96,128]{1,0:T(8,128)S(1)}, u32[]{:S(2)}, u32[]{:S(2)}) collective-permute-start(f32[96,128]{1,0:T(8,128)S(1)} %get-tuple-element.45), channel_id=1, source_target_pairs={{4,0},{8,4},{12,8},{16,12},{20,16},{24,20},{28,24},{5,1},{9,5},{13... | collective-permute-start | bytes 147464 | tf_op jit(solution)/shard_map/ppermute | solution.py:473

commit v7 on v6

--- a/solution.py
+++ b/solution.py
@@ -31,6 +31,7 @@
 PLACES = [(0, k) for k in range(EX)] + [(1, k) for k in range(1, EX - 1)]
 TILES = -(-len(PLACES) // PER)
 ROWS = HF * (EX - 2)
+PARTS = CX
 VMEM = pl.BlockSpec(memory_space=pltpu.VMEM)
 F32 = jnp.float32
 
@@ -102,12 +103,19 @@
     return jnp.concatenate([low, tile, high], axis=0)
 
 
-def start_kernel(bd_ref, v_ref, up_ref, down_ref, tmp):
-    b_ref, d_ref = bd_ref.at[0], bd_ref.at[1]
-    for i in range(NX):
-        v_ref[i] = damping / (6.0 + d_ref[i])
+def start_kernel(b_hbm, d_hbm, v_ref, up_ref, down_ref, b_ref, d_ref, tmp, sems):
+    copies = []
+    for part in range(PARTS):
+        at = pl.ds(NX // PARTS * part, NX // PARTS)
+        for which, (src, dst) in enumerate(((b_hbm, b_ref), (d_hbm, d_ref))):
+            copies.append(pltpu.make_async_copy(src.at[at], dst.at[at], sems.at[2 * part + which]))
+            copies[-1].start()
     g, vc = [], []
     for c in range(CX):
+        copies[2 * c].wait()
+        copies[2 * c + 1].wait()
+        for i in range(COARSEN * c, COARSEN * (c + 1)):
+            v_ref[i] = damping / (6.0 + d_ref[i])
         g.append(block_sums([b_ref[COARSEN * c + k] for k in range(COARSEN)], tmp) * 0.25)
         cd = 6.0 + block_sums([d_ref[COARSEN * c + k] for k in range(COARSEN)], tmp) * 0.25
         vc.append(damping / cd)
@@ -424,9 +432,6 @@
     store_sums(sum_ref, dict(enumerate(sums, 2)), first_ref[...])
 
 
-PARTS = 4
-
-
 def last_kernel(b_ref, p_ref, q_ref, m_ref, im_ref, sum_ref, x_out, r_out, x_ref, r_ref, sems):
     rp, pq, qm, rm, pim, mim = [
         jnp.sum(jnp.where(lanes((1, NZ)) // SHARE == i, sum_ref[...], 0.0), axis=1, keepdims=True) for i in range(6)
@@ -451,12 +456,12 @@
         copy.wait()
 
 
-def call(kernel, outs, scratch=(), name=None, out_space=pltpu.VMEM):
+def call(kernel, outs, scratch=(), name=None, in_space=pltpu.VMEM, out_space=pltpu.VMEM):
     def run(*args):
         return pl.pallas_call(
             kernel,
             out_shape=[jax.ShapeDtypeStruct(shape, F32) for shape in outs],
-            in_specs=[VMEM] * len(args),
+            in_specs=[pl.BlockSpec(memory_space=in_space)] * len(args),
             out_specs=[pl.BlockSpec(memory_space=out_space)] * len(outs),
             scratch_shapes=[pltpu.VMEM(shape, F32) if isinstance(shape, tuple) else shape for shape in scratch],
             compiler_params=pltpu.CompilerParams(vmem_limit_bytes=24 * 2**20),
@@ -483,8 +488,8 @@
 def on_device(b, d):
     block, fine, coarse = (NX, NY, NZ), (EX, EY, NZ), (2, EC, ER, NZ)
     work = [(2, EX, EY + 2 * PAD, NZ)] * 2 + [(2, EC, ER + 2 * PAD, NZ)] * 2
-    bd = lax.optimization_barrier(jnp.stack([b, d]))
-    v, up, down = call(start_kernel, [block] + [(COARSE + 2 * CY, NZ)] * 2, [(NY, NZ)], name="start")(bd)
+    bh, dh = (pltpu.with_memory_space_constraint(x, pltpu.HBM) for x in (b, d))
+    v, up, down = call(start_kernel, [block] + [(COARSE + 2 * CY, NZ)] * 2, [block, block, (NY, NZ), pltpu.SemaphoreType.DMA((2 * PARTS,))], name="start", in_space=pltpu.HBM)(bh, dh)
     mine = up
     before, after = both_ways(up, down, "gx")
     up, down = call(rows_kernel, [(2 * ROWS + 6 * HC, NZ)] * 2, name="rows")(b, v, mine, before, after)

time: 93.9 us -> 94.3 us (level)
  Pallas kernels: 6.65 us -> 8.16 us
  other arithmetic: 1.1 us -> 0.04 us
    pallas_call x7, Pallas kernels: 6.65 us -> 8.16 us  [run(): pl.pallas_call(kernel, out_shape=[jax.ShapeDtypeStruct(shape, F32) for sh...]
    another operation x1 -> x0, other arithmetic: 1.07 us -> none  [on_device(): bd = lax.optimization_barrier(jnp.stack([b, d]))]
where the time goes in v7:
time: 94.3 us; the launch traced here: 94 us
  blocking collectives  35.7 us (38%)
  starting transfers between devices  31.3 us (33%)
  waiting for transfers between devices  17.9 us (19%)
  Pallas kernels  8.16 us (9%)
    all_to_all x2, blocking collectives, total(): return jnp.sum(lax.all_to_all(spread, axis, 0, 0, tiled=True), axis=0)  35.7 us
    ppermute x5, starting transfers between devices, both_ways(): after = lax.ppermute(down, axis, [(j, i) for i, j in steps])  21.8 us
    ppermute x5, waiting for transfers between devices, both_ways(): after = lax.ppermute(down, axis, [(j, i) for i, j in steps])  13.6 us
    ppermute x5, starting transfers between devices, both_ways(): before = lax.ppermute(up, axis, steps)  9.54 us
    pallas_call x7, Pallas kernels, run(): pl.pallas_call(kernel, out_shape=[jax.ShapeDtypeStruct(shape, F32) for sh...  8.16 us
    ppermute x5, waiting for transfers between devices, both_ways(): before = lax.ppermute(up, axis, steps)  4.35 us
  transfers between devices with their start and end apart: 10, of which 8 were waited for; matrix products, arithmetic and copies ran while one was open for 0% of the time, Pallas kernels for 0%

profile of v7, /device:TPU:1, one launch (start us, length us, event | category | flops | bytes accessed | tf_op | source)
XLA Modules:
  0.0 94.0 jit_solution(8347696056772214658)
XLA Ops:
  0.6 0.0 copy-start
  0.6 1.7 %start.1 = (f32[16,32,128]{2,1,0:T(8,128)S(1)}, f32[176,128]{1,0:T(8,128)S(1)}, f32[176,128]{1,0:T(8,128)S(1)}) custom-call(f32[16,32,128]{2,1,0:T(8,128)} %b_ref.5, f32[16,32,128]{2,1,0:T(8,128)} %d_ref.3), custom_call_target="tpu_custom_call" | custom-call | tf_op jit(solution)/shard_map/start/pallas_call | solution.py:461
  2.4 10.5 %collective-permute-start.1 = (f32[176,128]{1,0:T(8,128)S(1)}, f32[176,128]{1,0:T(8,128)S(1)}, u32[]{:S(2)}, u32[]{:S(2)}) collective-permute-start(f32[176,128]{1,0:T(8,128)S(1)} %get-tuple-element.28), channel_id=1, source_target_pairs={{32,0},{64,32},{96,64},{128,96},{160,128},{192,160},{224,192},{256... | collective-permute-start | bytes 270344 | tf_op jit(solution)/shard_map/ppermute | solution.py:478
  12.9 0.0 collective-permute-start
  12.9 0.9 collective-permute-done.1.after
  13.8 3.0 %collective-permute-done.before = f32[176,128]{1,0:T(8,128)S(1)} collective-permute-done((f32[176,128]{1,0:T(8,128)S(1)}, f32[176,128]{1,0:T(8,128)S(1)}, u32[]{:S(2)}, u32[]{:S(2)}) %collective-permute-start) | collective-permute-done | bytes 90144 | tf_op jit(solution)/shard_map/ppermute | solution.py:477
  16.8 0.0 copy-done
  16.8 3.2 %collective-permute-start.2 = (f32[144,128]{1,0:T(8,128)S(1)}, f32[144,128]{1,0:T(8,128)S(1)}, u32[]{:S(2)}, u32[]{:S(2)}) collective-permute-start(f32[144,128]{1,0:T(8,128)S(1)} %get-tuple-element.29), channel_id=1, source_target_pairs={{0,4},{4,8},{8,12},{12,16},{16,20},{20,24},{24,28},{1,5},{5,9},{9,... | collective-permute-start | bytes 221192 | tf_op jit(solution)/shard_map/ppermute | solution.py:477
  20.0 0.0 copy-start.1
  20.1 1.4 %collective-permute-start.3 = (f32[144,128]{1,0:T(8,128)S(1)}, f32[144,128]{1,0:T(8,128)S(1)}, u32[]{:S(2)}, u32[]{:S(2)}) collective-permute-start(f32[144,128]{1,0:T(8,128)S(1)} %get-tuple-element.30), channel_id=1, source_target_pairs={{4,0},{8,4},{12,8},{16,12},{20,16},{24,20},{28,24},{5,1},{9,5},{13... | collective-permute-start | bytes 221192 | tf_op jit(solution)/shard_map/ppermute | solution.py:478
  21.5 0.0 collective-permute-done.2.low
  21.5 3.8 %collective-permute-done.3.high = f32[144,128]{1,0:T(8,128)S(1)} collective-permute-done((f32[144,128]{1,0:T(8,128)S(1)}, f32[144,128]{1,0:T(8,128)S(1)}, u32[]{:S(2)}, u32[]{:S(2)}) %collective-permute-start.3) | collective-permute-done | bytes 73760 | tf_op jit(solution)/shard_map/ppermute | solution.py:478
  25.3 0.3 lanes.1
  25.6 3.1 %collective-permute-start.4 = (f32[312,128]{1,0:T(8,128)S(1)}, f32[312,128]{1,0:T(8,128)S(1)}, u32[]{:S(2)}, u32[]{:S(2)}) collective-permute-start(f32[312,128]{1,0:T(8,128)S(1)} %get-tuple-element.35), channel_id=1, source_target_pairs={{0,1},{1,2},{2,3},{4,5},{5,6},{6,7},{8,9},{9,10},{10,11},{12,13},{... | collective-permute-start | bytes 479240 | tf_op jit(solution)/shard_map/ppermute | solution.py:477
  28.7 1.3 %collective-permute-start.5 = (f32[312,128]{1,0:T(8,128)S(1)}, f32[312,128]{1,0:T(8,128)S(1)}, u32[]{:S(2)}, u32[]{:S(2)}) collective-permute-start(f32[312,128]{1,0:T(8,128)S(1)} %get-tuple-element.36), channel_id=1, source_target_pairs={{1,0},{2,1},{3,2},{5,4},{6,5},{7,6},{9,8},{10,9},{11,10},{13,12},{... | collective-permute-start | bytes 479240 | tf_op jit(solution)/shard_map/ppermute | solution.py:478
  30.0 0.9 collective-permute-done.4.before
  30.9 3.8 %collective-permute-done.5.after = f32[312,128]{1,0:T(8,128)S(1)} collective-permute-done((f32[312,128]{1,0:T(8,128)S(1)}, f32[312,128]{1,0:T(8,128)S(1)}, u32[]{:S(2)}, u32[]{:S(2)}) %collective-permute-start.5) | collective-permute-done | bytes 159776 | tf_op jit(solution)/shard_map/ppermute | solution.py:478
  34.8 0.0 copy-done.1
  34.8 2.7 %first.1 = (f32[16,32,128]{2,1,0:T(8,128)S(1)}, f32[16,32,128]{2,1,0:T(8,128)S(1)}, f32[16,32,128]{2,1,0:T(8,128)S(1)}, f32[22,40,128]{2,1,0:T(8,128)S(1)}, f32[...) custom-call(f32[16,32,128]{2,1,0:T(8,128)S(1)} %copy-done, ...), custom_call_target="tpu_custom_call" | custom-call | tf_op jit(solution)/shard_map/first/pallas_call | solution.py:461
  37.5 7.2 %collective-permute-start.7 = (f32[144,128]{1,0:T(8,128)S(1)}, f32[144,128]{1,0:T(8,128)S(1)}, u32[]{:S(2)}, u32[]{:S(2)}) collective-permute-start(f32[144,128]{1,0:T(8,128)S(1)} %get-tuple-element.43), channel_id=1, source_target_pairs={{32,0},{64,32},{96,64},{128,96},{160,128},{192,160},{224,192},{256... | collective-permute-start | bytes 221192 | tf_op jit(solution)/shard_map/ppermute | solution.py:478
  44.7 0.0 collective-permute-start.6
  44.7 0.9 collective-permute-done.7.after
  45.7 0.5 collective-permute-done.6.before
  46.2 0.2 second_rows.1
  46.3 3.2 %collective-permute-start.8 = (f32[96,128]{1,0:T(8,128)S(1)}, f32[96,128]{1,0:T(8,128)S(1)}, u32[]{:S(2)}, u32[]{:S(2)}) collective-permute-start(f32[96,128]{1,0:T(8,128)S(1)} %get-tuple-element.44), channel_id=1, source_target_pairs={{0,4},{4,8},{8,12},{12,16},{16,20},{20,24},{24,28},{1,5},{5,9},{9,... | collective-permute-start | bytes 147464 | tf_op jit(solution)/shard_map/ppermute | solution.py:477
  49.5 1.3 %collective-permute-start.9 = (f32[96,128]{1,0:T(8,128)S(1)}, f32[96,128]{1,0:T(8,128)S(1)}, u32[]{:S(2)}, u32[]{:S(2)}) collective-permute-start(f32[96,128]{1,0:T(8,128)S(1)} %get-tuple-element.45), channel_id=1, source_target_pairs={{4,0},{8,4},{12,8},{16,12},{20,16},{24,20},{28,24},{5,1},{9,5},{13... | collective-permute-start | bytes 147464 | tf_op jit(solution)/shard_map/ppermute | solution.py:478
  50.8 0.0 collective-permute-done.8.low
  50.8 4.1 %collective-permute-done.9.high = f32[96,128]{1,0:T(8,128)S(1)} collective-permute-done((f32[96,128]{1,0:T(8,128)S(1)}, f32[96,128]{1,0:T(8,128)S(1)}, u32[]{:S(2)}, u32[]{:S(2)}) %collective-permute-start.9) | collective-permute-done | bytes 49184 | tf_op jit(solution)/shard_map/ppermute | solution.py:478
  55.0 2.2 %second.1 = (f32[16,32,128]{2,1,0:T(8,128)S(1)}, f32[16,32,128]{2,1,0:T(8,128)S(1)}, f32[1,128]{1,0:T(1,128)S(1)}) custom-call(f32[16,32,128]{2,1,0:T(8,128)S(1)} %copy-done, f32[16,32,128]{2,1,0:T(8,128)S(1)} %copy-done.1, f32[16,32,128]{2,1,0:T(8,128)S(1)} %get-tuple-element.37.p_ref, f32[16,32,128]{2,1,0:T(8,128)S(1)} %get-tuple-element.38.q.q_ref, ...), custom_call_target="tpu_custom_call" | custom-call | tf_op jit(solution)/shard_map/second/pallas_call | solution.py:461
  57.2 17.3 %all_to_all.10 = f32[32,1,128]{2,1,0:T(1,128)S(1)} all-to-all(f32[32,1,128]{2,1,0:T(1,128)S(1)} %broadcast_in_dim.7), channel_id=1, replica_groups=mesh['gx'=24,'gy'=8,'gz'=4] {'gy','gz'}, dimensions={0} | all-to-all | bytes 32768 | tf_op jit(solution)/shard_map/all_to_all | solution.py:485
  74.5 18.4 %all_to_all.11 = f32[24,1,128]{2,1,0:T(1,128)S(1)} all-to-all(f32[24,1,128]{2,1,0:T(1,128)S(1)} %broadcast_in_dim.16), channel_id=1, replica_groups=mesh['gx'=24,'gy'=8,'gz'=4] {'gx'}, dimensions={0} | all-to-all | bytes 24576 | tf_op jit(solution)/shard_map/all_to_all | solution.py:485
  93.0 1.0 %last.1 = (f32[16,32,128]{2,1,0:T(8,128)}, f32[16,32,128]{2,1,0:T(8,128)}) custom-call(f32[16,32,128]{2,1,0:T(8,128)S(1)} %copy-done, f32[16,32,128]{2,1,0:T(8,128)S(1)} %get-tuple-element.37.p_ref, f32[16,32,128]{2,1,0:T(8,128)S(1)} %get-tuple-element.38.q.q_ref, f32[16,32,128]{2,1,0:T(8,128)S(1)} %get-tuple-element.47.m_ref, ...), custom_call_target="tpu_custom_call" | custom-call | tf_op jit(solution)/shard_map/last/pallas_call | solution.py:461
  (5 shorter events, 0.1 us)
Async XLA Ops:
  0.6 16.2 %copy-start = (f32[16,32,128]{2,1,0:T(8,128)S(1)}, f32[16,32,128]{2,1,0:T(8,128)}, u32[]{:S(2)}) copy-start(f32[16,32,128]{2,1,0:T(8,128)} %b_ref.5) | copy-start | bytes 786436
  2.4 11.5 %collective-permute-start.1 = (f32[176,128]{1,0:T(8,128)S(1)}, f32[176,128]{1,0:T(8,128)S(1)}, u32[]{:S(2)}, u32[]{:S(2)}) collective-permute-start(f32[176,128]{1,0:T(8,128)S(1)} %get-tuple-element.28), channel_id=1, source_target_pairs={{32,0},{64,32},{96,64},{128,96},{160,128},{192,160},{224,192},{256... | collective-permute-start | bytes 270344 | tf_op jit(solution)/shard_map/ppermute | solution.py:478
  12.9 3.9 %collective-permute-start = (f32[176,128]{1,0:T(8,128)S(1)}, f32[176,128]{1,0:T(8,128)S(1)}, u32[]{:S(2)}, u32[]{:S(2)}) collective-permute-start(f32[176,128]{1,0:T(8,128)S(1)} %get-tuple-element.27.mine), channel_id=1, source_target_pairs={{0,32},{32,64},{64,96},{96,128},{128,160},{160,192},{192,224},{224... | collective-permute-start | bytes 270344 | tf_op jit(solution)/shard_map/ppermute | solution.py:477
  16.8 4.7 %collective-permute-start.2 = (f32[144,128]{1,0:T(8,128)S(1)}, f32[144,128]{1,0:T(8,128)S(1)}, u32[]{:S(2)}, u32[]{:S(2)}) collective-permute-start(f32[144,128]{1,0:T(8,128)S(1)} %get-tuple-element.29), channel_id=1, source_target_pairs={{0,4},{4,8},{8,12},{12,16},{16,20},{20,24},{24,28},{1,5},{5,9},{9,... | collective-permute-start | bytes 221192 | tf_op jit(solution)/shard_map/ppermute | solution.py:477
  20.0 14.7 %copy-start.1 = (f32[16,32,128]{2,1,0:T(8,128)S(1)}, f32[16,32,128]{2,1,0:T(8,128)}, u32[]{:S(2)}) copy-start(f32[16,32,128]{2,1,0:T(8,128)} %d_ref.3) | copy-start | bytes 786436
  20.1 5.2 %collective-permute-start.3 = (f32[144,128]{1,0:T(8,128)S(1)}, f32[144,128]{1,0:T(8,128)S(1)}, u32[]{:S(2)}, u32[]{:S(2)}) collective-permute-start(f32[144,128]{1,0:T(8,128)S(1)} %get-tuple-element.30), channel_id=1, source_target_pairs={{4,0},{8,4},{12,8},{16,12},{20,16},{24,20},{28,24},{5,1},{9,5},{13... | collective-permute-start | bytes 221192 | tf_op jit(solution)/shard_map/ppermute | solution.py:478
  25.6 5.3 %collective-permute-start.4 = (f32[312,128]{1,0:T(8,128)S(1)}, f32[312,128]{1,0:T(8,128)S(1)}, u32[]{:S(2)}, u32[]{:S(2)}) collective-permute-start(f32[312,128]{1,0:T(8,128)S(1)} %get-tuple-element.35), channel_id=1, source_target_pairs={{0,1},{1,2},{2,3},{4,5},{5,6},{6,7},{8,9},{9,10},{10,11},{12,13},{... | collective-permute-start | bytes 479240 | tf_op jit(solution)/shard_map/ppermute | solution.py:477
  28.7 6.0 %collective-permute-start.5 = (f32[312,128]{1,0:T(8,128)S(1)}, f32[312,128]{1,0:T(8,128)S(1)}, u32[]{:S(2)}, u32[]{:S(2)}) collective-permute-start(f32[312,128]{1,0:T(8,128)S(1)} %get-tuple-element.36), channel_id=1, source_target_pairs={{1,0},{2,1},{3,2},{5,4},{6,5},{7,6},{9,8},{10,9},{11,10},{13,12},{... | collective-permute-start | bytes 479240 | tf_op jit(solution)/shard_map/ppermute | solution.py:478
  37.5 8.2 %collective-permute-start.7 = (f32[144,128]{1,0:T(8,128)S(1)}, f32[144,128]{1,0:T(8,128)S(1)}, u32[]{:S(2)}, u32[]{:S(2)}) collective-permute-start(f32[144,128]{1,0:T(8,128)S(1)} %get-tuple-element.43), channel_id=1, source_target_pairs={{32,0},{64,32},{96,64},{128,96},{160,128},{192,160},{224,192},{256... | collective-permute-start | bytes 221192 | tf_op jit(solution)/shard_map/ppermute | solution.py:478
  44.7 1.4 %collective-permute-start.6 = (f32[144,128]{1,0:T(8,128)S(1)}, f32[144,128]{1,0:T(8,128)S(1)}, u32[]{:S(2)}, u32[]{:S(2)}) collective-permute-start(f32[144,128]{1,0:T(8,128)S(1)} %get-tuple-element.42.mine), channel_id=1, source_target_pairs={{0,32},{32,64},{64,96},{96,128},{128,160},{160,192},{192,224},{224... | collective-permute-start | bytes 221192 | tf_op jit(solution)/shard_map/ppermute | solution.py:477
  46.3 4.5 %collective-permute-start.8 = (f32[96,128]{1,0:T(8,128)S(1)}, f32[96,128]{1,0:T(8,128)S(1)}, u32[]{:S(2)}, u32[]{:S(2)}) collective-permute-start(f32[96,128]{1,0:T(8,128)S(1)} %get-tuple-element.44), channel_id=1, source_target_pairs={{0,4},{4,8},{8,12},{12,16},{16,20},{20,24},{24,28},{1,5},{5,9},{9,... | collective-permute-start | bytes 147464 | tf_op jit(solution)/shard_map/ppermute | solution.py:477
  49.5 5.5 %collective-permute-start.9 = (f32[96,128]{1,0:T(8,128)S(1)}, f32[96,128]{1,0:T(8,128)S(1)}, u32[]{:S(2)}, u32[]{:S(2)}) collective-permute-start(f32[96,128]{1,0:T(8,128)S(1)} %get-tuple-element.45), channel_id=1, source_target_pairs={{4,0},{8,4},{12,8},{16,12},{20,16},{24,20},{28,24},{5,1},{9,5},{13... | collective-permute-start | bytes 147464 | tf_op jit(solution)/shard_map/ppermute | solution.py:478

commit v8 on v6

--- a/solution.py
+++ b/solution.py
@@ -50,12 +50,6 @@
     return x + jnp.where(lane % 4 < 2, roll(x, -2), roll(x, 2))
 
 
-def block_sums(planes, tmp):
-    tmp[...] = group_sum(planes[0] + planes[1] + planes[2] + planes[3])
-    rows = [tmp[pl.ds(k, CY, stride=COARSEN), :] for k in range(COARSEN)]
-    return rows[0] + rows[1] + rows[2] + rows[3]
-
-
 def merge(planes):
     lane = lanes(planes[0].shape)
     out = planes[0]
@@ -64,16 +58,27 @@
     return out
 
 
-def unmerge(tile):
+def unmerge(tile, planes):
     lane = lanes(tile.shape) % 4
-    moved = {step: roll(tile, -step) if step else tile for step in range(-3, 4)}
-    planes = []
-    for c in range(4):
-        out = moved[c]
+    out = []
+    for c in planes:
+        moved = [roll(tile, at - c) if at != c else tile for at in range(4)]
+        plane = moved[0]
         for at in range(1, 4):
-            out = jnp.where(lane == at, moved[c - at], out)
-        planes.append(out)
-    return planes
+            plane = jnp.where(lane == at, moved[at], plane)
+        out.append(plane)
+    return out
+
+
+def block_sums(field, tmp):
+    rows = []
+    for c in range(CX):
+        first, second, third, fourth = [field[COARSEN * c + k] for k in range(COARSEN)]
+        tmp[c] = (first + second) + (third + fourth)
+        parts = [tmp[c, pl.ds(k, CY, stride=COARSEN), :] for k in range(COARSEN)]
+        rows.append((parts[0] + parts[1]) + (parts[2] + parts[3]))
+    sums = group_sum(jnp.concatenate(rows, axis=0))
+    return merge([sums[CY * c : CY * (c + 1)] for c in range(CX)])
 
 
 def edges(x, width):
@@ -106,14 +111,11 @@
     b_ref, d_ref = bd_ref.at[0], bd_ref.at[1]
     for i in range(NX):
         v_ref[i] = damping / (6.0 + d_ref[i])
-    g, vc = [], []
-    for c in range(CX):
-        g.append(block_sums([b_ref[COARSEN * c + k] for k in range(COARSEN)], tmp) * 0.25)
-        cd = 6.0 + block_sums([d_ref[COARSEN * c + k] for k in range(COARSEN)], tmp) * 0.25
-        vc.append(damping / cd)
+    g = block_sums(b_ref, tmp) * 0.25
+    vc = damping / (6.0 + block_sums(d_ref, tmp) * 0.25)
     for ref in (up_ref, down_ref):
-        for f, planes in enumerate((g, vc)):
-            ref[COARSE + CY * f : COARSE + CY * (f + 1)] = merge(planes)
+        ref[COARSE : COARSE + CY] = g
+        ref[COARSE + CY : COARSE + 2 * CY] = vc
     for k in range(HF):
         for ref, plane, far in ((down_ref, k, HF - 1), (up_ref, NX - HF + k, 0)):
             value, weight = b_ref[plane], v_ref[plane]
@@ -230,30 +232,49 @@
     first = lax.broadcasted_iota(jnp.int32, (8, NZ), 0) < 4
     groups = []
     for j in range(EY // 8):
-        row = PAD + 3 + 2 * j
+        row = 3 + 2 * j
         a = jnp.broadcast_to(coarse[part, c, row : row + 1], (8, NZ))
         b = jnp.broadcast_to(coarse[part, c, row + 1 : row + 2], (8, NZ))
         groups.append(jnp.where(first, a, b))
     return jnp.concatenate(groups, axis=0)
 
 
-def precondition(rhs, weight, crhs, cweight, fa, fb, ca, cb):
+def coarse_neighbours(src, group):
+    at = PAD
+    here = [src[part, group, at : at + ER] for part in range(2)]
+    along = crossed(here[0], here[1], COARSEN)
+    lane = lanes((ER, NZ)) % 4
+    out = []
+    for part in range(2):
+        below = roll(src[part, group - 1, at : at + ER], -3) if group > 0 else 0.0
+        above = roll(src[part, group + 1, at : at + ER], 3) if group < 2 else 0.0
+        beside = jnp.where(lane == 0, below, roll(here[part], 1)) + jnp.where(lane == 3, above, roll(here[part], -1))
+        beside = beside + (src[part, group, at - 1 : at - 1 + ER] + src[part, group, at + 1 : at + 1 + ER])
+        out.append(beside + along[part])
+    return here, out
+
+
+def precondition(rhs, weight, crhs, cweight, fa, fb, ca, cb, coarse):
     for ref, rows in ((fa, EY), (fb, EY), (ca, ER), (cb, ER)):
         for part in range(2):
             for k in range(ref.shape[1]):
                 ref[part, k, 0:PAD] = jnp.zeros((PAD, NZ), F32)
                 ref[part, k, PAD + rows :] = jnp.zeros((PAD, NZ), F32)
-    for k in range(EC):
+    for group in range(3):
         for part in range(2):
-            ca[part, k, PAD : PAD + ER] = cweight[part, k] * crhs[part, k]
+            ca[part, group, PAD : PAD + ER] = cweight[part][group] * crhs[part][group]
     src, dst = ca, cb
     for sweep in range(1, CSWEEPS):
-        for k in range(sweep, EC - sweep):
-            here, beside = neighbours(src, k, ER, COARSEN)
+        for group in range(3):
+            here, beside = coarse_neighbours(src, group)
             for part in range(2):
-                dst[part, k, PAD : PAD + ER] = keep * here[part] + cweight[part, k] * (crhs[part, k] + beside[part])
+                new = keep * here[part] + cweight[part][group] * (crhs[part][group] + beside[part])
+                dst[part, group, PAD : PAD + ER] = new
         src, dst = dst, src
-    coarse = src
+    for group, planes in enumerate(((3,), (0, 1, 2, 3), (0,))):
+        for part in range(2):
+            for c, plane in zip(planes, unmerge(src[part, group, PAD : PAD + ER], planes)):
+                coarse[part, 4 * group + c] = plane
     for k in range(EX):
         for part in range(2):
             value = rhs[part][k]
@@ -304,17 +325,15 @@
 
 
 def first_kernel(
-    b_ref, d_ref, b, v, gm, vcm, before, after, p_ref, q_ref, qh_ref, vh_ref, vcx_ref, up_ref, down_ref, sum_ref,
-    bh, gx, fa, fb, ca, cb, tmp,
+    b_ref, d_ref, b, v, gm, vcm, before, after, p_ref, q_ref, qh_ref, vh_ref, vch_ref, up_ref, down_ref, sum_ref,
+    bh, fa, fb, ca, cb, coarse, tmp,
 ):
     for f, k in PLACES:
         (bh, vh_ref)[f][k] = beyond_fine(k, f, before, after)
-    for f, (tiles, out) in enumerate(((gm, gx), (vcm, vcx_ref))):
-        for group in range(3):
-            for part, tile in enumerate((tiles[group], beyond_coarse(group, f, before, after))):
-                for c, plane in enumerate(unmerge(tile)):
-                    out[part, 4 * group + c] = plane
-    precondition((b, bh), (v, vh_ref), gx, vcx_ref, fa, fb, ca, cb)
+    gh = [beyond_coarse(group, 0, before, after) for group in range(3)]
+    for group in range(3):
+        vch_ref[group] = beyond_coarse(group, 1, before, after)
+    precondition((b, bh), (v, vh_ref), (gm, gh), (vcm, vch_ref), fa, fb, ca, cb, coarse)
     rp = jnp.zeros((8, NZ), F32)
     pq = jnp.zeros((8, NZ), F32)
     for i in range(NX):
@@ -329,10 +348,7 @@
         pq = pq + add_up(p * q)
     store_sums(sum_ref, {0: rp, 1: pq})
     for part, field in enumerate((q_ref, qh_ref)):
-        means = [
-            block_sums([field[COARSEN * c + k] for k in range(COARSEN)], tmp) * 0.25 for c in range(CX)
-        ]
-        tile = merge(means)
+        tile = block_sums(field, tmp) * 0.25
         if part == 1:
             tile = roll(tile, NEARC)
         for ref in (up_ref, down_ref):
@@ -387,8 +403,8 @@
 
 
 def second_kernel(
-    b_ref, d_ref, p_ref, q_ref, qh_ref, v, vh_ref, vcx_ref, mine, before, after, low, high, first_ref,
-    m_ref, im_ref, sum_ref, q, qh, gx, fa, fb, ca, cb,
+    b_ref, d_ref, p_ref, q_ref, qh_ref, v, vh_ref, vcm, vch, mine, before, after, low, high, first_ref,
+    m_ref, im_ref, sum_ref, q, qh, fa, fb, ca, cb, coarse,
 ):
     for k in range(EX):
         at, place = HF * (k - 1), -NEAR - 2 * NEAR * (k % SIDE)
@@ -403,16 +419,16 @@
         qh[k, 4 - HF : 4] = edges(roll(low[tile], place), NEAR)[8 - HF :]
         qh[k, 4 : 4 + NY] = layer_beyond(k, qh_ref, before, after)
         qh[k, 4 + NY : 4 + NY + HF] = edges(roll(high[tile], place), NEAR)[:HF]
+    g, gh = [], []
     for group in range(3):
         at, row = FACE + NY, ROWS + HC * group
         tile = with_rows(tile_of(group, at, mine, before, after), low[row : row + HC], high[row : row + HC])
         wide = [roll(ref[WIDE + 16 : WIDE + 24], -2 * NEARC * group) for ref in (low, high)]
         beyond = tile_of(group, at + CY, mine, before, after)
         beyond = with_rows(beyond, wide[0][CY - HC :], wide[1][:HC])
-        for part, merged in enumerate((tile, edges(roll(beyond, -NEARC), NEARC))):
-            for c, plane in enumerate(unmerge(merged)):
-                gx[part, 4 * group + c] = plane
-    precondition((q, qh), (v, vh_ref), gx, vcx_ref, fa, fb, ca, cb)
+        g.append(tile)
+        gh.append(edges(roll(beyond, -NEARC), NEARC))
+    precondition((q, qh), (v, vh_ref), (g, gh), (vcm, vch), fa, fb, ca, cb, coarse)
     sums = [jnp.zeros((8, NZ), F32)] * 4
     for i in range(NX):
         (m, _), (beside, _) = image_plane(fa, i)
@@ -481,30 +497,30 @@
 
 
 def on_device(b, d):
-    block, fine, coarse = (NX, NY, NZ), (EX, EY, NZ), (2, EC, ER, NZ)
-    work = [(2, EX, EY + 2 * PAD, NZ)] * 2 + [(2, EC, ER + 2 * PAD, NZ)] * 2
+    block, fine, tiles = (NX, NY, NZ), (EX, EY, NZ), (3, ER, NZ)
+    work = [(2, EX, EY + 2 * PAD, NZ)] * 2 + [(2, 3, ER + 2 * PAD, NZ)] * 2 + [(2, EC, ER, NZ)]
     bd = lax.optimization_barrier(jnp.stack([b, d]))
-    v, up, down = call(start_kernel, [block] + [(COARSE + 2 * CY, NZ)] * 2, [(NY, NZ)], name="start")(bd)
+    v, up, down = call(start_kernel, [block] + [(COARSE + 2 * CY, NZ)] * 2, [(CX, NY, NZ)], name="start")(bd)
     mine = up
     before, after = both_ways(up, down, "gx")
     up, down = call(rows_kernel, [(2 * ROWS + 6 * HC, NZ)] * 2, name="rows")(b, v, mine, before, after)
     low, high = both_ways(up, down, "gy")
     be, ve, gm, vcm, up, down = call(
-        lanes_kernel, [fine] * 2 + [(3, ER, NZ)] * 2 + [(EY * TILES + 2 * ER, NZ)] * 2, name="lanes"
+        lanes_kernel, [fine] * 2 + [tiles] * 2 + [(EY * TILES + 2 * ER, NZ)] * 2, name="lanes"
     )(b, v, mine, before, after, low, high)
     before, after = both_ways(up, down, "gz")
-    p, q, qh, vh, vcx, up, down, sums = call(
+    p, q, qh, vh, vch, up, down, sums = call(
         first_kernel,
-        [block] * 3 + [fine, coarse] + [(FACE + NY + 2 * CY, NZ)] * 2 + [(1, NZ)],
-        [fine, coarse] + work + [(NY, NZ)],
+        [block] * 3 + [fine, tiles] + [(FACE + NY + 2 * CY, NZ)] * 2 + [(1, NZ)],
+        [fine] + work + [(CX, NY, NZ)],
         name="first",
     )(b, d, be, ve, gm, vcm, before, after)
     mine = up
     before, after = both_ways(up, down, "gx")
     up, down = call(second_rows_kernel, [(WIDE + 24, NZ)] * 2, name="second_rows")(q, qh, mine, before, after)
     low, high = both_ways(up, down, "gy")
-    m, im, sums = call(second_kernel, [block, block, (1, NZ)], [fine, fine, coarse] + work, name="second")(
-        b, d, p, q, qh, ve, vh, vcx, mine, before, after, low, high, sums
+    m, im, sums = call(second_kernel, [block, block, (1, NZ)], [fine, fine] + work, name="second")(
+        b, d, p, q, qh, ve, vh, vcm, vch, mine, before, after, low, high, sums
     )
     for axis in (("gy", "gz"), ("gx",)):
         sums = total(sums, axis)

time: 93.9 us -> 93.3 us (level)
  no operation moved by 1% of the time
where the time goes in v8:
time: 93.3 us; the launch traced here: 93 us
  blocking collectives  35.7 us (38%)
  starting transfers between devices  31.3 us (34%)
  waiting for transfers between devices  17.9 us (19%)
  Pallas kernels  6.1 us (7%)
  other arithmetic  1.1 us (1%)
    all_to_all x2, blocking collectives, total(): return jnp.sum(lax.all_to_all(spread, axis, 0, 0, tiled=True), axis=0)  35.7 us
    ppermute x5, starting transfers between devices, both_ways(): after = lax.ppermute(down, axis, [(j, i) for i, j in steps])  21.8 us
    ppermute x5, waiting for transfers between devices, both_ways(): after = lax.ppermute(down, axis, [(j, i) for i, j in steps])  13.6 us
    ppermute x5, starting transfers between devices, both_ways(): before = lax.ppermute(up, axis, steps)  9.54 us
    pallas_call x7, Pallas kernels, run(): pl.pallas_call(kernel, out_shape=[jax.ShapeDtypeStruct(shape, F32) for sh...  6.1 us
    ppermute x5, waiting for transfers between devices, both_ways(): before = lax.ppermute(up, axis, steps)  4.35 us
  transfers between devices with their start and end apart: 10, of which 8 were waited for; matrix products, arithmetic and copies ran while one was open for 0% of the time, Pallas kernels for 0%

profile of v8, /device:TPU:1, one launch (start us, length us, event | category | flops | bytes accessed | tf_op | source)
XLA Modules:
  0.0 93.0 jit_solution(14816793186482014026)
XLA Ops:
  0.6 1.1 %pad_maximum_fusion.bd_ref = f32[2,16,32,128]{3,2,1,0:T(8,128)S(1)} fusion(f32[1,16,32,128]{3,2,1,0:T(8,128)} %bitcast.7, f32[1,16,32,128]{3,2,1,0:T(8,128)} %bitcast.6), kind=kLoop, calls=%fused_computation | loop fusion | flops 131072 | bytes 1048576 | tf_op jit(solution)/shard_map/stack | solution.py:502
  1.7 0.0 copy-start
  1.7 0.2 start.1
  1.9 10.5 %collective-permute-start.1 = (f32[176,128]{1,0:T(8,128)S(1)}, f32[176,128]{1,0:T(8,128)S(1)}, u32[]{:S(2)}, u32[]{:S(2)}) collective-permute-start(f32[176,128]{1,0:T(8,128)S(1)} %get-tuple-element.28), channel_id=1, source_target_pairs={{32,0},{64,32},{96,64},{128,96},{160,128},{192,160},{224,192},{256... | collective-permute-start | bytes 270344 | tf_op jit(solution)/shard_map/ppermute | solution.py:489
  12.4 0.0 collective-permute-start
  12.4 0.9 %collective-permute-done.1.after = f32[176,128]{1,0:T(8,128)S(1)} collective-permute-done((f32[176,128]{1,0:T(8,128)S(1)}, f32[176,128]{1,0:T(8,128)S(1)}, u32[]{:S(2)}, u32[]{:S(2)}) %collective-permute-start.1) | collective-permute-done | bytes 90144 | tf_op jit(solution)/shard_map/ppermute | solution.py:489
  13.4 3.0 %collective-permute-done.before = f32[176,128]{1,0:T(8,128)S(1)} collective-permute-done((f32[176,128]{1,0:T(8,128)S(1)}, f32[176,128]{1,0:T(8,128)S(1)}, u32[]{:S(2)}, u32[]{:S(2)}) %collective-permute-start) | collective-permute-done | bytes 90144 | tf_op jit(solution)/shard_map/ppermute | solution.py:488
  16.3 0.0 copy-done
  16.4 3.2 %collective-permute-start.2 = (f32[144,128]{1,0:T(8,128)S(1)}, f32[144,128]{1,0:T(8,128)S(1)}, u32[]{:S(2)}, u32[]{:S(2)}) collective-permute-start(f32[144,128]{1,0:T(8,128)S(1)} %get-tuple-element.29), channel_id=1, source_target_pairs={{0,4},{4,8},{8,12},{12,16},{16,20},{20,24},{24,28},{1,5},{5,9},{9,... | collective-permute-start | bytes 221192 | tf_op jit(solution)/shard_map/ppermute | solution.py:488
  19.6 0.0 copy-start.1
  19.6 1.4 %collective-permute-start.3 = (f32[144,128]{1,0:T(8,128)S(1)}, f32[144,128]{1,0:T(8,128)S(1)}, u32[]{:S(2)}, u32[]{:S(2)}) collective-permute-start(f32[144,128]{1,0:T(8,128)S(1)} %get-tuple-element.30), channel_id=1, source_target_pairs={{4,0},{8,4},{12,8},{16,12},{20,16},{24,20},{28,24},{5,1},{9,5},{13... | collective-permute-start | bytes 221192 | tf_op jit(solution)/shard_map/ppermute | solution.py:489
  21.0 0.0 collective-permute-done.2.low
  21.0 3.8 %collective-permute-done.3.high = f32[144,128]{1,0:T(8,128)S(1)} collective-permute-done((f32[144,128]{1,0:T(8,128)S(1)}, f32[144,128]{1,0:T(8,128)S(1)}, u32[]{:S(2)}, u32[]{:S(2)}) %collective-permute-start.3) | collective-permute-done | bytes 73760 | tf_op jit(solution)/shard_map/ppermute | solution.py:489
  24.8 0.3 lanes.1
  25.2 3.1 %collective-permute-start.4 = (f32[312,128]{1,0:T(8,128)S(1)}, f32[312,128]{1,0:T(8,128)S(1)}, u32[]{:S(2)}, u32[]{:S(2)}) collective-permute-start(f32[312,128]{1,0:T(8,128)S(1)} %get-tuple-element.35), channel_id=1, source_target_pairs={{0,1},{1,2},{2,3},{4,5},{5,6},{6,7},{8,9},{9,10},{10,11},{12,13},{... | collective-permute-start | bytes 479240 | tf_op jit(solution)/shard_map/ppermute | solution.py:488
  28.3 1.3 %collective-permute-start.5 = (f32[312,128]{1,0:T(8,128)S(1)}, f32[312,128]{1,0:T(8,128)S(1)}, u32[]{:S(2)}, u32[]{:S(2)}) collective-permute-start(f32[312,128]{1,0:T(8,128)S(1)} %get-tuple-element.36), channel_id=1, source_target_pairs={{1,0},{2,1},{3,2},{5,4},{6,5},{7,6},{9,8},{10,9},{11,10},{13,12},{... | collective-permute-start | bytes 479240 | tf_op jit(solution)/shard_map/ppermute | solution.py:489
  29.6 0.9 collective-permute-done.4.before
  30.5 3.8 %collective-permute-done.5.after = f32[312,128]{1,0:T(8,128)S(1)} collective-permute-done((f32[312,128]{1,0:T(8,128)S(1)}, f32[312,128]{1,0:T(8,128)S(1)}, u32[]{:S(2)}, u32[]{:S(2)}) %collective-permute-start.5) | collective-permute-done | bytes 159776 | tf_op jit(solution)/shard_map/ppermute | solution.py:489
  34.3 0.0 copy-done.1
  34.3 2.2 %first.1 = (f32[16,32,128]{2,1,0:T(8,128)S(1)}, f32[16,32,128]{2,1,0:T(8,128)S(1)}, f32[16,32,128]{2,1,0:T(8,128)S(1)}, f32[22,40,128]{2,1,0:T(8,128)S(1)}, f32[...) custom-call(f32[16,32,128]{2,1,0:T(8,128)S(1)} %copy-done, ...), custom_call_target="tpu_custom_call" | custom-call | tf_op jit(solution)/shard_map/first/pallas_call | solution.py:472
  36.6 7.3 %collective-permute-start.7 = (f32[144,128]{1,0:T(8,128)S(1)}, f32[144,128]{1,0:T(8,128)S(1)}, u32[]{:S(2)}, u32[]{:S(2)}) collective-permute-start(f32[144,128]{1,0:T(8,128)S(1)} %get-tuple-element.43), channel_id=1, source_target_pairs={{32,0},{64,32},{96,64},{128,96},{160,128},{192,160},{224,192},{256... | collective-permute-start | bytes 221192 | tf_op jit(solution)/shard_map/ppermute | solution.py:489
  43.8 0.0 collective-permute-start.6
  43.8 0.9 collective-permute-done.7.after
  44.7 0.5 collective-permute-done.6.before
  45.2 0.2 second_rows.1
  45.4 3.2 %collective-permute-start.8 = (f32[96,128]{1,0:T(8,128)S(1)}, f32[96,128]{1,0:T(8,128)S(1)}, u32[]{:S(2)}, u32[]{:S(2)}) collective-permute-start(f32[96,128]{1,0:T(8,128)S(1)} %get-tuple-element.44), channel_id=1, source_target_pairs={{0,4},{4,8},{8,12},{12,16},{16,20},{20,24},{24,28},{1,5},{5,9},{9,... | collective-permute-start | bytes 147464 | tf_op jit(solution)/shard_map/ppermute | solution.py:488
  48.6 1.3 %collective-permute-start.9 = (f32[96,128]{1,0:T(8,128)S(1)}, f32[96,128]{1,0:T(8,128)S(1)}, u32[]{:S(2)}, u32[]{:S(2)}) collective-permute-start(f32[96,128]{1,0:T(8,128)S(1)} %get-tuple-element.45), channel_id=1, source_target_pairs={{4,0},{8,4},{12,8},{16,12},{20,16},{24,20},{28,24},{5,1},{9,5},{13... | collective-permute-start | bytes 147464 | tf_op jit(solution)/shard_map/ppermute | solution.py:489
  49.9 0.0 collective-permute-done.8.low
  49.9 4.1 %collective-permute-done.9.high = f32[96,128]{1,0:T(8,128)S(1)} collective-permute-done((f32[96,128]{1,0:T(8,128)S(1)}, f32[96,128]{1,0:T(8,128)S(1)}, u32[]{:S(2)}, u32[]{:S(2)}) %collective-permute-start.9) | collective-permute-done | bytes 49184 | tf_op jit(solution)/shard_map/ppermute | solution.py:489
  54.1 2.2 %second.1 = (f32[16,32,128]{2,1,0:T(8,128)S(1)}, f32[16,32,128]{2,1,0:T(8,128)S(1)}, f32[1,128]{1,0:T(1,128)S(1)}) custom-call(f32[16,32,128]{2,1,0:T(8,128)S(1)} %copy-done, f32[16,32,128]{2,1,0:T(8,128)S(1)} %copy-done.1, f32[16,32,128]{2,1,0:T(8,128)S(1)} %get-tuple-element.37.p_ref, f32[16,32,128]{2,1,0:T(8,128)S(1)} %get-tuple-element.38.q.q_ref, ...), custom_call_target="tpu_custom_call" | custom-call | tf_op jit(solution)/shard_map/second/pallas_call | solution.py:472
  56.3 17.3 %all_to_all.10 = f32[32,1,128]{2,1,0:T(1,128)S(1)} all-to-all(f32[32,1,128]{2,1,0:T(1,128)S(1)} %broadcast_in_dim.7), channel_id=1, replica_groups=mesh['gx'=24,'gy'=8,'gz'=4] {'gy','gz'}, dimensions={0} | all-to-all | bytes 32768 | tf_op jit(solution)/shard_map/all_to_all | solution.py:496
  73.6 18.5 %all_to_all.11 = f32[24,1,128]{2,1,0:T(1,128)S(1)} all-to-all(f32[24,1,128]{2,1,0:T(1,128)S(1)} %broadcast_in_dim.16), channel_id=1, replica_groups=mesh['gx'=24,'gy'=8,'gz'=4] {'gx'}, dimensions={0} | all-to-all | bytes 24576 | tf_op jit(solution)/shard_map/all_to_all | solution.py:496
  92.0 1.0 %last.1 = (f32[16,32,128]{2,1,0:T(8,128)}, f32[16,32,128]{2,1,0:T(8,128)}) custom-call(f32[16,32,128]{2,1,0:T(8,128)S(1)} %copy-done, f32[16,32,128]{2,1,0:T(8,128)S(1)} %get-tuple-element.37.p_ref, f32[16,32,128]{2,1,0:T(8,128)S(1)} %get-tuple-element.38.q.q_ref, f32[16,32,128]{2,1,0:T(8,128)S(1)} %get-tuple-element.47.m_ref, ...), custom_call_target="tpu_custom_call" | custom-call | tf_op jit(solution)/shard_map/last/pallas_call | solution.py:472
  (5 shorter events, 0.1 us)
Async XLA Ops:
  1.7 14.6 %copy-start = (f32[16,32,128]{2,1,0:T(8,128)S(1)}, f32[16,32,128]{2,1,0:T(8,128)}, u32[]{:S(2)}) copy-start(f32[16,32,128]{2,1,0:T(8,128)} %b_ref.5) | copy-start | bytes 786436
  1.9 11.5 %collective-permute-start.1 = (f32[176,128]{1,0:T(8,128)S(1)}, f32[176,128]{1,0:T(8,128)S(1)}, u32[]{:S(2)}, u32[]{:S(2)}) collective-permute-start(f32[176,128]{1,0:T(8,128)S(1)} %get-tuple-element.28), channel_id=1, source_target_pairs={{32,0},{64,32},{96,64},{128,96},{160,128},{192,160},{224,192},{256... | collective-permute-start | bytes 270344 | tf_op jit(solution)/shard_map/ppermute | solution.py:489
  12.4 3.9 %collective-permute-start = (f32[176,128]{1,0:T(8,128)S(1)}, f32[176,128]{1,0:T(8,128)S(1)}, u32[]{:S(2)}, u32[]{:S(2)}) collective-permute-start(f32[176,128]{1,0:T(8,128)S(1)} %get-tuple-element.27.mine), channel_id=1, source_target_pairs={{0,32},{32,64},{64,96},{96,128},{128,160},{160,192},{192,224},{224... | collective-permute-start | bytes 270344 | tf_op jit(solution)/shard_map/ppermute | solution.py:488
  16.4 4.7 %collective-permute-start.2 = (f32[144,128]{1,0:T(8,128)S(1)}, f32[144,128]{1,0:T(8,128)S(1)}, u32[]{:S(2)}, u32[]{:S(2)}) collective-permute-start(f32[144,128]{1,0:T(8,128)S(1)} %get-tuple-element.29), channel_id=1, source_target_pairs={{0,4},{4,8},{8,12},{12,16},{16,20},{20,24},{24,28},{1,5},{5,9},{9,... | collective-permute-start | bytes 221192 | tf_op jit(solution)/shard_map/ppermute | solution.py:488
  19.6 14.7 %copy-start.1 = (f32[16,32,128]{2,1,0:T(8,128)S(1)}, f32[16,32,128]{2,1,0:T(8,128)}, u32[]{:S(2)}) copy-start(f32[16,32,128]{2,1,0:T(8,128)} %d_ref.3) | copy-start | bytes 786436
  19.6 5.2 %collective-permute-start.3 = (f32[144,128]{1,0:T(8,128)S(1)}, f32[144,128]{1,0:T(8,128)S(1)}, u32[]{:S(2)}, u32[]{:S(2)}) collective-permute-start(f32[144,128]{1,0:T(8,128)S(1)} %get-tuple-element.30), channel_id=1, source_target_pairs={{4,0},{8,4},{12,8},{16,12},{20,16},{24,20},{28,24},{5,1},{9,5},{13... | collective-permute-start | bytes 221192 | tf_op jit(solution)/shard_map/ppermute | solution.py:489
  25.2 5.3 %collective-permute-start.4 = (f32[312,128]{1,0:T(8,128)S(1)}, f32[312,128]{1,0:T(8,128)S(1)}, u32[]{:S(2)}, u32[]{:S(2)}) collective-permute-start(f32[312,128]{1,0:T(8,128)S(1)} %get-tuple-element.35), channel_id=1, source_target_pairs={{0,1},{1,2},{2,3},{4,5},{5,6},{6,7},{8,9},{9,10},{10,11},{12,13},{... | collective-permute-start | bytes 479240 | tf_op jit(solution)/shard_map/ppermute | solution.py:488
  28.3 6.0 %collective-permute-start.5 = (f32[312,128]{1,0:T(8,128)S(1)}, f32[312,128]{1,0:T(8,128)S(1)}, u32[]{:S(2)}, u32[]{:S(2)}) collective-permute-start(f32[312,128]{1,0:T(8,128)S(1)} %get-tuple-element.36), channel_id=1, source_target_pairs={{1,0},{2,1},{3,2},{5,4},{6,5},{7,6},{9,8},{10,9},{11,10},{13,12},{... | collective-permute-start | bytes 479240 | tf_op jit(solution)/shard_map/ppermute | solution.py:489
  36.6 8.2 %collective-permute-start.7 = (f32[144,128]{1,0:T(8,128)S(1)}, f32[144,128]{1,0:T(8,128)S(1)}, u32[]{:S(2)}, u32[]{:S(2)}) collective-permute-start(f32[144,128]{1,0:T(8,128)S(1)} %get-tuple-element.43), channel_id=1, source_target_pairs={{32,0},{64,32},{96,64},{128,96},{160,128},{192,160},{224,192},{256... | collective-permute-start | bytes 221192 | tf_op jit(solution)/shard_map/ppermute | solution.py:489
  43.8 1.4 %collective-permute-start.6 = (f32[144,128]{1,0:T(8,128)S(1)}, f32[144,128]{1,0:T(8,128)S(1)}, u32[]{:S(2)}, u32[]{:S(2)}) collective-permute-start(f32[144,128]{1,0:T(8,128)S(1)} %get-tuple-element.42.mine), channel_id=1, source_target_pairs={{0,32},{32,64},{64,96},{96,128},{128,160},{160,192},{192,224},{224... | collective-permute-start | bytes 221192 | tf_op jit(solution)/shard_map/ppermute | solution.py:488
  45.4 4.5 %collective-permute-start.8 = (f32[96,128]{1,0:T(8,128)S(1)}, f32[96,128]{1,0:T(8,128)S(1)}, u32[]{:S(2)}, u32[]{:S(2)}) collective-permute-start(f32[96,128]{1,0:T(8,128)S(1)} %get-tuple-element.44), channel_id=1, source_target_pairs={{0,4},{4,8},{8,12},{12,16},{16,20},{20,24},{24,28},{1,5},{5,9},{9,... | collective-permute-start | bytes 147464 | tf_op jit(solution)/shard_map/ppermute | solution.py:488
  48.6 5.5 %collective-permute-start.9 = (f32[96,128]{1,0:T(8,128)S(1)}, f32[96,128]{1,0:T(8,128)S(1)}, u32[]{:S(2)}, u32[]{:S(2)}) collective-permute-start(f32[96,128]{1,0:T(8,128)S(1)} %get-tuple-element.45), channel_id=1, source_target_pairs={{4,0},{8,4},{12,8},{16,12},{20,16},{24,20},{28,24},{5,1},{9,5},{13... | collective-permute-start | bytes 147464 | tf_op jit(solution)/shard_map/ppermute | solution.py:489

commit v9 on v8

--- a/solution.py
+++ b/solution.py
@@ -522,7 +522,7 @@
     m, im, sums = call(second_kernel, [block, block, (1, NZ)], [fine, fine] + work, name="second")(
         b, d, p, q, qh, ve, vh, vcm, vch, mine, before, after, low, high, sums
     )
-    for axis in (("gy", "gz"), ("gx",)):
+    for axis in (("gx",), ("gy", "gz")):
         sums = total(sums, axis)
     return call(
         last_kernel,

time: 93.3 us -> 91.9 us (0.985)
  blocking collectives: 35.7 us -> 34.3 us
    all_to_all x2, blocking collectives: 35.7 us -> 34.3 us  [total(): return jnp.sum(lax.all_to_all(spread, axis, 0, 0, tiled=True), axis=0)]
where the time goes in v9:
time: 91.9 us; the launch traced here: 91.6 us
  blocking collectives  34.3 us (37%)
  starting transfers between devices  31.3 us (34%)
  waiting for transfers between devices  17.9 us (19%)
  Pallas kernels  6.1 us (7%)
  other arithmetic  1.1 us (1%)
    all_to_all x2, blocking collectives, total(): return jnp.sum(lax.all_to_all(spread, axis, 0, 0, tiled=True), axis=0)  34.3 us
    ppermute x5, starting transfers between devices, both_ways(): after = lax.ppermute(down, axis, [(j, i) for i, j in steps])  21.8 us
    ppermute x5, waiting for transfers between devices, both_ways(): after = lax.ppermute(down, axis, [(j, i) for i, j in steps])  13.6 us
    ppermute x5, starting transfers between devices, both_ways(): before = lax.ppermute(up, axis, steps)  9.54 us
    pallas_call x7, Pallas kernels, run(): pl.pallas_call(kernel, out_shape=[jax.ShapeDtypeStruct(shape, F32) for sh...  6.1 us
    ppermute x5, waiting for transfers between devices, both_ways(): before = lax.ppermute(up, axis, steps)  4.35 us
  transfers between devices with their start and end apart: 10, of which 8 were waited for; matrix products, arithmetic and copies ran while one was open for 0% of the time, Pallas kernels for 0%

profile of v9, /device:TPU:1, one launch (start us, length us, event | category | flops | bytes accessed | tf_op | source)
XLA Modules:
  0.0 91.6 jit_solution(11221514469328216477)
XLA Ops:
  0.6 1.1 %pad_maximum_fusion.bd_ref = f32[2,16,32,128]{3,2,1,0:T(8,128)S(1)} fusion(f32[1,16,32,128]{3,2,1,0:T(8,128)} %bitcast.7, f32[1,16,32,128]{3,2,1,0:T(8,128)} %bitcast.6), kind=kLoop, calls=%fused_computation | loop fusion | flops 131072 | bytes 1048576 | tf_op jit(solution)/shard_map/stack | solution.py:502
  1.7 0.0 copy-start
  1.7 0.2 start.1
  1.9 10.5 %collective-permute-start.1 = (f32[176,128]{1,0:T(8,128)S(1)}, f32[176,128]{1,0:T(8,128)S(1)}, u32[]{:S(2)}, u32[]{:S(2)}) collective-permute-start(f32[176,128]{1,0:T(8,128)S(1)} %get-tuple-element.28), channel_id=1, source_target_pairs={{32,0},{64,32},{96,64},{128,96},{160,128},{192,160},{224,192},{256... | collective-permute-start | bytes 270344 | tf_op jit(solution)/shard_map/ppermute | solution.py:489
  12.4 0.0 collective-permute-start
  12.4 0.9 %collective-permute-done.1.after = f32[176,128]{1,0:T(8,128)S(1)} collective-permute-done((f32[176,128]{1,0:T(8,128)S(1)}, f32[176,128]{1,0:T(8,128)S(1)}, u32[]{:S(2)}, u32[]{:S(2)}) %collective-permute-start.1) | collective-permute-done | bytes 90144 | tf_op jit(solution)/shard_map/ppermute | solution.py:489
  13.4 3.0 %collective-permute-done.before = f32[176,128]{1,0:T(8,128)S(1)} collective-permute-done((f32[176,128]{1,0:T(8,128)S(1)}, f32[176,128]{1,0:T(8,128)S(1)}, u32[]{:S(2)}, u32[]{:S(2)}) %collective-permute-start) | collective-permute-done | bytes 90144 | tf_op jit(solution)/shard_map/ppermute | solution.py:488
  16.3 0.0 copy-done
  16.4 3.2 %collective-permute-start.2 = (f32[144,128]{1,0:T(8,128)S(1)}, f32[144,128]{1,0:T(8,128)S(1)}, u32[]{:S(2)}, u32[]{:S(2)}) collective-permute-start(f32[144,128]{1,0:T(8,128)S(1)} %get-tuple-element.29), channel_id=1, source_target_pairs={{0,4},{4,8},{8,12},{12,16},{16,20},{20,24},{24,28},{1,5},{5,9},{9,... | collective-permute-start | bytes 221192 | tf_op jit(solution)/shard_map/ppermute | solution.py:488
  19.6 0.0 copy-start.1
  19.6 1.4 %collective-permute-start.3 = (f32[144,128]{1,0:T(8,128)S(1)}, f32[144,128]{1,0:T(8,128)S(1)}, u32[]{:S(2)}, u32[]{:S(2)}) collective-permute-start(f32[144,128]{1,0:T(8,128)S(1)} %get-tuple-element.30), channel_id=1, source_target_pairs={{4,0},{8,4},{12,8},{16,12},{20,16},{24,20},{28,24},{5,1},{9,5},{13... | collective-permute-start | bytes 221192 | tf_op jit(solution)/shard_map/ppermute | solution.py:489
  21.0 0.0 collective-permute-done.2.low
  21.0 3.8 %collective-permute-done.3.high = f32[144,128]{1,0:T(8,128)S(1)} collective-permute-done((f32[144,128]{1,0:T(8,128)S(1)}, f32[144,128]{1,0:T(8,128)S(1)}, u32[]{:S(2)}, u32[]{:S(2)}) %collective-permute-start.3) | collective-permute-done | bytes 73760 | tf_op jit(solution)/shard_map/ppermute | solution.py:489
  24.8 0.3 lanes.1
  25.2 3.1 %collective-permute-start.4 = (f32[312,128]{1,0:T(8,128)S(1)}, f32[312,128]{1,0:T(8,128)S(1)}, u32[]{:S(2)}, u32[]{:S(2)}) collective-permute-start(f32[312,128]{1,0:T(8,128)S(1)} %get-tuple-element.35), channel_id=1, source_target_pairs={{0,1},{1,2},{2,3},{4,5},{5,6},{6,7},{8,9},{9,10},{10,11},{12,13},{... | collective-permute-start | bytes 479240 | tf_op jit(solution)/shard_map/ppermute | solution.py:488
  28.3 1.3 %collective-permute-start.5 = (f32[312,128]{1,0:T(8,128)S(1)}, f32[312,128]{1,0:T(8,128)S(1)}, u32[]{:S(2)}, u32[]{:S(2)}) collective-permute-start(f32[312,128]{1,0:T(8,128)S(1)} %get-tuple-element.36), channel_id=1, source_target_pairs={{1,0},{2,1},{3,2},{5,4},{6,5},{7,6},{9,8},{10,9},{11,10},{13,12},{... | collective-permute-start | bytes 479240 | tf_op jit(solution)/shard_map/ppermute | solution.py:489
  29.6 0.9 collective-permute-done.4.before
  30.5 3.8 %collective-permute-done.5.after = f32[312,128]{1,0:T(8,128)S(1)} collective-permute-done((f32[312,128]{1,0:T(8,128)S(1)}, f32[312,128]{1,0:T(8,128)S(1)}, u32[]{:S(2)}, u32[]{:S(2)}) %collective-permute-start.5) | collective-permute-done | bytes 159776 | tf_op jit(solution)/shard_map/ppermute | solution.py:489
  34.3 0.0 copy-done.1
  34.3 2.2 %first.1 = (f32[16,32,128]{2,1,0:T(8,128)S(1)}, f32[16,32,128]{2,1,0:T(8,128)S(1)}, f32[16,32,128]{2,1,0:T(8,128)S(1)}, f32[22,40,128]{2,1,0:T(8,128)S(1)}, f32[...) custom-call(f32[16,32,128]{2,1,0:T(8,128)S(1)} %copy-done, ...), custom_call_target="tpu_custom_call" | custom-call | tf_op jit(solution)/shard_map/first/pallas_call | solution.py:472
  36.6 7.3 %collective-permute-start.7 = (f32[144,128]{1,0:T(8,128)S(1)}, f32[144,128]{1,0:T(8,128)S(1)}, u32[]{:S(2)}, u32[]{:S(2)}) collective-permute-start(f32[144,128]{1,0:T(8,128)S(1)} %get-tuple-element.43), channel_id=1, source_target_pairs={{32,0},{64,32},{96,64},{128,96},{160,128},{192,160},{224,192},{256... | collective-permute-start | bytes 221192 | tf_op jit(solution)/shard_map/ppermute | solution.py:489
  43.8 0.0 collective-permute-start.6
  43.8 0.9 collective-permute-done.7.after
  44.7 0.5 collective-permute-done.6.before
  45.2 0.2 second_rows.1
  45.4 3.2 %collective-permute-start.8 = (f32[96,128]{1,0:T(8,128)S(1)}, f32[96,128]{1,0:T(8,128)S(1)}, u32[]{:S(2)}, u32[]{:S(2)}) collective-permute-start(f32[96,128]{1,0:T(8,128)S(1)} %get-tuple-element.44), channel_id=1, source_target_pairs={{0,4},{4,8},{8,12},{12,16},{16,20},{20,24},{24,28},{1,5},{5,9},{9,... | collective-permute-start | bytes 147464 | tf_op jit(solution)/shard_map/ppermute | solution.py:488
  48.6 1.3 %collective-permute-start.9 = (f32[96,128]{1,0:T(8,128)S(1)}, f32[96,128]{1,0:T(8,128)S(1)}, u32[]{:S(2)}, u32[]{:S(2)}) collective-permute-start(f32[96,128]{1,0:T(8,128)S(1)} %get-tuple-element.45), channel_id=1, source_target_pairs={{4,0},{8,4},{12,8},{16,12},{20,16},{24,20},{28,24},{5,1},{9,5},{13... | collective-permute-start | bytes 147464 | tf_op jit(solution)/shard_map/ppermute | solution.py:489
  49.9 0.0 collective-permute-done.8.low
  49.9 4.1 %collective-permute-done.9.high = f32[96,128]{1,0:T(8,128)S(1)} collective-permute-done((f32[96,128]{1,0:T(8,128)S(1)}, f32[96,128]{1,0:T(8,128)S(1)}, u32[]{:S(2)}, u32[]{:S(2)}) %collective-permute-start.9) | collective-permute-done | bytes 49184 | tf_op jit(solution)/shard_map/ppermute | solution.py:489
  54.1 2.2 %second.1 = (f32[16,32,128]{2,1,0:T(8,128)S(1)}, f32[16,32,128]{2,1,0:T(8,128)S(1)}, f32[1,128]{1,0:T(1,128)S(1)}) custom-call(f32[16,32,128]{2,1,0:T(8,128)S(1)} %copy-done, f32[16,32,128]{2,1,0:T(8,128)S(1)} %copy-done.1, f32[16,32,128]{2,1,0:T(8,128)S(1)} %get-tuple-element.37.p_ref, f32[16,32,128]{2,1,0:T(8,128)S(1)} %get-tuple-element.38.q.q_ref, ...), custom_call_target="tpu_custom_call" | custom-call | tf_op jit(solution)/shard_map/second/pallas_call | solution.py:472
  56.3 17.0 %all_to_all.10 = f32[24,1,128]{2,1,0:T(1,128)S(1)} all-to-all(f32[24,1,128]{2,1,0:T(1,128)S(1)} %broadcast_in_dim.7), channel_id=1, replica_groups=mesh['gx'=24,'gy'=8,'gz'=4] {'gx'}, dimensions={0} | all-to-all | bytes 24576 | tf_op jit(solution)/shard_map/all_to_all | solution.py:496
  73.3 17.3 %all_to_all.11 = f32[32,1,128]{2,1,0:T(1,128)S(1)} all-to-all(f32[32,1,128]{2,1,0:T(1,128)S(1)} %broadcast_in_dim.16), channel_id=1, replica_groups=mesh['gx'=24,'gy'=8,'gz'=4] {'gy','gz'}, dimensions={0} | all-to-all | bytes 32768 | tf_op jit(solution)/shard_map/all_to_all | solution.py:496
  90.6 1.0 %last.1 = (f32[16,32,128]{2,1,0:T(8,128)}, f32[16,32,128]{2,1,0:T(8,128)}) custom-call(f32[16,32,128]{2,1,0:T(8,128)S(1)} %copy-done, f32[16,32,128]{2,1,0:T(8,128)S(1)} %get-tuple-element.37.p_ref, f32[16,32,128]{2,1,0:T(8,128)S(1)} %get-tuple-element.38.q.q_ref, f32[16,32,128]{2,1,0:T(8,128)S(1)} %get-tuple-element.47.m_ref, ...), custom_call_target="tpu_custom_call" | custom-call | tf_op jit(solution)/shard_map/last/pallas_call | solution.py:472
  (5 shorter events, 0.1 us)
Async XLA Ops:
  1.7 14.6 %copy-start = (f32[16,32,128]{2,1,0:T(8,128)S(1)}, f32[16,32,128]{2,1,0:T(8,128)}, u32[]{:S(2)}) copy-start(f32[16,32,128]{2,1,0:T(8,128)} %b_ref.5) | copy-start | bytes 786436
  1.9 11.5 %collective-permute-start.1 = (f32[176,128]{1,0:T(8,128)S(1)}, f32[176,128]{1,0:T(8,128)S(1)}, u32[]{:S(2)}, u32[]{:S(2)}) collective-permute-start(f32[176,128]{1,0:T(8,128)S(1)} %get-tuple-element.28), channel_id=1, source_target_pairs={{32,0},{64,32},{96,64},{128,96},{160,128},{192,160},{224,192},{256... | collective-permute-start | bytes 270344 | tf_op jit(solution)/shard_map/ppermute | solution.py:489
  12.4 3.9 %collective-permute-start = (f32[176,128]{1,0:T(8,128)S(1)}, f32[176,128]{1,0:T(8,128)S(1)}, u32[]{:S(2)}, u32[]{:S(2)}) collective-permute-start(f32[176,128]{1,0:T(8,128)S(1)} %get-tuple-element.27.mine), channel_id=1, source_target_pairs={{0,32},{32,64},{64,96},{96,128},{128,160},{160,192},{192,224},{224... | collective-permute-start | bytes 270344 | tf_op jit(solution)/shard_map/ppermute | solution.py:488
  16.4 4.7 %collective-permute-start.2 = (f32[144,128]{1,0:T(8,128)S(1)}, f32[144,128]{1,0:T(8,128)S(1)}, u32[]{:S(2)}, u32[]{:S(2)}) collective-permute-start(f32[144,128]{1,0:T(8,128)S(1)} %get-tuple-element.29), channel_id=1, source_target_pairs={{0,4},{4,8},{8,12},{12,16},{16,20},{20,24},{24,28},{1,5},{5,9},{9,... | collective-permute-start | bytes 221192 | tf_op jit(solution)/shard_map/ppermute | solution.py:488
  19.6 14.7 %copy-start.1 = (f32[16,32,128]{2,1,0:T(8,128)S(1)}, f32[16,32,128]{2,1,0:T(8,128)}, u32[]{:S(2)}) copy-start(f32[16,32,128]{2,1,0:T(8,128)} %d_ref.3) | copy-start | bytes 786436
  19.6 5.2 %collective-permute-start.3 = (f32[144,128]{1,0:T(8,128)S(1)}, f32[144,128]{1,0:T(8,128)S(1)}, u32[]{:S(2)}, u32[]{:S(2)}) collective-permute-start(f32[144,128]{1,0:T(8,128)S(1)} %get-tuple-element.30), channel_id=1, source_target_pairs={{4,0},{8,4},{12,8},{16,12},{20,16},{24,20},{28,24},{5,1},{9,5},{13... | collective-permute-start | bytes 221192 | tf_op jit(solution)/shard_map/ppermute | solution.py:489
  25.2 5.3 %collective-permute-start.4 = (f32[312,128]{1,0:T(8,128)S(1)}, f32[312,128]{1,0:T(8,128)S(1)}, u32[]{:S(2)}, u32[]{:S(2)}) collective-permute-start(f32[312,128]{1,0:T(8,128)S(1)} %get-tuple-element.35), channel_id=1, source_target_pairs={{0,1},{1,2},{2,3},{4,5},{5,6},{6,7},{8,9},{9,10},{10,11},{12,13},{... | collective-permute-start | bytes 479240 | tf_op jit(solution)/shard_map/ppermute | solution.py:488
  28.3 6.0 %collective-permute-start.5 = (f32[312,128]{1,0:T(8,128)S(1)}, f32[312,128]{1,0:T(8,128)S(1)}, u32[]{:S(2)}, u32[]{:S(2)}) collective-permute-start(f32[312,128]{1,0:T(8,128)S(1)} %get-tuple-element.36), channel_id=1, source_target_pairs={{1,0},{2,1},{3,2},{5,4},{6,5},{7,6},{9,8},{10,9},{11,10},{13,12},{... | collective-permute-start | bytes 479240 | tf_op jit(solution)/shard_map/ppermute | solution.py:489
  36.6 8.2 %collective-permute-start.7 = (f32[144,128]{1,0:T(8,128)S(1)}, f32[144,128]{1,0:T(8,128)S(1)}, u32[]{:S(2)}, u32[]{:S(2)}) collective-permute-start(f32[144,128]{1,0:T(8,128)S(1)} %get-tuple-element.43), channel_id=1, source_target_pairs={{32,0},{64,32},{96,64},{128,96},{160,128},{192,160},{224,192},{256... | collective-permute-start | bytes 221192 | tf_op jit(solution)/shard_map/ppermute | solution.py:489
  43.8 1.4 %collective-permute-start.6 = (f32[144,128]{1,0:T(8,128)S(1)}, f32[144,128]{1,0:T(8,128)S(1)}, u32[]{:S(2)}, u32[]{:S(2)}) collective-permute-start(f32[144,128]{1,0:T(8,128)S(1)} %get-tuple-element.42.mine), channel_id=1, source_target_pairs={{0,32},{32,64},{64,96},{96,128},{128,160},{160,192},{192,224},{224... | collective-permute-start | bytes 221192 | tf_op jit(solution)/shard_map/ppermute | solution.py:488
  45.4 4.5 %collective-permute-start.8 = (f32[96,128]{1,0:T(8,128)S(1)}, f32[96,128]{1,0:T(8,128)S(1)}, u32[]{:S(2)}, u32[]{:S(2)}) collective-permute-start(f32[96,128]{1,0:T(8,128)S(1)} %get-tuple-element.44), channel_id=1, source_target_pairs={{0,4},{4,8},{8,12},{12,16},{16,20},{20,24},{24,28},{1,5},{5,9},{9,... | collective-permute-start | bytes 147464 | tf_op jit(solution)/shard_map/ppermute | solution.py:488
  48.6 5.5 %collective-permute-start.9 = (f32[96,128]{1,0:T(8,128)S(1)}, f32[96,128]{1,0:T(8,128)S(1)}, u32[]{:S(2)}, u32[]{:S(2)}) collective-permute-start(f32[96,128]{1,0:T(8,128)S(1)} %get-tuple-element.45), channel_id=1, source_target_pairs={{4,0},{8,4},{12,8},{16,12},{20,16},{24,20},{28,24},{5,1},{9,5},{13... | collective-permute-start | bytes 147464 | tf_op jit(solution)/shard_map/ppermute | solution.py:489

commit v10 on v9

--- a/solution.py
+++ b/solution.py
@@ -484,10 +484,14 @@
 
 def both_ways(up, down, axis):
     count = lax.axis_size(axis)
-    steps = [(i, (i + 1) % count) for i in range(count if axis == "gx" else count - 1)]
-    before = lax.ppermute(up, axis, steps)
-    after = lax.ppermute(down, axis, [(j, i) for i, j in steps])
-    return before, after
+    if axis != "gz":
+        steps = [(i, (i + 1) % count) for i in range(count if axis == "gx" else count - 1)]
+        return lax.ppermute(up, axis, steps), lax.ppermute(down, axis, [(j, i) for i, j in steps])
+    even = lax.axis_index(axis) % 2 == 0
+    one = lax.ppermute(jnp.where(even, up, down), axis, [(i, i ^ 1) for i in range(count) if i ^ 1 < count])
+    swaps = [(i, i + 1) for i in range(1, count - 1, 2)]
+    two = lax.ppermute(jnp.where(even, down, up), axis, swaps + [(j, i) for i, j in swaps])
+    return jnp.where(even, two, one), jnp.where(even, one, two)
 
 
 def total(x, axis):

time: 91.9 us -> 91.9 us (level)
  blocking collectives: 34.3 us -> 37.9 us
  waiting for transfers between devices: 17.9 us -> 15.3 us
    all_to_all x2, blocking collectives: 34.3 us -> 37.9 us  [total(): return jnp.sum(lax.all_to_all(spread, axis, 0, 0, tiled=True), axis=0)]
    ppermute x10, waiting for transfers between devices: 17.9 us -> 15.3 us  [the longest x4 9.69 us: both_ways(): lax.ppermute(down, axis, [(j, i) for i, j in steps])]
where the time goes in v10:
time: 91.9 us; the launch traced here: 91.6 us
  blocking collectives  37.9 us (41%)
  starting transfers between devices  30.4 us (33%)
  waiting for transfers between devices  15.3 us (17%)
  Pallas kernels  5.99 us (7%)
  other arithmetic  1.15 us (1%)
    all_to_all x2, blocking collectives, total(): return jnp.sum(lax.all_to_all(spread, axis, 0, 0, tiled=True), axis=0)  37.9 us
    ppermute x4, starting transfers between devices, both_ways(): lax.ppermute(down, axis, [(j, i) for i, j in steps])  20.1 us
    ppermute x4, waiting for transfers between devices, both_ways(): lax.ppermute(down, axis, [(j, i) for i, j in steps])  9.69 us
    ppermute x4, starting transfers between devices, both_ways(): lax.ppermute(up, axis, steps)  6.41 us
    pallas_call x7, Pallas kernels, run(): pl.pallas_call(kernel, out_shape=[jax.ShapeDtypeStruct(shape, F32) for sh...  5.99 us
    ppermute x4, waiting for transfers between devices, both_ways(): lax.ppermute(up, axis, steps)  3.53 us
    ppermute x1, starting transfers between devices, both_ways(): lax.ppermute(jnp.where(even, up, down), axis, [(i, i ^ 1) for i in range(...  3.12 us
    ppermute x1, waiting for transfers between devices, both_ways(): lax.ppermute(jnp.where(even, up, down), axis, [(i, i ^ 1) for i in range(...  2.07 us
  transfers between devices with their start and end apart: 10, of which 8 were waited for; matrix products, arithmetic and copies ran while one was open for 0% of the time, Pallas kernels for 0%

profile of v10, /device:TPU:1, one launch (start us, length us, event | category | flops | bytes accessed | tf_op | source)
XLA Modules:
  0.0 91.6 jit_solution(15700971110429020818)
XLA Ops:
  0.6 1.1 %pad_maximum_fusion.bd_ref = f32[2,16,32,128]{3,2,1,0:T(8,128)S(1)} fusion(f32[1,16,32,128]{3,2,1,0:T(8,128)} %bitcast.7, f32[1,16,32,128]{3,2,1,0:T(8,128)} %bitcast.6), kind=kLoop, calls=%fused_computation | loop fusion | flops 131072 | bytes 1048576 | tf_op jit(solution)/shard_map/stack | solution.py:506
  1.7 0.0 copy-start
  1.7 0.2 start.1
  1.9 10.5 %collective-permute-start.1 = (f32[176,128]{1,0:T(8,128)S(1)}, f32[176,128]{1,0:T(8,128)S(1)}, u32[]{:S(2)}, u32[]{:S(2)}) collective-permute-start(f32[176,128]{1,0:T(8,128)S(1)} %get-tuple-element.28), channel_id=1, source_target_pairs={{32,0},{64,32},{96,64},{128,96},{160,128},{192,160},{224,192},{256... | collective-permute-start | bytes 270344 | tf_op jit(solution)/shard_map/ppermute | solution.py:489
  12.4 0.0 collective-permute-start
  12.4 0.9 %collective-permute-done.1.after = f32[176,128]{1,0:T(8,128)S(1)} collective-permute-done((f32[176,128]{1,0:T(8,128)S(1)}, f32[176,128]{1,0:T(8,128)S(1)}, u32[]{:S(2)}, u32[]{:S(2)}) %collective-permute-start.1) | collective-permute-done | bytes 90144 | tf_op jit(solution)/shard_map/ppermute | solution.py:489
  13.4 3.0 %collective-permute-done.before = f32[176,128]{1,0:T(8,128)S(1)} collective-permute-done((f32[176,128]{1,0:T(8,128)S(1)}, f32[176,128]{1,0:T(8,128)S(1)}, u32[]{:S(2)}, u32[]{:S(2)}) %collective-permute-start) | collective-permute-done | bytes 90144 | tf_op jit(solution)/shard_map/ppermute | solution.py:489
  16.3 0.0 copy-done
  16.4 3.2 %collective-permute-start.2 = (f32[144,128]{1,0:T(8,128)S(1)}, f32[144,128]{1,0:T(8,128)S(1)}, u32[]{:S(2)}, u32[]{:S(2)}) collective-permute-start(f32[144,128]{1,0:T(8,128)S(1)} %get-tuple-element.29), channel_id=1, source_target_pairs={{0,4},{4,8},{8,12},{12,16},{16,20},{20,24},{24,28},{1,5},{5,9},{9,... | collective-permute-start | bytes 221192 | tf_op jit(solution)/shard_map/ppermute | solution.py:489
  19.6 1.3 %collective-permute-start.3 = (f32[144,128]{1,0:T(8,128)S(1)}, f32[144,128]{1,0:T(8,128)S(1)}, u32[]{:S(2)}, u32[]{:S(2)}) collective-permute-start(f32[144,128]{1,0:T(8,128)S(1)} %get-tuple-element.30), channel_id=1, source_target_pairs={{4,0},{8,4},{12,8},{16,12},{20,16},{24,20},{28,24},{5,1},{9,5},{13... | collective-permute-start | bytes 221192 | tf_op jit(solution)/shard_map/ppermute | solution.py:489
  20.9 0.1 collective-permute-done.2.low
  21.0 3.7 %collective-permute-done.3.high = f32[144,128]{1,0:T(8,128)S(1)} collective-permute-done((f32[144,128]{1,0:T(8,128)S(1)}, f32[144,128]{1,0:T(8,128)S(1)}, u32[]{:S(2)}, u32[]{:S(2)}) %collective-permute-start.3) | collective-permute-done | bytes 73760 | tf_op jit(solution)/shard_map/ppermute | solution.py:489
  24.7 0.3 lanes.1
  25.0 3.1 %collective-permute-start.5 = (f32[312,128]{1,0:T(8,128)S(1)}, f32[312,128]{1,0:T(8,128)S(1)}, u32[]{:S(2)}, u32[]{:S(2)}) collective-permute-start(f32[312,128]{1,0:T(8,128)S(1)} %get-tuple-element.52), channel_id=1, source_target_pairs={{0,1},{1,0},{2,3},{3,2},{4,5},{5,4},{6,7},{7,6},{8,9},{9,8},{10,11... | collective-permute-start | bytes 479240 | tf_op jit(solution)/shard_map/ppermute | solution.py:491
  28.2 0.0 copy-start.1
  28.2 0.8 collective-permute-start.4
  29.0 2.1 %collective-permute-done.5 = f32[312,128]{1,0:T(8,128)S(1)} collective-permute-done((f32[312,128]{1,0:T(8,128)S(1)}, f32[312,128]{1,0:T(8,128)S(1)}, u32[]{:S(2)}, u32[]{:S(2)}) %collective-permute-start.5) | collective-permute-done | bytes 159776 | tf_op jit(solution)/shard_map/ppermute | solution.py:491
  31.1 0.0 collective-permute-done.4
  31.1 0.0 copy-done.1
  31.1 2.2 %first.1 = (f32[16,32,128]{2,1,0:T(8,128)S(1)}, f32[16,32,128]{2,1,0:T(8,128)S(1)}, f32[16,32,128]{2,1,0:T(8,128)S(1)}, f32[22,40,128]{2,1,0:T(8,128)S(1)}, f32[...) custom-call(f32[16,32,128]{2,1,0:T(8,128)S(1)} %copy-done, ...), custom_call_target="tpu_custom_call" | custom-call | tf_op jit(solution)/shard_map/first/pallas_call | solution.py:472
  33.3 7.0 %collective-permute-start.7 = (f32[144,128]{1,0:T(8,128)S(1)}, f32[144,128]{1,0:T(8,128)S(1)}, u32[]{:S(2)}, u32[]{:S(2)}) collective-permute-start(f32[144,128]{1,0:T(8,128)S(1)} %get-tuple-element.43), channel_id=1, source_target_pairs={{32,0},{64,32},{96,64},{128,96},{160,128},{192,160},{224,192},{256... | collective-permute-start | bytes 221192 | tf_op jit(solution)/shard_map/ppermute | solution.py:489
  40.3 0.0 collective-permute-start.6
  40.3 0.9 collective-permute-done.7.after
  41.2 0.5 collective-permute-done.6.before
  41.7 0.2 second_rows.1
  41.9 3.2 %collective-permute-start.8 = (f32[96,128]{1,0:T(8,128)S(1)}, f32[96,128]{1,0:T(8,128)S(1)}, u32[]{:S(2)}, u32[]{:S(2)}) collective-permute-start(f32[96,128]{1,0:T(8,128)S(1)} %get-tuple-element.44), channel_id=1, source_target_pairs={{0,4},{4,8},{8,12},{12,16},{16,20},{20,24},{24,28},{1,5},{5,9},{9,... | collective-permute-start | bytes 147464 | tf_op jit(solution)/shard_map/ppermute | solution.py:489
  45.1 1.3 %collective-permute-start.9 = (f32[96,128]{1,0:T(8,128)S(1)}, f32[96,128]{1,0:T(8,128)S(1)}, u32[]{:S(2)}, u32[]{:S(2)}) collective-permute-start(f32[96,128]{1,0:T(8,128)S(1)} %get-tuple-element.45), channel_id=1, source_target_pairs={{4,0},{8,4},{12,8},{16,12},{20,16},{24,20},{28,24},{5,1},{9,5},{13... | collective-permute-start | bytes 147464 | tf_op jit(solution)/shard_map/ppermute | solution.py:489
  46.4 0.0 collective-permute-done.8.low
  46.4 4.1 %collective-permute-done.9.high = f32[96,128]{1,0:T(8,128)S(1)} collective-permute-done((f32[96,128]{1,0:T(8,128)S(1)}, f32[96,128]{1,0:T(8,128)S(1)}, u32[]{:S(2)}, u32[]{:S(2)}) %collective-permute-start.9) | collective-permute-done | bytes 49184 | tf_op jit(solution)/shard_map/ppermute | solution.py:489
  50.5 2.1 %second.1 = (f32[16,32,128]{2,1,0:T(8,128)S(1)}, f32[16,32,128]{2,1,0:T(8,128)S(1)}, f32[1,128]{1,0:T(1,128)S(1)}) custom-call(f32[16,32,128]{2,1,0:T(8,128)S(1)} %copy-done, f32[16,32,128]{2,1,0:T(8,128)S(1)} %copy-done.1, f32[16,32,128]{2,1,0:T(8,128)S(1)} %get-tuple-element.37.p_ref, f32[16,32,128]{2,1,0:T(8,128)S(1)} %get-tuple-element.38.q.q_ref, ...), custom_call_target="tpu_custom_call" | custom-call | tf_op jit(solution)/shard_map/second/pallas_call | solution.py:472
  52.7 17.0 %all_to_all.10 = f32[24,1,128]{2,1,0:T(1,128)S(1)} all-to-all(f32[24,1,128]{2,1,0:T(1,128)S(1)} %broadcast_in_dim.7), channel_id=1, replica_groups=mesh['gx'=24,'gy'=8,'gz'=4] {'gx'}, dimensions={0} | all-to-all | bytes 24576 | tf_op jit(solution)/shard_map/all_to_all | solution.py:500
  69.7 20.8 %all_to_all.11 = f32[32,1,128]{2,1,0:T(1,128)S(1)} all-to-all(f32[32,1,128]{2,1,0:T(1,128)S(1)} %broadcast_in_dim.16), channel_id=1, replica_groups=mesh['gx'=24,'gy'=8,'gz'=4] {'gy','gz'}, dimensions={0} | all-to-all | bytes 32768 | tf_op jit(solution)/shard_map/all_to_all | solution.py:500
  90.6 1.0 %last.1 = (f32[16,32,128]{2,1,0:T(8,128)}, f32[16,32,128]{2,1,0:T(8,128)}) custom-call(f32[16,32,128]{2,1,0:T(8,128)S(1)} %copy-done, f32[16,32,128]{2,1,0:T(8,128)S(1)} %get-tuple-element.37.p_ref, f32[16,32,128]{2,1,0:T(8,128)S(1)} %get-tuple-element.38.q.q_ref, f32[16,32,128]{2,1,0:T(8,128)S(1)} %get-tuple-element.47.m_ref, ...), custom_call_target="tpu_custom_call" | custom-call | tf_op jit(solution)/shard_map/last/pallas_call | solution.py:472
  (7 shorter events, 0.1 us)
Async XLA Ops:
  1.7 14.6 %copy-start = (f32[16,32,128]{2,1,0:T(8,128)S(1)}, f32[16,32,128]{2,1,0:T(8,128)}, u32[]{:S(2)}) copy-start(f32[16,32,128]{2,1,0:T(8,128)} %b_ref.5) | copy-start | bytes 786436
  1.9 11.5 %collective-permute-start.1 = (f32[176,128]{1,0:T(8,128)S(1)}, f32[176,128]{1,0:T(8,128)S(1)}, u32[]{:S(2)}, u32[]{:S(2)}) collective-permute-start(f32[176,128]{1,0:T(8,128)S(1)} %get-tuple-element.28), channel_id=1, source_target_pairs={{32,0},{64,32},{96,64},{128,96},{160,128},{192,160},{224,192},{256... | collective-permute-start | bytes 270344 | tf_op jit(solution)/shard_map/ppermute | solution.py:489
  12.4 3.9 %collective-permute-start = (f32[176,128]{1,0:T(8,128)S(1)}, f32[176,128]{1,0:T(8,128)S(1)}, u32[]{:S(2)}, u32[]{:S(2)}) collective-permute-start(f32[176,128]{1,0:T(8,128)S(1)} %get-tuple-element.27.mine), channel_id=1, source_target_pairs={{0,32},{32,64},{64,96},{96,128},{128,160},{160,192},{192,224},{224... | collective-permute-start | bytes 270344 | tf_op jit(solution)/shard_map/ppermute | solution.py:489
  16.4 4.6 %collective-permute-start.2 = (f32[144,128]{1,0:T(8,128)S(1)}, f32[144,128]{1,0:T(8,128)S(1)}, u32[]{:S(2)}, u32[]{:S(2)}) collective-permute-start(f32[144,128]{1,0:T(8,128)S(1)} %get-tuple-element.29), channel_id=1, source_target_pairs={{0,4},{4,8},{8,12},{12,16},{16,20},{20,24},{24,28},{1,5},{5,9},{9,... | collective-permute-start | bytes 221192 | tf_op jit(solution)/shard_map/ppermute | solution.py:489
  19.6 5.1 %collective-permute-start.3 = (f32[144,128]{1,0:T(8,128)S(1)}, f32[144,128]{1,0:T(8,128)S(1)}, u32[]{:S(2)}, u32[]{:S(2)}) collective-permute-start(f32[144,128]{1,0:T(8,128)S(1)} %get-tuple-element.30), channel_id=1, source_target_pairs={{4,0},{8,4},{12,8},{16,12},{20,16},{24,20},{28,24},{5,1},{9,5},{13... | collective-permute-start | bytes 221192 | tf_op jit(solution)/shard_map/ppermute | solution.py:489
  25.0 6.0 %collective-permute-start.5 = (f32[312,128]{1,0:T(8,128)S(1)}, f32[312,128]{1,0:T(8,128)S(1)}, u32[]{:S(2)}, u32[]{:S(2)}) collective-permute-start(f32[312,128]{1,0:T(8,128)S(1)} %get-tuple-element.52), channel_id=1, source_target_pairs={{0,1},{1,0},{2,3},{3,2},{4,5},{5,4},{6,7},{7,6},{8,9},{9,8},{10,11... | collective-permute-start | bytes 479240 | tf_op jit(solution)/shard_map/ppermute | solution.py:491
  28.2 2.9 %copy-start.1 = (f32[16,32,128]{2,1,0:T(8,128)S(1)}, f32[16,32,128]{2,1,0:T(8,128)}, u32[]{:S(2)}) copy-start(f32[16,32,128]{2,1,0:T(8,128)} %d_ref.3) | copy-start | bytes 786436
  28.2 2.9 %collective-permute-start.4 = (f32[312,128]{1,0:T(8,128)S(1)}, f32[312,128]{1,0:T(8,128)S(1)}, u32[]{:S(2)}, u32[]{:S(2)}) collective-permute-start(f32[312,128]{1,0:T(8,128)S(1)} %get-tuple-element.53), channel_id=1, source_target_pairs={{1,2},{2,1},{5,6},{6,5},{9,10},{10,9},{13,14},{14,13},{17,18},{18,... | collective-permute-start | bytes 479240 | tf_op jit(solution)/shard_map/ppermute | solution.py:493
  33.3 7.9 %collective-permute-start.7 = (f32[144,128]{1,0:T(8,128)S(1)}, f32[144,128]{1,0:T(8,128)S(1)}, u32[]{:S(2)}, u32[]{:S(2)}) collective-permute-start(f32[144,128]{1,0:T(8,128)S(1)} %get-tuple-element.43), channel_id=1, source_target_pairs={{32,0},{64,32},{96,64},{128,96},{160,128},{192,160},{224,192},{256... | collective-permute-start | bytes 221192 | tf_op jit(solution)/shard_map/ppermute | solution.py:489
  40.3 1.4 %collective-permute-start.6 = (f32[144,128]{1,0:T(8,128)S(1)}, f32[144,128]{1,0:T(8,128)S(1)}, u32[]{:S(2)}, u32[]{:S(2)}) collective-permute-start(f32[144,128]{1,0:T(8,128)S(1)} %get-tuple-element.42.mine), channel_id=1, source_target_pairs={{0,32},{32,64},{64,96},{96,128},{128,160},{160,192},{192,224},{224... | collective-permute-start | bytes 221192 | tf_op jit(solution)/shard_map/ppermute | solution.py:489
  41.9 4.5 %collective-permute-start.8 = (f32[96,128]{1,0:T(8,128)S(1)}, f32[96,128]{1,0:T(8,128)S(1)}, u32[]{:S(2)}, u32[]{:S(2)}) collective-permute-start(f32[96,128]{1,0:T(8,128)S(1)} %get-tuple-element.44), channel_id=1, source_target_pairs={{0,4},{4,8},{8,12},{12,16},{16,20},{20,24},{24,28},{1,5},{5,9},{9,... | collective-permute-start | bytes 147464 | tf_op jit(solution)/shard_map/ppermute | solution.py:489
  45.1 5.5 %collective-permute-start.9 = (f32[96,128]{1,0:T(8,128)S(1)}, f32[96,128]{1,0:T(8,128)S(1)}, u32[]{:S(2)}, u32[]{:S(2)}) collective-permute-start(f32[96,128]{1,0:T(8,128)S(1)} %get-tuple-element.45), channel_id=1, source_target_pairs={{4,0},{8,4},{12,8},{16,12},{20,16},{24,20},{28,24},{5,1},{9,5},{13... | collective-permute-start | bytes 147464 | tf_op jit(solution)/shard_map/ppermute | solution.py:489
